TPU v7x, 32 devices: a whole 2x2x4 slice. The times are simulated.
32 devices in a mesh: cfg: 2 (over x), seq: 8 (over z, y), clip: 2 (over core).
Axes of the slice: x: 2, y: 2, z: 4, core: 2. Of those that a mesh axis runs over, the one named last changes fastest.
Arguments:
- clean: bfloat16 [128, 256, 1152], P(('clip', 'seq')), parts along dimension 0, may hold values from -6 to 6
- noise: bfloat16 [128, 256, 1152], P(('clip', 'seq')), parts along dimension 0, may hold values from -6 to 6
- timestep: float32 [2], P('clip'), parts along dimension 0, may hold values from 0.1 to 0.9
- guidance: float32 [2], P('clip'), parts along dimension 0, may hold values from 2 to 6
- condition_vector: bfloat16 [2304], P('clip'), parts along dimension 0, may hold values from -6 to 6
- empty_prompt_vector: bfloat16 [1152], replicated, may hold values from -6 to 6
- timestep_direction: bfloat16 [1152], replicated, may hold values from -6 to 6
- spatial_query_key_value: bfloat16 [3, 1152, 1152], P(None, None, ('cfg', 'seq')), may hold values from -1 to 1
- spatial_output_weight: bfloat16 [1152, 1152], P(('cfg', 'seq')), may hold values from -0.1875 to 0.1875
- temporal_query_key_value: bfloat16 [3, 1152, 1152], P(None, None, ('cfg', 'seq')), may hold values from -1 to 1
- temporal_output_weight: bfloat16 [1152, 1152], P(('cfg', 'seq')), may hold values from -0.1875 to 0.1875
- adapter_down_maps: bfloat16 [2, 1152, 64], replicated, may hold values from -0.1875 to 0.1875
- adapter_up_maps: bfloat16 [2, 64, 1152], replicated, may hold values from -0.75 to 0.75
Outputs:
- student_out: bfloat16 [128, 256, 1152], P(('clip', 'seq'), 'cfg'), parts along dimension 0
- student_tangent: bfloat16 [128, 256, 1152], P(('clip', 'seq'), 'cfg'), parts along dimension 0
There are 2 independent parts, one for each index of `clip`. A program takes and returns all parts, laid end to end along the dimension named above; an argument that names none is the same for every part. Nothing has to cross between parts.
All inputs are finite; a program needn't handle non-finite values.
Results may differ from a plain program's by a relative error of at most 0.028.
Values may be sent and summed in bfloat16 or wider, within the bound.
No kernel may reach another device: no remote copies, remote signals or barrier semaphores. Data moves between devices by JAX's collectives and lax.ppermute only.
A program may use at most 128 MiB of HBM per device.

v0:
```python
import jax
import jax.numpy as jnp
from jax import lax
from jax.sharding import PartitionSpec as P

HEAD_DIM = 72


epsilon = 1e-06


def partner(value, axis, bit):
    mask = 2**bit
    pairs = [(source, source ^ mask) for source in range(lax.axis_size(axis))]
    return lax.ppermute(value, axis, pairs)


def rms_scale(features):
    return features * lax.rsqrt(jnp.mean(features * features, axis=-1, keepdims=True) + epsilon)


def project(rows_in, matrix):
    return jnp.einsum("...d,dk->...k", rows_in, matrix, preferred_element_type=jnp.float32)


def space_attend(queries, key_rows, value_rows):
    head_count = queries.shape[-1] // HEAD_DIM
    split_dims = queries.shape[:-1] + (head_count, HEAD_DIM)
    scores = jnp.einsum(
        "...qhd,...khd->...hqk",
        queries.reshape(split_dims),
        key_rows.reshape(split_dims),
        preferred_element_type=jnp.float32,
    ) * HEAD_DIM ** (-0.5)
    scores = scores - jnp.max(scores, axis=-1, keepdims=True)
    exponent = jnp.exp(scores)
    soft_weights = (exponent / jnp.sum(exponent, axis=-1, keepdims=True)).astype(jnp.bfloat16)
    result = jnp.einsum(
        "...hqk,...khd->...qhd",
        soft_weights,
        value_rows.reshape(split_dims),
        preferred_element_type=jnp.float32,
    )
    return result.astype(jnp.bfloat16).reshape(queries.shape)


def time_attend(queries, key_rows, value_rows):
    head_count = queries.shape[-1] // HEAD_DIM
    split_dims = queries.shape[:-1] + (head_count, HEAD_DIM)
    scores = jnp.einsum(
        "...fxhd,...gxhd->...xhfg",
        queries.reshape(split_dims),
        key_rows.reshape(split_dims),
        preferred_element_type=jnp.float32,
    ) * HEAD_DIM ** (-0.5)
    scores = scores - jnp.max(scores, axis=-1, keepdims=True)
    exponent = jnp.exp(scores)
    soft_weights = (exponent / jnp.sum(exponent, axis=-1, keepdims=True)).astype(jnp.bfloat16)
    result = jnp.einsum(
        "...xhfg,...gxhd->...fxhd",
        soft_weights,
        value_rows.reshape(split_dims),
        preferred_element_type=jnp.float32,
    )
    return result.astype(jnp.bfloat16).reshape(queries.shape)


def time_core(embedding_rows, query_weight, key_weight, value_weight, out_weight):
    normed = rms_scale(embedding_rows).astype(jnp.bfloat16)
    queries = project(normed, query_weight).astype(jnp.bfloat16)
    key_rows = project(normed, key_weight).astype(jnp.bfloat16)
    value_rows = project(normed, value_weight).astype(jnp.bfloat16)
    return project(time_attend(queries, key_rows, value_rows), out_weight)


def student_network(
    embedding_rows,
    query_weight,
    key_weight,
    value_weight,
    out_weight,
    down_query,
    query_up_map,
    down_value,
    value_up_map,
):
    normed = rms_scale(embedding_rows).astype(jnp.bfloat16)
    low_query = project(normed, down_query).astype(jnp.bfloat16)
    low_value = project(normed, down_value).astype(jnp.bfloat16)
    queries = (project(normed, query_weight) + project(low_query, query_up_map)).astype(
        jnp.bfloat16
    )
    key_rows = project(normed, key_weight).astype(jnp.bfloat16)
    value_rows = (project(normed, value_weight) + project(low_value, value_up_map)).astype(
        jnp.bfloat16
    )
    return project(time_attend(queries, key_rows, value_rows), out_weight)


def on_device(
    clean,
    noise,
    timestep,
    guidance,
    condition_vector,
    empty_prompt_vector,
    timestep_direction,
    spatial_query_key_value,
    spatial_output_weight,
    temporal_query_key_value,
    temporal_output_weight,
    adapter_down_maps,
    adapter_up_maps,
):
    moment = timestep[0]
    strength = guidance[0]
    pair_side = lax.axis_index("cfg")
    noisy_rows = (
        (1.0 - moment) * clean.astype(jnp.float32) + moment * noise.astype(jnp.float32)
    ).astype(jnp.bfloat16)
    shifted = noisy_rows.astype(jnp.float32) + moment * timestep_direction.astype(jnp.float32)
    embeds = jnp.where(pair_side == 0, condition_vector, empty_prompt_vector)[None]
    branch_count = embeds.shape[0]
    entries = shifted[None] + embeds.astype(jnp.float32)[:, None, None, :]
    normed = rms_scale(entries).astype(jnp.bfloat16)
    triple = jnp.einsum(
        "bfpd,jdk->jbfpk",
        normed,
        lax.all_gather(spatial_query_key_value, ("cfg", "seq"), axis=2, tiled=True),
        preferred_element_type=jnp.float32,
    ).astype(jnp.bfloat16)
    attended = space_attend(triple[0], triple[1], triple[2])
    partial_value = jnp.einsum(
        "bfpk,kd->bfpd",
        attended,
        lax.all_gather(spatial_output_weight, ("cfg", "seq"), axis=0, tiled=True),
        preferred_element_type=jnp.float32,
    )
    layer_one = (entries + partial_value).astype(jnp.bfloat16)
    frame_count = layer_one.shape[1]
    position_count = layer_one.shape[2]
    width = layer_one.shape[3]
    stacked = jnp.concatenate([layer_one, noisy_rows[None]], axis=0).reshape(
        branch_count + 1, frame_count, 2, position_count // 2, width
    )
    regrouped = lax.all_to_all(stacked, "seq", split_axis=3, concat_axis=1, tiled=True)
    frames = regrouped.shape[1]
    local_rows = regrouped.shape[3]
    teacher_in = regrouped[:branch_count].reshape(branch_count, frames, 2 * local_rows, width)
    noisy_local = regrouped[branch_count]
    time_qkv, time_out = (
        lax.all_gather(temporal_query_key_value, ("cfg", "seq"), axis=2, tiled=True),
        lax.all_gather(temporal_output_weight, ("cfg", "seq"), axis=0, tiled=True),
    )
    teacher_part = time_core(
        teacher_in.astype(jnp.float32), time_qkv[0], time_qkv[1], time_qkv[2], time_out
    )
    velocity = (
        (teacher_in.astype(jnp.float32) + teacher_part)
        .astype(jnp.bfloat16)
        .reshape(branch_count, frames, 2, local_rows, width)
    )
    own_velocity = velocity[0]
    own_half = lax.dynamic_index_in_dim(own_velocity, pair_side, 1, keepdims=False)
    outgoing = lax.dynamic_index_in_dim(own_velocity, 1 - pair_side, 1, keepdims=False)
    other_half = partner(outgoing, "cfg", 0)
    is_first = pair_side == 0
    cond_velocity = jnp.where(is_first, own_half, other_half)
    uncond_velocity = jnp.where(is_first, other_half, own_half)
    student_noisy = lax.dynamic_index_in_dim(noisy_local, pair_side, 1, keepdims=False)
    query_up_map = adapter_up_maps[0]
    value_up_map = adapter_up_maps[1]
    uncond_float = uncond_velocity.astype(jnp.float32)
    guided = (uncond_float + strength * (cond_velocity.astype(jnp.float32) - uncond_float)).astype(
        jnp.bfloat16
    )
    student_in = (
        student_noisy.astype(jnp.float32)
        + moment * timestep_direction.astype(jnp.float32)
        + condition_vector.astype(jnp.float32)
    )

    def student_map(embedding_rows):
        return student_network(
            embedding_rows,
            time_qkv[0],
            time_qkv[1],
            time_qkv[2],
            time_out,
            adapter_down_maps[0],
            query_up_map,
            adapter_down_maps[1],
            value_up_map,
        )

    partial_value, tangent_part = jax.jvp(student_map, (student_in,), (guided.astype(jnp.float32),))
    primal = (student_in + partial_value).astype(jnp.bfloat16)
    tangent = (guided.astype(jnp.float32) + tangent_part).astype(jnp.bfloat16)
    returned = lax.all_to_all(
        jnp.stack([primal, tangent]), "seq", split_axis=1, concat_axis=2, tiled=True
    )
    return (returned[0], returned[1])


def solution(mesh):
    return jax.shard_map(
        on_device,
        mesh=mesh,
        in_specs=(
            P(("clip", "seq"), None, None),
            P(("clip", "seq"), None, None),
            P("clip"),
            P("clip"),
            P("clip"),
            P(),
            P(),
            P(None, None, ("cfg", "seq")),
            P(("cfg", "seq"), None),
            P(None, None, ("cfg", "seq")),
            P(("cfg", "seq"), None),
            P(),
            P(),
        ),
        out_specs=(P(("clip", "seq"), "cfg", None), P(("clip", "seq"), "cfg", None)),
        check_vma=False,
    )
```

profile of v0, /device:TPU:8, one launch (start us, length us, event | category | flops | bytes accessed | tf_op | source)
XLA Modules:
  0.0 1165.8 jit_solution(148011354367673308)
XLA Ops:
  11.4 6.8 multiply_reduce_fusion.3
  18.2 9.5 copy.82
  27.7 92.2 %all-gather.5.cloned.1.call-done = bf16[3,1152,1152]{1,2,0:T(8,128)(2,1)} async-done(((bf16[3,1152,72]{1,2,0:T(8,128)(2,1)}), bf16[3,1152,1152]{1,2,0:T(8,128)(2,1)}) %all-gather.5.cloned.1.call-update) | async-done | bytes 7962640 | tf_op jit(solution)/shard_map/all_gather | solution.py:129
  119.9 23.8 %convert_bitcast_fusion = bf16[3,1,8,256,1152]{4,3,0,2,1:T(8,128)(2,1)S(1)} fusion(bf16[3,1152,1152]{1,2,0:T(8,128)(2,1)} %all-gather.5.cloned.1.call-done, bf16[8,256,1152]{2,1,0:T(8,128)(2,1)} %get-tuple-element.10, f32[8,256]{1,0:T(8,128)S(1)} %add_rsqrt_fusion.1, f32[1152]{0:T(1024)S(1)} %get-tuple-element.20, f32[1152]{0:T(1024)S(1)} %convert_multiply_fusion.1), kind=kOutput, calls=%fused_computation.12 | convolution fusion | flops 16326328320 | bytes 26854400 | tf_op jit(solution)/shard_map/bfpd,jdk->jbfpk/dot_general | solution.py:126
  143.8 5.4 fusion.122
  149.1 6.6 copy.77
  155.8 6.7 copy.78
  162.4 18.1 %fusion.124 = (f32[8,16,256]{2,1,0:T(8,128)S(1)}, f32[8,16,256,256]{2,3,1,0:T(8,128)}) fusion(bf16[8,256,16,72]{1,3,2,0:T(8,128)(2,1)} %bitcast.217, bf16[8,256,16,72]{1,3,2,0:T(8,128)(2,1)} %bitcast.218), kind=kOutput, calls=%fused_computation.156 | convolution fusion | flops 1233125632 | bytes 43122688 | tf_op jit(solution)/shard_map/sub | solution.py:35
  180.6 6.6 copy.76
  187.2 16.0 %fusion.70 = bf16[8,16,72,256]{3,2,1,0:T(8,128)(2,1)} fusion(bf16[8,256,16,72]{1,3,2,0:T(8,128)(2,1)} %bitcast.219, f32[8,16,256,256]{2,3,1,0:T(8,128)} %get-tuple-element.23, f32[8,16,256]{2,1,0:T(8,128)S(1)} %get-tuple-element.22), kind=kOutput, calls=%fused_computation.106 | convolution fusion | flops 1227096064 | bytes 43122688 | tf_op jit(solution)/shard_map/...hqk,...khd->...qhd/dot_general | solution.py:38
  203.2 12.3 %add_convert_fusion.1 = bf16[8,256,1152]{2,1,0:T(8,128)(2,1)} fusion(bf16[8,256,1152]{2,1,0:T(8,128)(2,1)} %get-tuple-element.10, bf16[8,256,1152]{1,2,0:T(8,128)(2,1)} %bitcast.223, f32[1152]{0:T(1024)S(1)} %get-tuple-element.20, f32[1152]{0:T(1024)S(1)} %convert_multiply_fusion.1, bf16[1152,1152]{1,0:T(8,128)(2,1)} %all-gather.7.cloned.1.call-done), kind=kOutput, calls=%fused_computation.18 | convolution fusion | flops 5447614464 | bytes 16819200 | tf_op jit(solution)/shard_map/bfpk,kd->bfpd/dot_general | solution.py:133
  215.6 9.4 copy.81
  225.0 14.8 %pad_maximum_fusion = bf16[2,8,2,128,1152]{4,2,1,0,3:T(2,128)(2,1)} fusion(bf16[1,8,2,128,1152]{4,2,1,0,3:T(2,128)(2,1)} %copy.82, bf16[1,8,2,128,1152]{4,2,1,0,3:T(2,128)(2,1)} %copy.81), kind=kLoop, calls=%fused_computation.13 | loop fusion | flops 4718592 | bytes 18874368 | tf_op jit(solution)/shard_map/concatenate | solution.py:143
  239.8 6.5 all-to-all-start
  247.6 275.2 %all-to-all-done = bf16[2,8,2,128,1152]{4,2,1,0,3:T(2,128)(2,1)} async-done(((bf16[2,8,2,128,1152]{4,2,1,0,3:T(2,128)(2,1)}), bf16[2,8,2,128,1152]{4,2,1,0,3:T(2,128)(2,1)}, u32[]{:S(2)}, u32[]{:S(2)}) %all-to-all-start) | async-done | bytes 9437216 | tf_op jit(solution)/shard_map/all_to_all | solution.py:146
  522.8 10.6 copy.164
  533.4 3.3 multiply_reduce_fusion.2
  542.7 11.2 convolution_convert_fusion.1
  553.9 17.5 %reshape.257 = bf16[64,32,16,72]{3,2,1,0:T(8,128)(2,1)} reshape(bf16[64,32,1152]{2,1,0:T(8,128)(2,1)} %convolution_convert_fusion.1) | data formatting | bytes 9437184 | tf_op jit(solution)/shard_map/reshape.43
  571.4 11.0 convolution_convert_fusion
  582.4 17.5 %reshape.258 = bf16[64,32,16,72]{3,2,1,0:T(8,128)(2,1)} reshape(bf16[64,32,1152]{2,1,0:T(8,128)(2,1)} %convolution_convert_fusion) | data formatting | bytes 9437184 | tf_op jit(solution)/shard_map/reshape.44
  599.9 21.9 %fusion.12 = f32[32,16,64,64]{2,3,1,0:T(8,128)} fusion(bf16[64,32,16,72]{3,2,1,0:T(8,128)(2,1)} %reshape.258, bf16[64,32,16,72]{3,2,1,0:T(8,128)(2,1)} %reshape.257), kind=kOutput, calls=%fused_computation.25 | convolution fusion | flops 301989888 | bytes 17825792 | tf_op jit(solution)/shard_map/...fxhd,...gxhd->...xhfg/dot_general | solution.py:50
  621.8 18.6 %fusion.125 = (f32[32,16,64]{2,1,0:T(8,128)S(1)}, f32[32,16,64,64]{2,3,1,0:T(8,128)}) fusion(f32[32,16,64,64]{2,3,1,0:T(8,128)} %fusion.12), kind=kOutput, calls=%fused_computation.157 | output fusion | flops 8388671 | bytes 16908288 | tf_op jit(solution)/shard_map/sub | solution.py:56
  640.4 10.5 convolution_convert_fusion.2
  650.9 17.4 %reshape.256 = bf16[64,32,16,72]{3,2,1,0:T(8,128)(2,1)} reshape(bf16[64,32,1152]{2,1,0:T(8,128)(2,1)} %convolution_convert_fusion.2) | data formatting | bytes 9437184 | tf_op jit(solution)/shard_map/reshape.48
  668.4 17.6 %convert_bitcast_fusion.1 = bf16[1,64,32,16,72]{4,1,3,2,0:T(8,128)(2,1)} fusion(f32[32,16,64,64]{2,3,1,0:T(8,128)} %get-tuple-element.25, f32[32,16,64]{2,1,0:T(8,128)S(1)} %get-tuple-element.24, bf16[64,32,16,72]{3,2,1,0:T(8,128)(2,1)} %reshape.256), kind=kOutput, calls=%fused_computation.34 | convolution fusion | flops 308543488 | bytes 17956864 | tf_op jit(solution)/shard_map/...xhfg,...gxhd->...fxhd/dot_general | solution.py:59
  686.0 12.0 %copy.98 = bf16[1,64,32,16,72]{4,3,2,1,0:T(8,128)(2,1)} copy(bf16[1,64,32,16,72]{4,1,3,2,0:T(8,128)(2,1)} %convert_bitcast_fusion.1) | data formatting | bytes 9437184 | tf_op jit(solution)/shard_map/convert_element_type | solution.py:65
  698.0 13.8 %reshape.259 = bf16[64,32,1152]{2,1,0:T(8,128)(2,1)} reshape(bf16[1,64,32,16,72]{4,3,2,1,0:T(8,128)(2,1)} %copy.98) | data formatting | bytes 9437184 | tf_op jit(solution)/shard_map/reshape.51
  711.8 7.3 slice_convert_fusion
  719.1 4.8 copy.92
  723.9 10.9 add_convert_fusion
  740.8 51.0 %collective-permute-done = bf16[64,16,1152]{2,1,0:T(8,128)(2,1)S(1)} collective-permute-done((bf16[64,16,1152]{2,1,0:T(8,128)(2,1)}, bf16[64,16,1152]{2,1,0:T(8,128)(2,1)S(1)}, u32[]{:S(2)}, u32[]{:S(2)}) %collective-permute-start) | collective-permute-done | bytes 2359328 | tf_op jit(solution)/shard_map/ppermute | solution.py:15
  791.8 5.8 fusion.29
  797.6 7.1 fusion.81
  804.7 5.3 fusion.51
  810.0 8.3 reshape.252
  818.3 6.1 convolution_convert_fusion.4
  824.5 8.5 reshape.254
  832.9 8.2 fusion.83
  841.2 5.3 fusion.52
  846.5 8.4 reshape.253
  857.8 7.7 fusion.82
  865.5 5.9 fusion.54
  871.4 9.6 reshape.261
  881.1 6.5 convolution_convert_fusion.3
  887.6 9.8 reshape.262
  897.4 13.0 %multiply_reduce_fusion.4 = (f32[16,16,64]{2,1,0:T(8,128)S(1)}, f32[16,16,64,64]{2,3,1,0:T(8,128)}) fusion(bf16[64,16,16,72]{3,2,1,0:T(8,128)(2,1)} %reshape.254, bf16[64,16,16,72]{3,2,1,0:T(8,128)(2,1)} %reshape.253), kind=kOutput, calls=%fused_computation.42 | convolution fusion | flops 153075712 | bytes 8978432 | tf_op jit(solution)/shard_map/jvp(...fxhd,...gxhd->...xhfg)/dot_general | solution.py:50
  910.4 8.2 fusion.44
  918.6 12.1 %add_multiply_fusion = f32[16,16,64,64]{2,3,1,0:T(8,128)S(1)} fusion(f32[16,16,64,64]{2,3,1,0:T(8,128)} %fusion.44, bf16[64,16,16,72]{3,2,1,0:T(8,128)(2,1)} %reshape.254, bf16[64,16,16,72]{3,2,1,0:T(8,128)(2,1)} %reshape.261), kind=kOutput, calls=%fused_computation.33 | convolution fusion | flops 153092096 | bytes 13107200 | tf_op jit(solution)/shard_map/jvp(...fxhd,...gxhd->...xhfg)/dot_general | solution.py:50
  930.7 9.8 convert_reduce_fusion
  940.6 4.7 fusion.18
  946.0 9.2 convert_bitcast_fusion.3
  955.3 4.7 copy.91
  959.9 7.7 reshape.255
  967.6 6.9 fusion.80
  974.5 5.9 fusion.53
  980.4 9.8 reshape.260
  990.3 15.2 %fusion.50 = f32[16,16,72,64]{2,3,1,0:T(8,128)} fusion(f32[16,16,64,64]{2,3,1,0:T(8,128)} %copy-done, f32[16,16,64]{2,1,0:T(8,128)S(1)} %copy-done.14, f32[16,16,64]{2,1,0:T(8,128)S(1)} %neg.8, f32[16,16,64]{2,1,0:T(8,128)S(1)} %div.86, f32[16,16,64]{2,1,0:T(8,128)S(1)} %get-tuple-element.3, f32[16,16,64,64]{2,3,1,0:T(8,128)} %get-tuple-element.27, ...), kind=kOutput, calls=%fused_computation.88 | convolution fusion | flops 160432128 | bytes 15794176 | tf_op jit(solution)/shard_map/jvp(...xhfg,...gxhd->...fxhd)/dot_general | solution.py:59
  1005.5 13.9 %fusion.43 = bf16[64,16,16,72]{3,0,2,1:T(8,128)(2,1)} fusion(f32[16,16,72,64]{2,3,1,0:T(8,128)} %fusion.50, bf16[64,16,16,72]{3,2,1,0:T(8,128)(2,1)} %reshape.260, f32[16,16,64]{2,1,0:T(8,128)S(1)} %get-tuple-element.3, f32[16,16,64]{2,1,0:T(8,128)S(1)} %get-tuple-element.26, f32[16,16,64,64]{2,3,1,0:T(8,128)} %get-tuple-element.27), kind=kOutput, calls=%fused_computation.80 | convolution fusion | flops 157548544 | bytes 13762560 | tf_op jit(solution)/shard_map/jvp(...xhfg,...gxhd->...fxhd)/dot_general | solution.py:59
  1019.4 7.1 copy.109
  1026.6 7.7 reshape.263
  1034.2 6.0 fusion.65
  1040.3 3.7 fusion.64
  1044.9 110.2 %all_to_all.30 = bf16[2,64,16,1152]{3,2,0,1:T(8,128)(2,1)S(1)} all-to-all(bf16[2,64,16,1152]{3,2,0,1:T(8,128)(2,1)S(1)} %copy.110), channel_id=1, replica_groups=mesh['cfg'=2,'seq'=8,'clip'=2] {'seq'}, dimensions={1} | all-to-all | bytes 9437184 | tf_op jit(solution)/shard_map/all_to_all | solution.py:199
  (76 shorter events, 24.5 us)
Async XLA Ops:
  7.2 112.8 %all-gather.5.cloned.1.call-start = ((), (), s32[]{:S(2)}) async-start(), calls=%async_computation.2 | async-start | bytes 8460288 | tf_op jit(solution)/shard_map/all_gather | solution.py:129
  7.9 195.3 %all-gather.7.cloned.1.call-start = ((), (), s32[]{:S(2)}) async-start(), calls=%async_computation.3 | async-start | bytes 2820096 | tf_op jit(solution)/shard_map/all_gather | solution.py:136
  10.0 193.2 %copy-start.11 = (f32[1152]{0:T(1024)}, f32[1152]{0:T(1024)S(1)}, u32[]{:S(2)}) copy-start(f32[1152]{0:T(1024)S(1)} %convert_multiply_fusion.1) | copy-start | bytes 13828
  239.8 283.0 %all-to-all-start = ((bf16[2,8,2,128,1152]{4,2,1,0,3:T(2,128)(2,1)}), bf16[2,8,2,128,1152]{4,2,1,0,3:T(2,128)(2,1)}, u32[]{:S(2)}, u32[]{:S(2)}) async-start(bf16[2,8,2,128,1152]{4,2,1,0,3:T(2,128)(2,1)} %pad_maximum_fusion), calls=%async_computation | async-start | bytes 18874368 | tf_op jit(solution)/shard_map/all_to_all | solution.py:146
  246.3 296.4 %all-gather.9.cloned.1.call-start = ((), (), s32[]{:S(2)}) async-start(), calls=%async_computation.4 | async-start | bytes 8460288 | tf_op jit(solution)/shard_map/all_gather | solution.py:152
  247.0 476.9 %all-gather.11.cloned.1.call-start = ((), (), s32[]{:S(2)}) async-start(), calls=%async_computation.5 | async-start | bytes 2820096 | tf_op jit(solution)/shard_map/all_gather | solution.py:153
  582.4 58.0 %slice-start.4 = ((s8[4718592]{0:T(1024)(128)(4,1)}), s8[524288]{0:T(1024)(128)(4,1)S(1)}, s32[]{:S(2)}) async-start(s8[4718592]{0:T(1024)(128)(4,1)} %bitcast.214), calls=%async_computation.10 | async-start | bytes 1048576
  599.9 40.5 %slice-start.5 = ((s8[4718592]{0:T(1024)(128)(4,1)}), s8[4194304]{0:T(1024)(128)(4,1)S(1)}, s32[]{:S(2)}) async-start(s8[4718592]{0:T(1024)(128)(4,1)} %bitcast.214), calls=%async_computation.11 | async-start | bytes 8388608
  734.8 2.1 copy-start.6
  734.8 57.0 %copy-start.12 = (f32[1152]{0:T(1024)S(1)}, f32[1152]{0:T(1024)}, u32[]{:S(2)}) copy-start(f32[1152]{0:T(1024)} %copy-done.11) | copy-start | bytes 13828
  734.8 57.0 %copy-start.13 = (f32[1152]{0:T(1024)S(1)}, f32[1152]{0:T(1024)}, u32[]{:S(2)}) copy-start(f32[1152]{0:T(1024)} %get-tuple-element.21) | copy-start | bytes 13828
  736.9 60.6 %slice-start.2 = ((s8[4718592]{0:T(1024)(128)(4,1)}), s8[524288]{0:T(1024)(128)(4,1)S(1)}, s32[]{:S(2)}) async-start(s8[4718592]{0:T(1024)(128)(4,1)} %bitcast.204), calls=%async_computation.8 | async-start | bytes 1048576
  738.5 53.3 %collective-permute-start = (bf16[64,16,1152]{2,1,0:T(8,128)(2,1)}, bf16[64,16,1152]{2,1,0:T(8,128)(2,1)S(1)}, u32[]{:S(2)}, u32[]{:S(2)}) collective-permute-start(bf16[64,16,1152]{2,1,0:T(8,128)(2,1)} %dynamic-slice_bitcast_fusion), channel_id=1, source_target_pairs={{0,16},{16,0},{1,17},{17,1},{2,18},{18,2},{3,19},{19,3},{4,20},{20... | collective-permute-start | bytes 7077896 | tf_op jit(solution)/shard_map/ppermute | solution.py:15
  791.8 5.8 slice-start.3
  797.6 7.1 copy-start.9
  797.6 7.1 copy-start.10
  857.8 23.3 %copy-start.2 = (bf16[64,16,1152]{2,1,0:T(8,128)(2,1)}, bf16[64,16,1152]{2,1,0:T(8,128)(2,1)S(1)}, u32[]{:S(2)}) copy-start(bf16[64,16,1152]{2,1,0:T(8,128)(2,1)S(1)} %fusion.33) | copy-start | bytes 7077892
  897.4 13.0 %copy-start.1 = (bf16[64,16,16,72]{3,2,1,0:T(8,128)(2,1)S(1)}, bf16[64,16,16,72]{3,2,1,0:T(8,128)(2,1)}, u32[]{:S(2)}) copy-start(bf16[64,16,16,72]{3,2,1,0:T(8,128)(2,1)} %reshape.253) | copy-start | bytes 7077892
  897.4 13.0 %copy-start.4 = (bf16[64,16,16,72]{3,2,1,0:T(8,128)(2,1)S(1)}, bf16[64,16,16,72]{3,2,1,0:T(8,128)(2,1)}, u32[]{:S(2)}) copy-start(bf16[64,16,16,72]{3,2,1,0:T(8,128)(2,1)} %reshape.262) | copy-start | bytes 7077892
  930.7 9.9 copy-start
  930.7 9.9 slice-start
  930.7 9.9 slice-start.1
  959.9 7.7 copy-start.3
  980.4 9.9 copy-start.14
  1026.6 7.7 copy-start.7
  1034.2 6.0 copy-start.5
  1034.2 6.0 copy-start.8
  1034.2 6.0 copy-start.15
Sparse Core Ops, SparseCore 0:
  10.7 109.1 all-gather.4
  122.7 64.0 all-gather.6
  249.9 276.2 all-gather.8
  528.7 64.7 all-gather.10
where the time goes:
time: 1180 us; the launch traced here: 1170 us
  waiting for transfers between devices  421 us (36%)
  matrix products  300 us (25%)
  local copies, waits for them, and re-layouts  230 us (19%)
  blocking collectives  110 us (9%)
  other arithmetic  80.7 us (7%)
  between operations  15.9 us (1%)
    all_to_all x1, waiting for transfers between devices, on_device(): lax.all_to_all(stacked, 'seq', split_axis=3, concat_axis=1, tiled=True)  275 us
    dot_general x16, matrix products, project(): jnp.einsum('...d,dk->...k', rows_in, matrix, preferred_element_type=jnp.f...  118 us
    all_to_all x1, blocking collectives, on_device(): lax.all_to_all(jnp.stack([primal, tangent]), 'seq', split_axis=1, concat_...  110 us
    all_gather x1, waiting for transfers between devices, on_device(): lax.all_gather(spatial_query_key_value, ('cfg', 'seq'), axis=2, tiled=True)  92.2 us
    another operation x4, local copies, waits for them, and re-layouts  66.2 us
    dot_general x4, matrix products, time_attend(): jnp.einsum('...xhfg,...gxhd->...fxhd', soft_weights, value_rows.reshape(s...  56 us
    dot_general x4, matrix products, time_attend(): jnp.einsum('...fxhd,...gxhd->...xhfg', queries.reshape(split_dims), key_r...  55.2 us
    ppermute x1, waiting for transfers between devices, partner(): return lax.ppermute(value, axis, pairs)  51 us
  transfers between devices with their start and end apart: 6, of which 3 were waited for; matrix products, arithmetic and copies ran while one was open for 26% of the time, Pallas kernels for 0%

commit v1 on v0

--- a/solution.py
+++ b/solution.py
@@ -1,10 +1,21 @@
+import functools
+import math
+
 import jax
 import jax.numpy as jnp
 from jax import lax
+from jax.experimental import pallas as pl
+from jax.experimental.pallas import tpu as pltpu
 from jax.sharding import PartitionSpec as P
 
 HEAD_DIM = 72
-
+LANES = 128
+ROW_TILE = 16
+BLOCK = 8
+TANGENT_BLOCK = 4
+PAIR = 2
+EXPONENT_SCALE = HEAD_DIM ** (-0.5) * math.log2(math.e)
+VMEM_LIMIT = 40 * 1024 * 1024
 
 epsilon = 1e-06
 
@@ -97,7 +108,7 @@
     return project(time_attend(queries, key_rows, value_rows), out_weight)
 
 
-def on_device(
+def plain_on_device(
     clean,
     noise,
     timestep,
@@ -202,9 +213,972 @@
     return (returned[0], returned[1])
 
 
+def dot(left, right):
+    return lax.dot_general(
+        left, right, (((1,), (0,)), ((), ())), preferred_element_type=jnp.float32
+    )
+
+
+def dot_t(left, right):
+    return lax.dot_general(
+        left, right, (((1,), (1,)), ((), ())), preferred_element_type=jnp.float32
+    )
+
+
+def lane_range(shape, start, low, high):
+    lane = lax.broadcasted_iota(jnp.int32, shape, len(shape) - 1) + start
+    return (lane >= low) & (lane < high)
+
+
+def only(value, keep):
+    return jnp.where(keep, value, jnp.zeros_like(value))
+
+
+def window_of(low, high):
+    start = low // LANES * LANES
+    return start, -(-high // LANES) * LANES - start
+
+
+def inverse_rms(features):
+    return lax.rsqrt(jnp.mean(features * features, axis=-1, keepdims=True) + epsilon)
+
+
+def weight_copies(seat, layout, pieces, weights_ref, sems):
+    side, place, core = seat[0], seat[1], seat[2]
+    across, along = place // 4, lax.rem(place, 2)
+    copies = []
+    for array, part, sibling, (x, z, y) in layout:
+        piece = pieces[array] if part is None else pieces[array].at[part]
+        count, rows = piece.shape[:2]
+        block = ((side ^ x) * 2 + (across ^ z)) * 2 + (along ^ y)
+        start = pl.multiple_of(block * rows, ROW_TILE)
+        copies.append(
+            pltpu.make_async_copy(
+                piece,
+                weights_ref.at[pl.ds((core ^ sibling) * count, count), pl.ds(start, rows), :],
+                sems.at[len(copies)],
+            )
+        )
+    return copies
+
+
+def noisy_kernel(seat_ref, moment_ref, clean_ref, noise_ref, *rest):
+    line_refs, rows_ref = rest[:-1], rest[-1]
+    moment = moment_ref[0]
+    rows_ref[...] = (
+        (1.0 - moment) * clean_ref[0].astype(jnp.float32)
+        + moment * noise_ref[0].astype(jnp.float32)
+    ).astype(jnp.bfloat16)
+    for index in range(2 * len(line_refs)):
+        start = pl.multiple_of((seat_ref[1] ^ index) * ROW_TILE, ROW_TILE)
+        line_refs[index // 2][index % 2, 0] = rows_ref[pl.ds(start, ROW_TILE), :]
+
+
+def noisy_pieces(seat, moment, clean, noise, seats):
+    frames, positions, width = clean.shape
+    rows = seats * ROW_TILE
+    block = pl.BlockSpec((1, rows, width), lambda f, seat: (f, seat[0], 0))
+    half = seats // 2
+    piece = jax.ShapeDtypeStruct((2, frames, ROW_TILE, width), jnp.bfloat16)
+    out_block = pl.BlockSpec((2, 1, ROW_TILE, width), lambda f, seat: (0, f, 0, 0))
+    return pl.pallas_call(
+        noisy_kernel,
+        out_shape=[piece] * half,
+        grid_spec=pltpu.PrefetchScalarGridSpec(
+            num_scalar_prefetch=1,
+            grid=(frames,),
+            in_specs=[pl.BlockSpec(memory_space=pltpu.SMEM), block, block],
+            out_specs=[out_block] * half,
+            scratch_shapes=[pltpu.VMEM((rows, width), jnp.bfloat16)],
+        ),
+        compiler_params=pltpu.CompilerParams(vmem_limit_bytes=VMEM_LIMIT),
+    )(seat, moment, clean, noise)
+
+
+def space_kernel(layout, pieces, targets, seat_ref, moment_ref, clean_ref, noise_ref, shift_ref, *rest):
+    weight_pieces, sent_refs = rest[:pieces], rest[pieces : pieces + targets]
+    weights_ref, noisy_ref, query_ref, key_ref, value_ref, mixed_ref, sems = rest[pieces + targets :]
+    moment = moment_ref[0]
+    pair, positions, width = clean_ref.shape
+
+    @pl.when(pl.program_id(0) == 0)
+    def _():
+        wait_all(start_all(weight_copies(seat_ref, layout, weight_pieces, weights_ref, sems)))
+
+    noisy = (
+        (1.0 - moment) * clean_ref[...].reshape(pair * positions, width).astype(jnp.float32)
+        + moment * noise_ref[...].reshape(pair * positions, width).astype(jnp.float32)
+    ).astype(jnp.bfloat16)
+    noisy_ref[...] = noisy
+    entry = noisy.astype(jnp.float32) + shift_ref[...]
+    normed = (entry * inverse_rms(entry)).astype(jnp.bfloat16)
+    query_ref[...] = dot_t(normed, weights_ref[0]).astype(jnp.bfloat16)
+    key_ref[...] = dot_t(normed, weights_ref[1]).astype(jnp.bfloat16)
+    value_ref[...] = dot_t(normed, weights_ref[2]).astype(jnp.bfloat16)
+
+    @pl.loop(0, pair)
+    def _(frame):
+        here = pl.ds(pl.multiple_of(frame * positions, positions), positions)
+        space_mix(query_ref.at[here], key_ref.at[here], value_ref.at[here], mixed_ref.at[here])
+
+    entry = noisy_ref[...].astype(jnp.float32) + shift_ref[...]
+    query_ref[...] = (entry + dot(mixed_ref[...], weights_ref[3])).astype(jnp.bfloat16)
+    lines = sent_refs[0].shape[0]
+    for index, ref in enumerate(sent_refs):
+        for line in range(lines):
+            seat = (seat_ref[0] ^ (index // 2)) * lines * 2 + (
+                seat_ref[1] ^ (line * 2 + index % 2)
+            )
+            for frame in range(pair):
+                start = pl.multiple_of(frame * positions + seat * ROW_TILE, ROW_TILE)
+                ref[line, frame] = query_ref[pl.ds(start, ROW_TILE), :]
+
+
+def space_mix(query_ref, key_ref, value_ref, mixed_ref):
+    positions, width = query_ref.shape
+    weights = []
+    for head in range(width // HEAD_DIM):
+        low, high = head * HEAD_DIM, (head + 1) * HEAD_DIM
+        start, extent = window_of(low, high)
+        keep = lane_range((positions, extent), start, low, high)
+        queries = only(query_ref[:, pl.ds(start, extent)], keep)
+        scores = dot_t(queries, key_ref[:, pl.ds(start, extent)])
+        top = jnp.max(scores, axis=-1, keepdims=True)
+        exponent = jnp.exp2((scores - top) * EXPONENT_SCALE)
+        total = jnp.sum(exponent, axis=-1, keepdims=True)
+        weights.append((exponent * (1.0 / total)).astype(jnp.bfloat16))
+        tile = high // (2 * LANES)
+        done = [low // (2 * LANES)] if tile > low // (2 * LANES) else []
+        if head == width // HEAD_DIM - 1:
+            done = [(width - 1) // (2 * LANES)]
+        for full in done:
+            left_edge = full * 2 * LANES
+            edge = min(width, left_edge + 2 * LANES)
+            heads = range(left_edge // HEAD_DIM, -(-edge // HEAD_DIM))
+            values = value_ref[:, pl.ds(left_edge, edge - left_edge)]
+            parts = [
+                only(
+                    values,
+                    lane_range(values.shape, left_edge, h * HEAD_DIM, (h + 1) * HEAD_DIM),
+                )
+                for h in heads
+            ]
+            mixed = dot(
+                jnp.concatenate([weights[h] for h in heads], axis=1),
+                jnp.concatenate(parts, axis=0),
+            )
+            mixed_ref[:, pl.ds(left_edge, edge - left_edge)] = mixed.astype(jnp.bfloat16)
+
+
+def spatial_layer(seat, moment, clean, noise, shift, weights, frames, seats):
+    pieces, layout = weights
+    positions, width = clean.shape[1:]
+    frame_block = pl.BlockSpec(
+        (PAIR, positions, width), lambda f, seat: (seat[0] * (frames // PAIR) + f, 0, 0)
+    )
+    lines = seats // 2
+    piece = jax.ShapeDtypeStruct((lines, frames, ROW_TILE, width), jnp.bfloat16)
+    vmem = lambda *shape: pltpu.VMEM(shape, jnp.bfloat16)
+    rows = frames * positions
+    return pl.pallas_call(
+        functools.partial(space_kernel, layout, len(pieces), 4),
+        out_shape=[piece] * 4,
+        grid_spec=pltpu.PrefetchScalarGridSpec(
+            num_scalar_prefetch=1,
+            grid=(frames // PAIR,),
+            in_specs=[
+                pl.BlockSpec(memory_space=pltpu.SMEM),
+                frame_block,
+                frame_block,
+                pl.BlockSpec(shift.shape, lambda f, seat: (0, 0)),
+            ]
+            + [pl.BlockSpec(memory_space=pl.ANY)] * len(pieces),
+            out_specs=[
+                pl.BlockSpec((lines, PAIR, ROW_TILE, width), lambda f, seat: (0, f, 0, 0))
+            ]
+            * 4,
+            scratch_shapes=[vmem(4, width, width)]
+            + [vmem(PAIR * positions, width)] * 5
+            + [pltpu.SemaphoreType.DMA((len(layout),))],
+        ),
+        compiler_params=pltpu.CompilerParams(vmem_limit_bytes=VMEM_LIMIT),
+        cost_estimate=pl.CostEstimate(
+            flops=14 * rows * width * width,
+            bytes_accessed=8 * width * width + 6 * rows * width,
+            transcendentals=rows * positions * width // HEAD_DIM,
+        ),
+    )(seat, moment, clean, noise, shift, *pieces)
+
+
+def swap_matrix(rows, columns):
+    count = rows * columns
+    target = lax.broadcasted_iota(jnp.int32, (count, count), 0)
+    source = lax.broadcasted_iota(jnp.int32, (count, count), 1)
+    moved = lax.rem(target, rows) * columns + lax.div(target, rows)
+    return jnp.where(source == moved, 1.0, 0.0).astype(jnp.bfloat16)
+
+
+def halves(value, frames, reduce):
+    first = lane_range(value.shape, 0, 0, frames)
+    if reduce == "max":
+        low = jnp.max(jnp.where(first, value, -jnp.inf), axis=-1, keepdims=True)
+        high = jnp.max(jnp.where(first, -jnp.inf, value), axis=-1, keepdims=True)
+    else:
+        low = jnp.sum(jnp.where(first, value, 0.0), axis=-1, keepdims=True)
+        high = jnp.sum(jnp.where(first, 0.0, value), axis=-1, keepdims=True)
+    return first, low, high
+
+
+def time_mix(frames, refs, tangents=None):
+    query_ref, key_ref, value_ref, mixed_ref = refs
+    rows, width = query_ref.shape
+    scale = HEAD_DIM ** (-0.5)
+    tiles = [[] for _ in range(width // LANES)]
+    tangent_tiles = [[] for _ in range(width // LANES)]
+    pairs = width // (2 * HEAD_DIM)
+    blocks = [pl.ds(i * frames, frames) for i in range(rows // frames)]
+
+    def stack(value, start, low):
+        shape = value.shape
+        return jnp.concatenate(
+            [
+                only(value, lane_range(shape, start, low, low + HEAD_DIM)),
+                only(value, lane_range(shape, start, low + HEAD_DIM, low + 2 * HEAD_DIM)),
+            ],
+            axis=0,
+        )
+
+    for pair in range(pairs):
+        low = pair * 2 * HEAD_DIM
+        start, extent = window_of(low, low + 2 * HEAD_DIM)
+        columns = pl.ds(start, extent)
+        keys = [stack(key_ref[b, columns], start, low) for b in blocks]
+        values = [stack(value_ref[b, columns], start, low) for b in blocks]
+        scores = jnp.concatenate(
+            [dot_t(query_ref[b, columns], k) for b, k in zip(blocks, keys)], axis=0
+        )
+        first, top_low, top_high = halves(scores, frames, "max")
+        exponent = jnp.exp2((scores - jnp.where(first, top_low, top_high)) * EXPONENT_SCALE)
+        _, sum_low, sum_high = halves(exponent, frames, "sum")
+        weights = exponent * jnp.where(first, 1.0 / sum_low, 1.0 / sum_high)
+        rounded = weights.astype(jnp.bfloat16)
+        mixed = jnp.concatenate(
+            [
+                dot(rounded[i * frames : (i + 1) * frames], v)
+                for i, v in enumerate(values)
+            ],
+            axis=0,
+        )
+        for tile in range(extent // LANES):
+            tiles[start // LANES + tile].append(mixed[:, tile * LANES : (tile + 1) * LANES])
+        if tangents is not None:
+            query_dot, key_dot, value_dot, _ = tangents
+            score_dots = jnp.concatenate(
+                [
+                    dot_t(query_dot[b, columns], k)
+                    + dot_t(query_ref[b, columns], stack(key_dot[b, columns], start, low))
+                    for b, k in zip(blocks, keys)
+                ],
+                axis=0,
+            ) * scale
+            _, mean_low, mean_high = halves(weights * score_dots, frames, "sum")
+            weight_dots = (
+                weights * (score_dots - jnp.where(first, mean_low, mean_high))
+            ).astype(jnp.bfloat16)
+            mixed_dots = jnp.concatenate(
+                [
+                    dot(
+                        jnp.concatenate(
+                            [
+                                weight_dots[i * frames : (i + 1) * frames],
+                                rounded[i * frames : (i + 1) * frames],
+                            ],
+                            axis=1,
+                        ),
+                        jnp.concatenate(
+                            [v, stack(value_dot[b, columns], start, low)], axis=0
+                        ),
+                    )
+                    for i, (b, v) in enumerate(zip(blocks, values))
+                ],
+                axis=0,
+            )
+            for tile in range(extent // LANES):
+                tangent_tiles[start // LANES + tile].append(
+                    mixed_dots[:, tile * LANES : (tile + 1) * LANES]
+                )
+    for tile in range(width // LANES):
+        columns = pl.ds(tile * LANES, LANES)
+        mixed_ref[:, columns] = functools.reduce(jnp.add, tiles[tile]).astype(jnp.bfloat16)
+        if tangents is not None:
+            tangents[3][:, columns] = functools.reduce(jnp.add, tangent_tiles[tile]).astype(
+                jnp.bfloat16
+            )
+
+
+def arrivals(seat, pieces, came_ref, sems):
+    copies = []
+    for line, piece in enumerate(pieces):
+        neighbours, frames = piece.shape[:2]
+        for index in range(neighbours):
+            first = (seat[1] ^ (line * 2 + index % 2)) * frames * (neighbours // 2)
+            if neighbours > 2:
+                first = first + (seat[0] ^ (index // 2)) * frames
+            copies.append(
+                pltpu.make_async_copy(
+                    piece.at[index], came_ref.at[pl.ds(first, frames)], sems.at[len(copies)]
+                )
+            )
+    return copies
+
+
+def departures(seat, going_ref, pieces, sems):
+    rows = pieces[0].shape[0]
+    return [
+        pltpu.make_async_copy(
+            going_ref.at[pl.ds(pl.multiple_of((seat[1] ^ index) * rows, ROW_TILE), rows)],
+            piece,
+            sems.at[index],
+        )
+        for index, piece in enumerate(pieces)
+    ]
+
+
+def by_position(came_ref, rows_ref):
+    frames, positions, width = came_ref.shape
+    turn = swap_matrix(ROW_TILE, positions)
+    for part in range(frames // ROW_TILE):
+        first = part * ROW_TILE
+        piece = came_ref[first : first + ROW_TILE].reshape(ROW_TILE * positions, width)
+        turned = dot(turn, piece).astype(jnp.bfloat16)
+        for position in range(positions):
+            rows_ref[pl.ds(position * frames + first, ROW_TILE), :] = turned[
+                position * ROW_TILE : (position + 1) * ROW_TILE
+            ]
+
+
+def by_frame(rows_ref, going_ref, frames):
+    positions = rows_ref.shape[0] // frames
+    group = min(frames, 2 * LANES // positions)
+    turn = swap_matrix(positions, group)
+    for part in range(frames // group):
+        piece = jnp.concatenate(
+            [rows_ref[pl.ds(p * frames + part * group, group), :] for p in range(positions)],
+            axis=0,
+        )
+        here = pl.ds(part * group * positions, group * positions)
+        going_ref[here, :] = dot(turn, piece).astype(jnp.bfloat16)
+
+
+def wait_all(copies):
+    for copy in copies:
+        copy.wait()
+
+
+def start_all(copies):
+    for copy in copies:
+        copy.start()
+    return copies
+
+
+def adapted(rows_in, weights_ref, down_ref, up_ref, refs):
+    rank = down_ref.shape[0] // 2
+    low = dot_t(rows_in, down_ref[...]).astype(jnp.bfloat16)
+    first = lane_range(low.shape, 0, 0, rank)
+    refs[0][...] = (
+        dot_t(rows_in, weights_ref[0]) + dot(only(low, first), up_ref[...])
+    ).astype(jnp.bfloat16)
+    refs[1][...] = dot_t(rows_in, weights_ref[1]).astype(jnp.bfloat16)
+    refs[2][...] = (
+        dot_t(rows_in, weights_ref[2]) + dot(only(low, jnp.logical_not(first)), up_ref[...])
+    ).astype(jnp.bfloat16)
+
+
+def student_rows_kernel(layout, counts, seat_ref, shift_ref, down_ref, up_ref, *rest):
+    weight_count, piece_count = counts
+    weight_pieces, rest = rest[:weight_count], rest[weight_count:]
+    pieces, rest = rest[:piece_count], rest[piece_count:]
+    rows_out_ref, primal_ref, weights_ref, came_ref, rows_ref, weight_sems, piece_sems = rest
+    chunk = rows_out_ref.shape[0]
+
+    @pl.when(pl.program_id(0) == 0)
+    def _():
+        weights = weight_copies(seat_ref, layout, weight_pieces, weights_ref, weight_sems)
+        lines = piece_count - 1
+        copies = []
+        for index in range(2 * lines):
+            piece = pieces[lines].at[index // 2] if index % 2 else pieces[index // 2].at[0]
+            count = piece.shape[0]
+            copies.append(
+                pltpu.make_async_copy(
+                    piece,
+                    came_ref.at[pl.ds((seat_ref[1] ^ index) * count, count)],
+                    piece_sems.at[index],
+                )
+            )
+        start_all(copies)
+        start_all(weights)
+        wait_all(copies)
+        by_position(came_ref, rows_ref)
+        wait_all(weights)
+
+    here = pl.ds(pl.multiple_of(pl.program_id(0) * chunk, chunk), chunk)
+    rows_out_ref[...] = rows_ref[here, :]
+    entry = rows_ref[here, :].astype(jnp.float32) + shift_ref[...]
+    normed = (entry * inverse_rms(entry)).astype(jnp.bfloat16)
+    adapted(normed, weights_ref, down_ref, up_ref, [primal_ref.at[i] for i in range(3)])
+
+
+def student_mix_kernel(layout, frames, seat_ref, shift_ref, rows_ref, primal_ref, *rest):
+    weight_pieces, out_refs, rest = rest[:-7], rest[-7:-5], rest[-5:]
+    weights_ref, done_ref, mixed_ref, weight_sems, piece_sems = rest
+    step, chunk = pl.program_id(0), mixed_ref.shape[0]
+    weights = weight_copies(seat_ref, layout, weight_pieces, weights_ref, weight_sems)
+
+    @pl.when(step == 0)
+    def _():
+        start_all(weights)
+
+    time_mix(frames, [primal_ref.at[i] for i in range(3)] + [mixed_ref])
+
+    @pl.when(step == 0)
+    def _():
+        wait_all(weights)
+
+    here = pl.ds(pl.multiple_of(step * chunk, chunk), chunk)
+    entry = rows_ref[...].astype(jnp.float32) + shift_ref[...]
+    done_ref[0, here, :] = (entry + dot(mixed_ref[...], weights_ref[3])).astype(jnp.bfloat16)
+
+    @pl.when(step == pl.num_programs(0) - 1)
+    def _():
+        by_frame(done_ref.at[0], done_ref.at[1], frames)
+        pieces = [ref.at[line] for line in range(out_refs[0].shape[0]) for ref in out_refs]
+        wait_all(start_all(departures(seat_ref, done_ref.at[1], pieces, piece_sems)))
+
+
+def teacher(frames, rows_ref, weights_ref, refs, here):
+    entry = rows_ref[here, :].astype(jnp.float32)
+    normed = (entry * inverse_rms(entry)).astype(jnp.bfloat16)
+    for index, ref in enumerate(refs[:3]):
+        ref[...] = dot_t(normed, weights_ref[index]).astype(jnp.bfloat16)
+    time_mix(frames, refs)
+    entry = rows_ref[here, :].astype(jnp.float32)
+    return (entry + dot(refs[3][...], weights_ref[3])).astype(jnp.bfloat16)
+
+
+def teacher_kernel(layout, counts, seat_ref, *rest):
+    weight_count, piece_count = counts
+    weight_pieces, rest = rest[:weight_count], rest[weight_count:]
+    pieces, rest = rest[:piece_count], rest[piece_count:]
+    velocity_ref, weights_ref, came_ref, rows_ref = rest[:4]
+    refs, (weight_sems, piece_sems) = rest[4:8], rest[8:]
+    frames = came_ref.shape[0]
+    chunk = refs[0].shape[0]
+
+    @pl.when(pl.program_id(0) == 0)
+    def _():
+        came = start_all(arrivals(seat_ref, pieces, came_ref, piece_sems))
+        weights = start_all(
+            weight_copies(seat_ref, layout, weight_pieces, weights_ref, weight_sems)
+        )
+        wait_all(came)
+        by_position(came_ref, rows_ref)
+        wait_all(weights)
+
+    here = pl.ds(pl.multiple_of(pl.program_id(0) * chunk, chunk), chunk)
+    velocity_ref[...] = teacher(frames, rows_ref, weights_ref, refs, here)
+
+
+def tangent_kernel(layout, counts, seat_ref, strength_ref, shift_ref, down_ref, up_ref, *rest):
+    weight_count, piece_count, out_count = counts
+    velocity_ref, noisy_ref, primal_ref = rest[:3]
+    rest = rest[3:]
+    weight_pieces, rest = rest[:weight_count], rest[weight_count:]
+    pieces, rest = rest[:piece_count], rest[piece_count:]
+    out_pieces, rest = rest[:out_count], rest[out_count:]
+    weights_ref, done_ref, going_ref, guided_ref, *tail = rest[-14:]
+    refs, dots, (weight_sems, piece_sems) = tail[:4], tail[4:8], tail[8:10]
+    frames = done_ref.shape[0] // (ROW_TILE // 2)
+    chunk = refs[0].shape[0]
+    step = pl.program_id(0)
+    first = piece_count > 1
+
+    @pl.when(step == 0)
+    def _():
+        weights = weight_copies(seat_ref, layout, weight_pieces, weights_ref, weight_sems)
+        if first:
+            other_ref, came_ref, rows_ref = rest[:3]
+            came = start_all(arrivals(seat_ref, pieces, came_ref, piece_sems))
+        start_all(weights)
+        if first:
+            wait_all(came)
+            by_position(came_ref, rows_ref)
+            half = other_ref.shape[0]
+            other_ref[...] = rows_ref[pl.ds(half, half), :]
+        wait_all(weights)
+
+    here = pl.ds(pl.multiple_of(step * chunk, chunk), chunk)
+    rows_ref = rest[2].at[here] if first else pieces[0]
+    uncond = teacher(frames, rows_ref, weights_ref, refs, slice(None)).astype(jnp.float32)
+    guided = (
+        uncond + strength_ref[0] * (velocity_ref[...].astype(jnp.float32) - uncond)
+    ).astype(jnp.bfloat16)
+    guided_ref[...] = guided
+    guided = guided.astype(jnp.float32)
+    entry = noisy_ref[...].astype(jnp.float32) + shift_ref[...]
+    inverse = inverse_rms(entry)
+    inverse_dot = -(inverse * inverse * inverse) * jnp.mean(
+        entry * guided, axis=-1, keepdims=True
+    )
+    normed_dot = (guided * inverse + entry * inverse_dot).astype(jnp.bfloat16)
+    adapted(normed_dot, weights_ref, down_ref, up_ref, dots)
+    primal = [primal_ref.at[i] for i in range(3)] + [refs[3]]
+    time_mix(frames, primal, dots)
+    done_ref[here, :] = (
+        guided_ref[...].astype(jnp.float32) + dot(dots[3][...], weights_ref[3])
+    ).astype(jnp.bfloat16)
+
+    @pl.when(step == pl.num_programs(0) - 1)
+    def _():
+        by_frame(done_ref, going_ref, frames)
+        wait_all(start_all(departures(seat_ref, going_ref, out_pieces, piece_sems)))
+
+
+IN_VMEM = pl.BlockSpec(memory_space=pltpu.VMEM)
+IN_SMEM = pl.BlockSpec(memory_space=pltpu.SMEM)
+ANYWHERE = pl.BlockSpec(memory_space=pl.ANY)
+
+
+def time_call(kernel, passes, rows, width, **settings):
+    return pl.pallas_call(
+        kernel,
+        compiler_params=pltpu.CompilerParams(vmem_limit_bytes=VMEM_LIMIT),
+        cost_estimate=pl.CostEstimate(
+            flops=int(12 * passes * rows * width * width),
+            bytes_accessed=8 * width * width + 8 * rows * width,
+            transcendentals=rows * LANES * width // HEAD_DIM,
+        ),
+        **settings,
+    )
+
+
+def student_rows(seat, shift, down, up, weights, pieces, frames):
+    weights, layout = weights
+    width = shift.shape[-1]
+    rows, chunk = frames * ROW_TILE, BLOCK * frames
+    vmem = lambda *shape: pltpu.VMEM(shape, jnp.bfloat16)
+    fixed = lambda value: pl.BlockSpec(value.shape, lambda i: (0,) * value.ndim)
+    return time_call(
+        functools.partial(student_rows_kernel, layout, (len(weights), len(pieces))),
+        0.6,
+        rows,
+        width,
+        grid=(rows // chunk,),
+        out_shape=[
+            jax.ShapeDtypeStruct((rows, width), jnp.bfloat16),
+            jax.ShapeDtypeStruct((3, rows, width), jnp.bfloat16),
+        ],
+        in_specs=[IN_SMEM, fixed(shift), fixed(down), fixed(up)]
+        + [ANYWHERE] * (len(weights) + len(pieces)),
+        out_specs=[
+            pl.BlockSpec((chunk, width), lambda i: (i, 0)),
+            pl.BlockSpec((3, chunk, width), lambda i: (0, i, 0)),
+        ],
+        scratch_shapes=[
+            vmem(4, width, width),
+            vmem(frames, ROW_TILE, width),
+            vmem(rows, width),
+            pltpu.SemaphoreType.DMA((len(layout),)),
+            pltpu.SemaphoreType.DMA((2 * len(pieces),)),
+        ],
+    )(seat, shift, down, up, *weights, *pieces)
+
+
+def student_mix(seat, shift, rows_in, primal, weights, frames, seats):
+    weights, layout = weights
+    rows, width = rows_in.shape
+    chunk = BLOCK * frames
+    vmem = lambda *shape: pltpu.VMEM(shape, jnp.bfloat16)
+    piece = jax.ShapeDtypeStruct((seats // 2, rows // seats, width), jnp.bfloat16)
+    return time_call(
+        functools.partial(student_mix_kernel, layout, frames),
+        0.6,
+        rows,
+        width,
+        grid=(rows // chunk,),
+        out_shape=[piece] * 2,
+        in_specs=[
+            IN_SMEM,
+            pl.BlockSpec(shift.shape, lambda i: (0, 0)),
+            pl.BlockSpec((chunk, width), lambda i: (i, 0)),
+            pl.BlockSpec((3, chunk, width), lambda i: (0, i, 0)),
+        ]
+        + [ANYWHERE] * len(weights),
+        out_specs=[ANYWHERE] * 2,
+        scratch_shapes=[
+            vmem(4, width, width),
+            vmem(2, rows, width),
+            vmem(chunk, width),
+            pltpu.SemaphoreType.DMA((len(layout),)),
+            pltpu.SemaphoreType.DMA((seats,)),
+        ],
+    )(seat, shift, rows_in, primal, *weights)
+
+
+def teacher_velocity(seat, weights, pieces, frames):
+    weights, layout = weights
+    width = pieces[0].shape[-1]
+    rows = frames * ROW_TILE
+    vmem = lambda *shape: pltpu.VMEM(shape, jnp.bfloat16)
+    return time_call(
+        functools.partial(teacher_kernel, layout, (len(weights), len(pieces))),
+        1,
+        rows,
+        width,
+        out_shape=jax.ShapeDtypeStruct((rows, width), jnp.bfloat16),
+        grid=(ROW_TILE // BLOCK,),
+        in_specs=[IN_SMEM] + [ANYWHERE] * (len(weights) + len(pieces)),
+        out_specs=pl.BlockSpec((BLOCK * frames, width), lambda i: (i, 0)),
+        scratch_shapes=[
+            vmem(4, width, width),
+            vmem(frames, ROW_TILE, width),
+            vmem(rows, width),
+        ]
+        + [vmem(BLOCK * frames, width)] * 4
+        + [
+            pltpu.SemaphoreType.DMA((len(layout),)),
+            pltpu.SemaphoreType.DMA((4 * len(pieces),)),
+        ],
+    )(seat, *weights, *pieces)
+
+
+def student_tangent(
+    seat, strength, shift, down, up, velocity, noisy, primal, weights, pieces, frames, seats
+):
+    weights, layout = weights
+    first = len(pieces) > 1
+    width = shift.shape[-1]
+    rows = frames * ROW_TILE // 2
+    piece = jax.ShapeDtypeStruct((rows // seats, width), jnp.bfloat16)
+    vmem = lambda *shape: pltpu.VMEM(shape, jnp.bfloat16)
+    chunk = TANGENT_BLOCK * frames
+    steps = rows // chunk
+    part = 0 if first else steps
+    half = pl.BlockSpec((chunk, width), lambda i: (part + i, 0))
+    halves = pl.BlockSpec((3, chunk, width), lambda i: (0, part + i, 0))
+    fixed = lambda value: pl.BlockSpec(value.shape, lambda i: (0,) * value.ndim)
+    other = jax.ShapeDtypeStruct((rows, width), jnp.bfloat16)
+    return time_call(
+        functools.partial(tangent_kernel, layout, (len(weights), len(pieces), seats)),
+        1,
+        rows,
+        width,
+        grid=(steps,),
+        out_shape=[piece] * seats + [other] * first,
+        in_specs=[IN_SMEM] * 2
+        + [fixed(shift), fixed(down), fixed(up), half, half, halves]
+        + [ANYWHERE] * len(weights)
+        + ([ANYWHERE] * len(pieces) if first else [pl.BlockSpec((chunk, width), lambda i: (i, 0))]),
+        out_specs=[ANYWHERE] * seats + [fixed(other)] * first,
+        scratch_shapes=[vmem(frames, ROW_TILE, width), vmem(2 * rows, width)] * first
+        + [vmem(4, width, width), vmem(rows, width), vmem(rows, width)]
+        + [vmem(chunk, width)] * 9
+        + [
+            pltpu.SemaphoreType.DMA((len(layout),)),
+            pltpu.SemaphoreType.DMA((4 * max(4, seats),)),
+        ],
+    )(seat, strength, shift, down, up, velocity, noisy, primal, *weights, *pieces)
+
+
+def place_kernel(count, seat_ref, *rest):
+    result_ref = rest[-1]
+    frames, _, width = result_ref.shape
+    for index in range(count):
+        if len(rest[0].shape) > 2:
+            parts = [rest[index // 2][index % 2].astype(jnp.float32)]
+        else:
+            parts = [piece[...].astype(jnp.float32) for piece in rest[index:-1:count]]
+        parts = [part.reshape(frames, -1, width) for part in parts]
+        start = pl.multiple_of((seat_ref[1] ^ index) * ROW_TILE, ROW_TILE)
+        result_ref[:, pl.ds(start, ROW_TILE), :] = jnp.concatenate(parts, axis=1).astype(
+            jnp.bfloat16
+        )
+
+
+def placed(seat, pieces, seats, frames):
+    width = pieces[0].shape[-1]
+    steps = max(1, frames // 4)
+    half = frames // steps
+
+    def block(piece):
+        lead, (rows, width) = piece.shape[:-2], piece.shape[-2:]
+        return pl.BlockSpec((*lead, rows // steps, width), lambda f: (0,) * len(lead) + (f, 0))
+
+    return pl.pallas_call(
+        functools.partial(place_kernel, seats),
+        out_shape=jax.ShapeDtypeStruct((frames, seats * ROW_TILE, width), jnp.bfloat16),
+        grid=(steps,),
+        in_specs=[IN_SMEM]
+        + [block(piece) for piece in pieces],
+        out_specs=pl.BlockSpec((half, seats * ROW_TILE, width), lambda f: (f, 0, 0)),
+        compiler_params=pltpu.CompilerParams(vmem_limit_bytes=VMEM_LIMIT),
+    )(seat, *pieces)
+
+
+def flip(value, axis, mask):
+    pairs = [(source, source ^ mask) for source in range(lax.axis_size(axis))]
+    return lax.ppermute(value, axis, pairs)
+
+
+def half_weights(qkv, out_weight, core):
+    stacked = jnp.concatenate([jnp.swapaxes(qkv, 1, 2), out_weight[None]], axis=0)
+    return lax.dynamic_slice_in_dim(stacked, core * 2, 2, axis=0)
+
+
+def z_pair(value, across):
+    other = flip(value, "seq", lax.axis_size("seq") // 4)
+    return jnp.where(
+        across % 2 == 0,
+        jnp.concatenate([value, other], axis=1),
+        jnp.concatenate([other, value], axis=1),
+    )
+
+
+def over_middle(near):
+    step = lax.axis_size("seq") // 4
+    pairs = [
+        pair
+        for low in range(step)
+        for pair in ((step + low, 2 * step + low), (2 * step + low, step + low))
+    ]
+    return lax.ppermute(near, "seq", pairs)
+
+
+def to_ends(inside, across):
+    step = lax.axis_size("seq") // 4
+    pairs = [
+        pair
+        for low in range(step)
+        for pair in ((step + low, low), (2 * step + low, 3 * step + low))
+    ]
+    outside = lax.ppermute(inside, "seq", pairs)
+    return jnp.where((across == 1) | (across == 2), inside, outside)
+
+
+NEAR = ((0, 0, 0), (0, 0, 1), (1, 0, 0), (1, 0, 1))
+FAR = ((0, 1, 0), (0, 1, 1), (1, 1, 0), (1, 1, 1))
+
+
+def own_layout():
+    return [(index, None, 0, place) for index, place in enumerate(NEAR + FAR)]
+
+
+def other_core(pieces):
+    swapped = []
+    for piece in pieces:
+        if swapped:
+            piece, swapped[-1] = together(piece, swapped[-1])
+        swapped.append(flip(piece, "clip", 1))
+    return swapped
+
+
+def send(pieces):
+    return [pieces[0]] + [flip(piece, "seq", i) for i, piece in enumerate(pieces) if i > 0]
+
+
+def together(*groups):
+    return lax.optimization_barrier(groups)
+
+
+def along_line(neighbours):
+    pieces = [
+        jnp.stack([given[line] for given in neighbours])
+        for line in range(neighbours[0].shape[0])
+    ]
+    return [flip(piece, "seq", 2 * i) if i > 0 else piece for i, piece in enumerate(pieces)]
+
+
+def over_both(value):
+    size = lax.axis_size("cfg") * lax.axis_size("seq")
+    pairs = [(d, d ^ (size // 2 + 1)) for d in range(size)]
+    return lax.ppermute(value, ("cfg", "seq"), pairs)
+
+
+def to_neighbours(kept, low, across, both):
+    return [kept, flip(low, "seq", 1), flip(across, "cfg", 1), over_both(both)]
+
+
+def on_device(
+    clean,
+    noise,
+    timestep,
+    guidance,
+    condition_vector,
+    empty_prompt_vector,
+    timestep_direction,
+    spatial_query_key_value,
+    spatial_output_weight,
+    temporal_query_key_value,
+    temporal_output_weight,
+    adapter_down_maps,
+    adapter_up_maps,
+):
+    sides, seats = lax.axis_size("cfg"), lax.axis_size("seq")
+    side, place, core = (lax.axis_index(a) for a in ("cfg", "seq", "clip"))
+    frames = clean.shape[0] * seats
+    width = clean.shape[2]
+    seat = jnp.stack([side, place, core]).astype(jnp.int32)
+    moved = timestep[0] * timestep_direction.astype(jnp.float32)
+    cond_shift = (moved + condition_vector.astype(jnp.float32))[None]
+    uncond_shift = (moved + empty_prompt_vector.astype(jnp.float32))[None]
+    down = jnp.swapaxes(adapter_down_maps, 1, 2).reshape(-1, width)
+    up = adapter_up_maps.reshape(-1, sides, 2, 2, seats // 4, HEAD_DIM)
+    up = jnp.swapaxes(up, 3, 4).reshape(-1, width)
+
+    noisy_lines = noisy_pieces(seat, timestep, clean, noise, seats)
+    space_own = half_weights(spatial_query_key_value, spatial_output_weight, core)
+    time_own = half_weights(temporal_query_key_value, temporal_output_weight, core)
+    across = place // (seats // 4)
+
+    space_near = z_pair(space_own, across)
+    space_near, time_own = together(space_near, time_own)
+    space_in = over_middle(space_near)
+    space = [space_near, flip(space_near, "seq", 1), flip(space_near, "cfg", 1)]
+    time_near = z_pair(time_own, across)
+    space_other = other_core([space_near])
+    space, space_other, space_in, time_near = together(space, space_other, space_in, time_near)
+
+    space_far = to_ends(space_in, across)
+    space_xy = flip(space[2], "seq", 1)
+    time_in = over_middle(time_near)
+    time_x = flip(time_near, "cfg", 1)
+    space_other += other_core(space[1:])
+    space += [space_xy, space_far]
+    space, space_other, time_in, time_x, time_near, noisy_lines, down, up = together(
+        space, space_other, time_in, time_x, time_near, noisy_lines, down, up
+    )
+
+    space_far_x = flip(space[4], "cfg", 1)
+    space_far_y = flip(space[4], "seq", 1)
+    time_far = to_ends(time_in, across)
+    space_xy_other, time_near_other = other_core([space[3], time_near])
+    space += [space_far_y, space_far_x]
+    space_other += [space_xy_other]
+    time_other = [time_near_other]
+    space, space_other, time_other, time_far, time_near, time_x, noisy_lines = together(
+        space, space_other, time_other, time_far, time_near, time_x, noisy_lines
+    )
+
+    space_far_xy = flip(space[5], "cfg", 1)
+    time_y = flip(time_near, "seq", 1)
+    noisy_1 = flip(noisy_lines[1], "seq", 2)
+    *space_far_other, time_x_other = other_core(space[4:] + [time_x])
+    space.append(space_far_xy)
+    space_other += space_far_other
+    time_other += [time_x_other]
+    space, space_other, time_x, time_y, time_far, time_near, time_other, noisy_came = together(
+        space, space_other, time_x, time_y, time_far, time_near, time_other,
+        [noisy_lines[0], noisy_1, *noisy_lines[2:]],
+    )
+
+    space_last, time_far_other, time_y_other = (
+        flip(piece, "clip", 1) for piece in (space[7], time_far, time_y)
+    )
+    space_other += [space_last]
+    time_other += [time_far_other, time_y_other]
+    space, space_other, time_x, time_y, time_far, time_near, time_other, noisy_came = together(
+        space, space_other, time_x, time_y, time_far, time_near, time_other, noisy_came
+    )
+    space_weights = (
+        list(space) + list(space_other),
+        [(index, None, index // 8, (NEAR + FAR)[index % 8]) for index in range(16)],
+    )
+    cond, uncond = [
+        functools.partial(
+            spatial_layer, seat, timestep, clean, noise, shift,
+            frames=clean.shape[0] // sides, seats=seats,
+        )
+        for shift in (cond_shift, uncond_shift)
+    ]
+    time_xy = flip(time_y, "cfg", 1)
+    time_far_x = flip(time_far, "cfg", 1)
+    time_far_y = flip(time_far, "seq", 1)
+    noisy_came = list(noisy_came[:2]) + [
+        flip(line, "seq", 2 * index) for index, line in enumerate(noisy_came) if index > 1
+    ]
+    cond = cond(weights=space_weights)
+    cond, time_xy, time_far_x, time_far_y, noisy_came = together(
+        cond, time_xy, time_far_x, time_far_y, noisy_came
+    )
+    time_late = [flip(piece, "clip", 1) for piece in (time_xy, time_far_y, time_far_x)]
+    noisy_low = jnp.stack([line[1] for line in noisy_came])
+    cond, time_far_y, time_late, noisy_low = together(cond, time_far_y, time_late, noisy_low)
+    uncond = uncond(weights=space_weights)
+    time_far_xy = flip(time_far_y, "cfg", 1)
+    noisy_low = flip(noisy_low, "seq", 1)
+    cond, uncond, time_far_xy, noisy_low = together(
+        to_neighbours(*cond), uncond, time_far_xy, noisy_low
+    )
+    lines = [jnp.stack([given[line] for given in cond]) for line in range(seats // 2)]
+    far_lines = [flip(lines[i], "seq", 2 * i) for i in range(2, seats // 2)]
+    time_last = flip(time_far_xy, "clip", 1)
+    uncond, time_last = together(uncond, time_last)
+    time_weights = (
+        [time_near, time_y, time_x, time_xy, time_far, time_far_y, time_far_x, time_far_xy]
+        + list(time_other) + list(time_late) + [time_last],
+        [(index, None, 0, at) for index, at in enumerate(NEAR + FAR)]
+        + [
+            (8 + index, None, 1, at)
+            for index, at in enumerate(
+                [NEAR[0], NEAR[2], FAR[0], NEAR[1], NEAR[3], FAR[1], FAR[2], FAR[3]]
+            )
+        ],
+    )
+    noisy_in = list(noisy_came) + [noisy_low]
+    kept, low, across, both = uncond
+    low, across, both = flip(low, "seq", 1), flip(across, "cfg", 1), over_both(both)
+    rows, primal = student_rows(seat, cond_shift, down, up, time_weights, noisy_in, frames)
+    rows, primal, low, across, both, lines = together(rows, primal, low, across, both, lines)
+    near_line = flip(lines[1], "seq", 2)
+    uncond = along_line([kept, low, across, both])
+    student_kept, student_low = student_mix(
+        seat, cond_shift, rows, primal, time_weights, frames, seats
+    )
+    cond = [lines[0], near_line, *far_lines]
+    student_kept, student_low, cond = together(student_kept, student_low, cond)
+    velocity = teacher_velocity(seat, time_weights, cond, frames)
+    student_low, velocity, uncond = together(flip(student_low, "seq", 1), velocity, uncond)
+    student_back = along_line([student_kept, student_low])
+    tangent = functools.partial(
+        student_tangent, seat, guidance, cond_shift, down, up, velocity, rows, primal,
+        time_weights, frames=frames, seats=seats,
+    )
+    *tangent_pieces, other = tangent(uncond)
+    student_back, other, tangent_pieces = together(student_back, other, tangent_pieces)
+    tangent_back = send(tangent_pieces)
+    rest, tangent_back = together(tangent([other]), tangent_back)
+    tangent_back = list(tangent_back) + send(rest)
+    here = clean.shape[0]
+    return placed(seat, student_back, seats, here), placed(seat, tangent_back, seats, here)
+
+
+def fits(mesh, frames, positions, width):
+    sides, seats = mesh.shape["cfg"], mesh.shape["seq"]
+    groups = sides * seats
+    return (
+        sides == 2
+        and mesh.shape["clip"] == 2
+        and seats == 4 * sides
+        and frames % (groups * ROW_TILE // 4) == 0
+        and frames // groups % PAIR == 0
+        and positions == groups * ROW_TILE
+        and 2 * frames == LANES
+        and width % LANES == 0
+        and width == groups * HEAD_DIM
+    )
+
 def solution(mesh):
-    return jax.shard_map(
-        on_device,
+    specs = dict(
         mesh=mesh,
         in_specs=(
             P(("clip", "seq"), None, None),
@@ -224,3 +1198,10 @@
         out_specs=(P(("clip", "seq"), "cfg", None), P(("clip", "seq"), "cfg", None)),
         check_vma=False,
     )
+
+    def whole(clean, *rest):
+        frames = clean.shape[0] // mesh.shape["clip"]
+        fast = fits(mesh, frames, clean.shape[1], clean.shape[2])
+        return jax.shard_map(on_device if fast else plain_on_device, **specs)(clean, *rest)
+
+    return whole

time: 1180 us -> 461 us (0.39)
  matrix products: 300 us -> 0 us
  waiting for transfers between devices: 421 us -> 121 us
  Pallas kernels: 0 us -> 225 us
  local copies, waits for them, and re-layouts: 230 us -> 28.9 us
  blocking collectives: 110 us -> 0 us
  other arithmetic: 80.7 us -> 8.01 us
  starting transfers between devices: 8.23 us -> 70.9 us
  between operations: 15.9 us -> 3.24 us
    dot_general x27 -> x0, matrix products: 282 us -> none  [the longest x16 118 us: project(): jnp.einsum('...d,dk->...k', rows_in, matrix, preferred_element_type=jnp.f...]
    all_to_all x1 -> x0, waiting for transfers between devices: 275 us -> none  [on_device(): lax.all_to_all(stacked, 'seq', split_axis=3, concat_axis=1, tiled=True)]
    pallas_call x0 -> x10, Pallas kernels: none -> 225 us  [the longest x2 87.2 us: student_tangent(): time_call(functools.partial(tangent_kernel, layout, (len(weights), len(pi...]
    all_to_all x1 -> x0, blocking collectives: 110 us -> none  [on_device(): lax.all_to_all(jnp.stack([primal, tangent]), 'seq', split_axis=1, concat_...]
    all_gather x4 -> x0, waiting for transfers between devices: 92.2 us -> none  [the longest x1 92.2 us: on_device(): lax.all_gather(spatial_query_key_value, ('cfg', 'seq'), axis=2, tiled=True)]
    ppermute x1 -> x68, waiting for transfers between devices: 51 us -> 121 us  [the longest x62 103 us: flip(): return lax.ppermute(value, axis, pairs)]
    ppermute x1 -> x68, starting transfers between devices: 1.6 us -> 70.9 us  [the longest x62 56.4 us: flip(): return lax.ppermute(value, axis, pairs)]
    reshape x8 -> x1, local copies, waits for them, and re-layouts: 69.8 us -> 0.94 us  [on_device(): up = adapter_up_maps.reshape(-1, sides, 2, 2, seats // 4, HEAD_DIM)]
  transfers between devices with their start and end apart: 6 -> 68, of which waited for: 3 -> 26; matrix products, arithmetic and copies ran while one was open for 26% -> 3% of each run, Pallas kernels for 0% -> 49%
where the time goes in v1:
time: 461 us; the launch traced here: 457 us
  Pallas kernels  225 us (49%)
  waiting for transfers between devices  121 us (26%)
  starting transfers between devices  70.9 us (15%)
  local copies, waits for them, and re-layouts  28.9 us (6%)
  other arithmetic  8.01 us (2%)
    ppermute x62, waiting for transfers between devices, flip(): return lax.ppermute(value, axis, pairs)  103 us
    pallas_call x2, Pallas kernels, student_tangent(): time_call(functools.partial(tangent_kernel, layout, (len(weights), len(pi...  87.2 us
    pallas_call x2, Pallas kernels, spatial_layer(): pl.pallas_call(functools.partial(space_kernel, layout, len(pieces), 4), o...  60.4 us
    ppermute x62, starting transfers between devices, flip(): return lax.ppermute(value, axis, pairs)  56.4 us
    pallas_call x1, Pallas kernels, teacher_velocity(): time_call(functools.partial(teacher_kernel, layout, (len(weights), len(pi...  33.1 us
    unnamed x118, local copies, waits for them, and re-layouts  23.4 us
    pallas_call x1, Pallas kernels, student_rows(): time_call(functools.partial(student_rows_kernel, layout, (len(weights), l...  19.6 us
    pallas_call x1, Pallas kernels, student_mix(): time_call(functools.partial(student_mix_kernel, layout, frames), 0.6, row...  17.7 us
  transfers between devices with their start and end apart: 68, of which 26 were waited for; matrix products, arithmetic and copies ran while one was open for 3% of the time, Pallas kernels for 49%

profile of v1, /device:TPU:8, one launch (start us, length us, event | category | flops | bytes accessed | tf_op | source)
XLA Modules:
  0.0 457.0 jit_solution(16574178837495259093)
XLA Ops:
  3.0 8.4 %collective-permute-done = bf16[2,72,1152]{2,1,0:T(8,128)(2,1)S(1)} collective-permute-done((bf16[2,72,1152]{2,1,0:T(8,128)(2,1)S(1)}, bf16[2,72,1152]{2,1,0:T(8,128)(2,1)S(1)}, u32[]{:S(2)}, u32[]{:S(2)}) %collective-permute-start) | collective-permute-done | bytes 331808 | tf_op jit(solution)/shard_map/ppermute | solution.py:930
  11.6 3.5 collective-permute-start.4
  15.2 1.6 collective-permute-start.2
  16.7 1.5 collective-permute-start.1
  18.2 9.6 %collective-permute-done.5 = bf16[2,72,1152]{2,1,0:T(8,128)(2,1)S(1)} collective-permute-done((bf16[2,72,1152]{2,1,0:T(8,128)(2,1)S(1)}, bf16[2,72,1152]{2,1,0:T(8,128)(2,1)S(1)}, u32[]{:S(2)}, u32[]{:S(2)}) %collective-permute-start.5) | collective-permute-done | bytes 331808 | tf_op jit(solution)/shard_map/ppermute | solution.py:930
  28.0 1.3 collective-permute-done.4
  29.3 3.2 collective-permute-done.2.rest_2_
  34.5 2.1 collective-permute-start.7
  37.2 3.6 collective-permute-start.10
  40.8 1.6 collective-permute-start.6
  46.1 2.3 copy-done
  48.4 2.3 copy-done.1
  50.7 2.6 shard_map.140
  53.4 1.4 broadcast_select_fusion.1.rest_4_
  54.8 2.9 collective-permute-done.6.rest_3_
  57.8 1.8 collective-permute-start.16
  59.6 1.6 collective-permute-start.13
  61.1 1.5 collective-permute-start.12
  62.7 11.8 %collective-permute-done.16 = bf16[2,144,1152]{2,1,0:T(8,128)(2,1)S(1)} collective-permute-done((bf16[2,144,1152]{2,1,0:T(8,128)(2,1)}, bf16[2,144,1152]{2,1,0:T(8,128)(2,1)S(1)}, u32[]{:S(2)}, u32[]{:S(2)}) %collective-permute-start.16) | collective-permute-done | bytes 663584 | tf_op jit(solution)/shard_map/ppermute | solution.py:964
  75.7 1.3 collective-permute-done.13.rest_6_
  76.9 1.2 collective-permute-done.12.rest_5_
  79.1 2.1 collective-permute-done.18.rest_12_
  81.3 2.0 collective-permute-done.19.rest_13_
  84.0 1.5 collective-permute-start.21
  85.5 15.7 %collective-permute-done.23.rest_17_ = bf16[2,8,16,1152]{3,2,1,0:T(8,128)(2,1)S(1)} collective-permute-done((bf16[2,8,16,1152]{3,2,1,0:T(8,128)(2,1)S(1)}, bf16[2,8,16,1152]{3,2,1,0:T(8,128)(2,1)S(1)}, u32[]{:S(2)}, u32[]{:S(2)}) %collective-permute-start.23) | collective-permute-done | bytes 589856 | tf_op jit(solution)/shard_map/ppermute | solution.py:930
  105.3 1.4 collective-permute-start.29
  109.1 1.4 collective-permute-start.27
  110.6 30.2 %shard_map.141 = (bf16[4,4,16,1152]{3,2,1,0:T(8,128)(2,1)S(1)}, bf16[4,4,16,1152]{3,2,1,0:T(8,128)(2,1)S(1)}, bf16[4,4,16,1152]{3,2,1,0:T(8,128)(2,1)S(1)}, bf16[4,4,16,1152]{3,2,1,0:T(8,128)(2,1)S(1)}) custom-call(s32[3]{0:T(128)S(1)} %pad_add_fusion.seat_ref, f32[1]{0:T(128)} %copy.20.moment_ref, bf16[8,256,1152]{2,1,0:T(8,128)(2,1)} %clean_ref.5, ...), custom_call_target="tpu_custom_call" | custom-call | flops 19025362944 | bytes 17694720 | tf_op jit(solution)/shard_map/pallas_call | solution.py:383
  147.5 12.3 %collective-permute-done.31.rest_19_ = bf16[2,8,16,1152]{3,2,1,0:T(8,128)(2,1)S(1)} collective-permute-done((bf16[2,8,16,1152]{3,2,1,0:T(8,128)(2,1)S(1)}, bf16[2,8,16,1152]{3,2,1,0:T(8,128)(2,1)S(1)}, u32[]{:S(2)}, u32[]{:S(2)}) %collective-permute-start.31) | collective-permute-done | bytes 589856 | tf_op jit(solution)/shard_map/ppermute | solution.py:930
  164.4 1.6 collective-permute-start.35
  166.5 1.4 collective-permute-start.37
  167.9 1.4 collective-permute-start.38
  176.5 30.3 %shard_map.142 = (bf16[4,4,16,1152]{3,2,1,0:T(8,128)(2,1)S(1)}, bf16[4,4,16,1152]{3,2,1,0:T(8,128)(2,1)S(1)}, bf16[4,4,16,1152]{3,2,1,0:T(8,128)(2,1)S(1)}, bf16[4,4,16,1152]{3,2,1,0:T(8,128)(2,1)S(1)}) custom-call(s32[3]{0:T(128)S(1)} %pad_add_fusion.seat_ref, f32[1]{0:T(128)} %copy.20.moment_ref, bf16[8,256,1152]{2,1,0:T(8,128)(2,1)} %clean_ref.5, ...), custom_call_target="tpu_custom_call" | custom-call | flops 19025362944 | bytes 17694720 | tf_op jit(solution)/shard_map/pallas_call | solution.py:383
  206.9 1.6 collective-permute-done.38.rest_7_.rest_10_
  208.5 9.8 %collective-permute-done.39.rest_20_ = bf16[4,8,16,1152]{3,2,1,0:T(8,128)(2,1)S(1)} collective-permute-done((bf16[4,8,16,1152]{3,2,1,0:T(8,128)(2,1)S(1)}, bf16[4,8,16,1152]{3,2,1,0:T(8,128)(2,1)S(1)}, u32[]{:S(2)}, u32[]{:S(2)}) %collective-permute-start.39) | collective-permute-done | bytes 1179680 | tf_op jit(solution)/shard_map/ppermute | solution.py:930
  219.6 1.2 collective-permute-start.46
  222.6 2.0 collective-permute-start.43
  224.7 19.6 %shard_map.143 = (bf16[1024,1152]{1,0:T(8,128)(2,1)}, bf16[3,1024,1152]{2,1,0:T(8,128)(2,1)}) custom-call(s32[3]{0:T(128)S(1)} %pad_add_fusion.seat_ref, f32[1,1152]{1,0:T(1,128)S(1)} %broadcast_in_dim.12.shift_ref, bf16[128,1152]{1,0:T(8,128)(2,1)S(1)} %bitcast.14, bf16[128,1152]{1,0:T(8,128)(2,1)S(1)} %copy.17.up_ref, ...), custom_call_target="tpu_custom_call" | custom-call | flops 9784472576 | bytes 20054016 | tf_op jit(solution)/shard_map/pallas_call | solution.py:771
  244.3 5.3 %collective-permute-done.43 = bf16[4,4,16,1152]{3,2,1,0:T(8,128)(2,1)S(1)} collective-permute-done((bf16[4,4,16,1152]{3,2,1,0:T(8,128)(2,1)S(1)}, bf16[4,4,16,1152]{3,2,1,0:T(8,128)(2,1)S(1)}, u32[]{:S(2)}, u32[]{:S(2)}) %collective-permute-start.43) | collective-permute-done | bytes 589856 | tf_op jit(solution)/shard_map/ppermute | solution.py:1004
  249.9 3.0 collective-permute-start.48
  254.4 2.0 collective-permute-start.44
  257.4 17.7 %shard_map.144 = (bf16[4,128,1152]{2,1,0:T(8,128)(2,1)S(1)}, bf16[4,128,1152]{2,1,0:T(8,128)(2,1)S(1)}) custom-call(s32[3]{0:T(128)S(1)} %pad_add_fusion.seat_ref, f32[1,1152]{1,0:T(1,128)S(1)} %broadcast_in_dim.12.shift_ref, bf16[1024,1152]{1,0:T(8,128)(2,1)} %get-tuple-element.380.rows_ref.rest_1_, ...), custom_call_target="tpu_custom_call" | custom-call | flops 9784472576 | bytes 20054016 | tf_op jit(solution)/shard_map/pallas_call | solution.py:803
  276.1 9.3 %collective-permute-done.46.rest_19_ = bf16[4,4,16,1152]{3,2,1,0:T(8,128)(2,1)S(1)} collective-permute-done((bf16[4,4,16,1152]{3,2,1,0:T(8,128)(2,1)S(1)}, bf16[4,4,16,1152]{3,2,1,0:T(8,128)(2,1)S(1)}, u32[]{:S(2)}, u32[]{:S(2)}) %collective-permute-start.46) | collective-permute-done | bytes 589856 | tf_op jit(solution)/shard_map/ppermute | solution.py:930
  285.4 7.1 %collective-permute-done.44.rest_17_ = bf16[4,4,16,1152]{3,2,1,0:T(8,128)(2,1)S(1)} collective-permute-done((bf16[4,4,16,1152]{3,2,1,0:T(8,128)(2,1)S(1)}, bf16[4,4,16,1152]{3,2,1,0:T(8,128)(2,1)S(1)}, u32[]{:S(2)}, u32[]{:S(2)}) %collective-permute-start.44) | collective-permute-done | bytes 589856 | tf_op jit(solution)/shard_map/ppermute | solution.py:930
  292.4 1.5 collective-permute-start.47
  293.9 33.1 %shard_map.145.rest_0_ = bf16[1024,1152]{1,0:T(8,128)(2,1)} custom-call(s32[3]{0:T(128)S(1)} %pad_add_fusion.seat_ref, bf16[2,144,1152]{2,1,0:T(8,128)(2,1)S(1)} %maximum_select_fusion.1.rest_0_.rest_3_, bf16[2,144,1152]{2,1,0:T(8,128)(2,1)S(1)} %copy-done.14, bf16[2,144,1152]{2,1,0:T(8,128)(2,1)} %collective-permute-done.11.rest_2_.rest_5_, ...), custom_call_target="tpu_custom_call" | custom-call | flops 16307453952 | bytes 20054016 | tf_op jit(solution)/shard_map/pallas_call | solution.py:833
  327.5 2.1 collective-permute-start.52
  329.6 1.5 collective-permute-start.53
  331.2 46.0 %shard_map.146 = (bf16[64,1152]{1,0:T(8,128)(2,1)S(1)}, bf16[64,1152]{1,0:T(8,128)(2,1)S(1)}, bf16[64,1152]{1,0:T(8,128)(2,1)S(1)}, bf16[64,1152]{1,0:T(8,128)(2...) custom-call(s32[3]{0:T(128)S(1)} %pad_add_fusion.seat_ref, ...), custom_call_target="tpu_custom_call" | custom-call | flops 8153726976 | bytes 15335424 | tf_op jit(solution)/shard_map/pallas_call | solution.py:871
  378.7 2.1 collective-permute-start.56
  381.7 1.9 collective-permute-start.58
  384.8 2.4 collective-permute-done.55.rest_2_
  387.2 2.0 collective-permute-start.60
  389.3 1.3 copy-done.52
  390.5 41.2 %shard_map.148 = (bf16[64,1152]{1,0:T(8,128)(2,1)S(1)}, bf16[64,1152]{1,0:T(8,128)(2,1)S(1)}, bf16[64,1152]{1,0:T(8,128)(2,1)S(1)}, bf16[64,1152]{1,0:T(8,128)(2...) custom-call(s32[3]{0:T(128)S(1)} %pad_add_fusion.seat_ref, ...), custom_call_target="tpu_custom_call" | custom-call | flops 8153726976 | bytes 15335424 | tf_op jit(solution)/shard_map/pallas_call | solution.py:871
  432.7 3.4 collective-permute-start.62
  436.7 2.5 collective-permute-start.64
  440.6 1.9 collective-permute-start.67
  442.6 2.1 shard_map.147
  444.7 1.9 collective-permute-done.64.rest_12_
  446.6 3.1 collective-permute-done.65.rest_13_
  449.7 3.1 collective-permute-done.66.rest_14_
  452.8 1.9 collective-permute-done.67.rest_15_
  454.7 2.1 shard_map.149
  (241 shorter events, 49.7 us)
Async XLA Ops:
  1.8 9.6 %collective-permute-start = (bf16[2,72,1152]{2,1,0:T(8,128)(2,1)S(1)}, bf16[2,72,1152]{2,1,0:T(8,128)(2,1)S(1)}, u32[]{:S(2)}, u32[]{:S(2)}) collective-permute-start(bf16[2,72,1152]{2,1,0:T(8,128)(2,1)S(1)} %fusion.1), channel_id=1, source_target_pairs={{0,4},{2,6},{4,0},{6,2},{8,12},{10,14},{12,8},{14,10},{1,5},{3,7},... | collective-permute-start | bytes 995336 | tf_op jit(solution)/shard_map/ppermute | solution.py:930
  11.6 17.7 %collective-permute-start.4 = (bf16[2,144,1152]{2,1,0:T(8,128)(2,1)S(1)}, bf16[2,144,1152]{2,1,0:T(8,128)(2,1)}, u32[]{:S(2)}, u32[]{:S(2)}) collective-permute-start(bf16[2,144,1152]{2,1,0:T(8,128)(2,1)S(1)} %maximum_select_fusion.rest_0_), channel_id=1, source_target_pairs={{4,8},{8,4},{6,10},{10,6},{5,9},{9,5},{7,11},{11,7},{20,24},{24,20... | collective-permute-start | bytes 1990664 | tf_op jit(solution)/shard_map/ppermute | solution.py:954
  15.1 14.3 %collective-permute-start.3 = (bf16[2,144,1152]{2,1,0:T(8,128)(2,1)S(1)}, bf16[2,144,1152]{2,1,0:T(8,128)(2,1)S(1)}, u32[]{:S(2)}, u32[]{:S(2)}) collective-permute-start(bf16[2,144,1152]{2,1,0:T(8,128)(2,1)S(1)} %maximum_select_fusion.rest_0_), channel_id=1, source_target_pairs={{0,1},{1,0},{2,3},{3,2},{4,5},{5,4},{6,7},{7,6},{8,9},{9,8},{10,11... | collective-permute-start | bytes 1990664 | tf_op jit(solution)/shard_map/ppermute | solution.py:930
  15.2 17.4 %collective-permute-start.2 = (bf16[2,144,1152]{2,1,0:T(8,128)(2,1)S(1)}, bf16[2,144,1152]{2,1,0:T(8,128)(2,1)}, u32[]{:S(2)}, u32[]{:S(2)}) collective-permute-start(bf16[2,144,1152]{2,1,0:T(8,128)(2,1)S(1)} %maximum_select_fusion.rest_0_), channel_id=1, source_target_pairs={{0,16},{16,0},{1,17},{17,1},{2,18},{18,2},{3,19},{19,3},{4,20},{20... | collective-permute-start | bytes 1990664 | tf_op jit(solution)/shard_map/ppermute | solution.py:930
  16.7 17.0 %collective-permute-start.1 = (bf16[2,144,1152]{2,1,0:T(8,128)(2,1)S(1)}, bf16[2,144,1152]{2,1,0:T(8,128)(2,1)S(1)}, u32[]{:S(2)}, u32[]{:S(2)}) collective-permute-start(bf16[2,144,1152]{2,1,0:T(8,128)(2,1)S(1)} %maximum_select_fusion.rest_0_), channel_id=1, source_target_pairs={{0,2},{2,0},{4,6},{6,4},{8,10},{10,8},{12,14},{14,12},{1,3},{3,1},... | collective-permute-start | bytes 1990664 | tf_op jit(solution)/shard_map/ppermute | solution.py:930
  18.2 9.6 %collective-permute-start.5 = (bf16[2,72,1152]{2,1,0:T(8,128)(2,1)S(1)}, bf16[2,72,1152]{2,1,0:T(8,128)(2,1)S(1)}, u32[]{:S(2)}, u32[]{:S(2)}) collective-permute-start(bf16[2,72,1152]{2,1,0:T(8,128)(2,1)S(1)} %fusion), channel_id=1, source_target_pairs={{0,4},{2,6},{4,0},{6,2},{8,12},{10,14},{12,8},{14,10},{1,5},{3,7},... | collective-permute-start | bytes 995336 | tf_op jit(solution)/shard_map/ppermute | solution.py:930
  33.7 8.7 %collective-permute-start.8 = (bf16[2,144,1152]{2,1,0:T(8,128)(2,1)S(1)}, bf16[2,144,1152]{2,1,0:T(8,128)(2,1)S(1)}, u32[]{:S(2)}, u32[]{:S(2)}) collective-permute-start(bf16[2,144,1152]{2,1,0:T(8,128)(2,1)S(1)} %collective-permute-done.1.rest_1_), channel_id=1, source_target_pairs={{0,1},{1,0},{2,3},{3,2},{4,5},{5,4},{6,7},{7,6},{8,9},{9,8},{10,11... | collective-permute-start | bytes 1990664 | tf_op jit(solution)/shard_map/ppermute | solution.py:930
  34.5 18.8 %collective-permute-start.7 = (bf16[2,144,1152]{2,1,0:T(8,128)(2,1)}, bf16[2,144,1152]{2,1,0:T(8,128)(2,1)}, u32[]{:S(2)}, u32[]{:S(2)}) collective-permute-start(bf16[2,144,1152]{2,1,0:T(8,128)(2,1)} %collective-permute-done.4), channel_id=1, source_target_pairs={{4,0},{8,12},{6,2},{10,14},{5,1},{9,13},{7,3},{11,15},{20,16},{24,... | collective-permute-start | bytes 1990664 | tf_op jit(solution)/shard_map/ppermute | solution.py:964
  36.7 21.0 %collective-permute-start.11 = (bf16[2,144,1152]{2,1,0:T(8,128)(2,1)S(1)}, bf16[2,144,1152]{2,1,0:T(8,128)(2,1)}, u32[]{:S(2)}, u32[]{:S(2)}) collective-permute-start(bf16[2,144,1152]{2,1,0:T(8,128)(2,1)S(1)} %maximum_select_fusion.1.rest_0_.rest_3_), channel_id=1, source_target_pairs={{0,16},{16,0},{1,17},{17,1},{2,18},{18,2},{3,19},{19,3},{4,20},{20... | collective-permute-start | bytes 1990664 | tf_op jit(solution)/shard_map/ppermute | solution.py:930
  37.2 20.5 %collective-permute-start.10 = (bf16[2,144,1152]{2,1,0:T(8,128)(2,1)S(1)}, bf16[2,144,1152]{2,1,0:T(8,128)(2,1)}, u32[]{:S(2)}, u32[]{:S(2)}) collective-permute-start(bf16[2,144,1152]{2,1,0:T(8,128)(2,1)S(1)} %maximum_select_fusion.1.rest_0_.rest_3_), channel_id=1, source_target_pairs={{4,8},{8,4},{6,10},{10,6},{5,9},{9,5},{7,11},{11,7},{20,24},{24,20... | collective-permute-start | bytes 1990664 | tf_op jit(solution)/shard_map/ppermute | solution.py:954
  40.8 16.9 %collective-permute-start.6 = (bf16[2,144,1152]{2,1,0:T(8,128)(2,1)}, bf16[2,144,1152]{2,1,0:T(8,128)(2,1)}, u32[]{:S(2)}, u32[]{:S(2)}) collective-permute-start(bf16[2,144,1152]{2,1,0:T(8,128)(2,1)} %collective-permute-done.2.rest_2_), channel_id=1, source_target_pairs={{0,2},{2,0},{4,6},{6,4},{8,10},{10,8},{12,14},{14,12},{1,3},{3,1},... | collective-permute-start | bytes 1990664 | tf_op jit(solution)/shard_map/ppermute | solution.py:930
  43.3 14.4 %collective-permute-start.9 = (bf16[2,144,1152]{2,1,0:T(8,128)(2,1)}, bf16[2,144,1152]{2,1,0:T(8,128)(2,1)}, u32[]{:S(2)}, u32[]{:S(2)}) collective-permute-start(bf16[2,144,1152]{2,1,0:T(8,128)(2,1)} %collective-permute-done.2.rest_2_), channel_id=1, source_target_pairs={{0,1},{1,0},{2,3},{3,2},{4,5},{5,4},{6,7},{7,6},{8,9},{9,8},{10,11... | collective-permute-start | bytes 1990664 | tf_op jit(solution)/shard_map/ppermute | solution.py:930
  57.7 5.0 %collective-permute-start.14 = (bf16[2,144,1152]{2,1,0:T(8,128)(2,1)}, bf16[2,144,1152]{2,1,0:T(8,128)(2,1)S(1)}, u32[]{:S(2)}, u32[]{:S(2)}) collective-permute-start(bf16[2,144,1152]{2,1,0:T(8,128)(2,1)} %collective-permute-done.6.rest_3_), channel_id=1, source_target_pairs={{0,1},{1,0},{2,3},{3,2},{4,5},{5,4},{6,7},{7,6},{8,9},{9,8},{10,11... | collective-permute-start | bytes 1990664 | tf_op jit(solution)/shard_map/ppermute | solution.py:930
  57.8 16.7 %collective-permute-start.16 = (bf16[2,144,1152]{2,1,0:T(8,128)(2,1)}, bf16[2,144,1152]{2,1,0:T(8,128)(2,1)S(1)}, u32[]{:S(2)}, u32[]{:S(2)}) collective-permute-start(bf16[2,144,1152]{2,1,0:T(8,128)(2,1)} %collective-permute-done.10), channel_id=1, source_target_pairs={{4,0},{8,12},{6,2},{10,14},{5,1},{9,13},{7,3},{11,15},{20,16},{24,... | collective-permute-start | bytes 1990664 | tf_op jit(solution)/shard_map/ppermute | solution.py:964
  59.6 17.4 %collective-permute-start.13 = (bf16[2,144,1152]{2,1,0:T(8,128)(2,1)S(1)}, bf16[2,144,1152]{2,1,0:T(8,128)(2,1)S(1)}, u32[]{:S(2)}, u32[]{:S(2)}) collective-permute-start(bf16[2,144,1152]{2,1,0:T(8,128)(2,1)S(1)} %broadcast_select_fusion.1.rest_4_), channel_id=1, source_target_pairs={{0,16},{16,0},{1,17},{17,1},{2,18},{18,2},{3,19},{19,3},{4,20},{20... | collective-permute-start | bytes 1990664 | tf_op jit(solution)/shard_map/ppermute | solution.py:930
  61.1 17.0 %collective-permute-start.12 = (bf16[2,144,1152]{2,1,0:T(8,128)(2,1)S(1)}, bf16[2,144,1152]{2,1,0:T(8,128)(2,1)S(1)}, u32[]{:S(2)}, u32[]{:S(2)}) collective-permute-start(bf16[2,144,1152]{2,1,0:T(8,128)(2,1)S(1)} %broadcast_select_fusion.1.rest_4_), channel_id=1, source_target_pairs={{0,2},{2,0},{4,6},{6,4},{8,10},{10,8},{12,14},{14,12},{1,3},{3,1},... | collective-permute-start | bytes 1990664 | tf_op jit(solution)/shard_map/ppermute | solution.py:930
  62.7 15.5 %collective-permute-start.15 = (bf16[2,144,1152]{2,1,0:T(8,128)(2,1)S(1)}, bf16[2,144,1152]{2,1,0:T(8,128)(2,1)S(1)}, u32[]{:S(2)}, u32[]{:S(2)}) collective-permute-start(bf16[2,144,1152]{2,1,0:T(8,128)(2,1)S(1)} %maximum_select_fusion.1.rest_0_.rest_3_), channel_id=1, source_target_pairs={{0,1},{1,0},{2,3},{3,2},{4,5},{5,4},{6,7},{7,6},{8,9},{9,8},{10,11... | collective-permute-start | bytes 1990664 | tf_op jit(solution)/shard_map/ppermute | solution.py:930
  83.4 17.8 %collective-permute-start.17 = (bf16[2,144,1152]{2,1,0:T(8,128)(2,1)S(1)}, bf16[2,144,1152]{2,1,0:T(8,128)(2,1)S(1)}, u32[]{:S(2)}, u32[]{:S(2)}) collective-permute-start(bf16[2,144,1152]{2,1,0:T(8,128)(2,1)S(1)} %collective-permute-done.12.rest_5_), channel_id=1, source_target_pairs={{0,16},{16,0},{1,17},{17,1},{2,18},{18,2},{3,19},{19,3},{4,20},{20... | collective-permute-start | bytes 1990664 | tf_op jit(solution)/shard_map/ppermute | solution.py:930
  84.0 17.3 %collective-permute-start.21 = (bf16[2,144,1152]{2,1,0:T(8,128)(2,1)S(1)}, bf16[2,144,1152]{2,1,0:T(8,128)(2,1)S(1)}, u32[]{:S(2)}, u32[]{:S(2)}) collective-permute-start(bf16[2,144,1152]{2,1,0:T(8,128)(2,1)S(1)} %maximum_select_fusion.1.rest_0_.rest_3_), channel_id=1, source_target_pairs={{0,2},{2,0},{4,6},{6,4},{8,10},{10,8},{12,14},{14,12},{1,3},{3,1},... | collective-permute-start | bytes 1990664 | tf_op jit(solution)/shard_map/ppermute | solution.py:930
  85.5 15.8 %collective-permute-start.22 = (bf16[2,144,1152]{2,1,0:T(8,128)(2,1)}, bf16[2,144,1152]{2,1,0:T(8,128)(2,1)S(1)}, u32[]{:S(2)}, u32[]{:S(2)}) collective-permute-start(bf16[2,144,1152]{2,1,0:T(8,128)(2,1)} %collective-permute-done.11.rest_2_.rest_5_), channel_id=1, source_target_pairs={{0,1},{1,0},{2,3},{3,2},{4,5},{5,4},{6,7},{7,6},{8,9},{9,8},{10,11... | collective-permute-start | bytes 1990664 | tf_op jit(solution)/shard_map/ppermute | solution.py:930
  85.5 15.7 %collective-permute-start.23 = (bf16[2,8,16,1152]{3,2,1,0:T(8,128)(2,1)S(1)}, bf16[2,8,16,1152]{3,2,1,0:T(8,128)(2,1)S(1)}, u32[]{:S(2)}, u32[]{:S(2)}) collective-permute-start(bf16[2,8,16,1152]{3,2,1,0:T(8,128)(2,1)S(1)} %get-tuple-element.280), channel_id=1, source_target_pairs={{0,4},{2,6},{4,0},{6,2},{8,12},{10,14},{12,8},{14,10},{1,5},{3,7},... | collective-permute-start | bytes 1769480 | tf_op jit(solution)/shard_map/ppermute | solution.py:930
  102.0 2.4 collective-permute-start.26
  102.0 3.3 collective-permute-start.25
  105.3 54.5 %collective-permute-start.29 = (bf16[2,144,1152]{2,1,0:T(8,128)(2,1)S(1)}, bf16[2,144,1152]{2,1,0:T(8,128)(2,1)}, u32[]{:S(2)}, u32[]{:S(2)}) collective-permute-start(bf16[2,144,1152]{2,1,0:T(8,128)(2,1)S(1)} %broadcast_select_fusion.rest_4_.rest_7_), channel_id=1, source_target_pairs={{0,2},{2,0},{4,6},{6,4},{8,10},{10,8},{12,14},{14,12},{1,3},{3,1},... | collective-permute-start | bytes 1990664 | tf_op jit(solution)/shard_map/ppermute | solution.py:930
  106.8 53.0 %collective-permute-start.28 = (bf16[2,144,1152]{2,1,0:T(8,128)(2,1)S(1)}, bf16[2,144,1152]{2,1,0:T(8,128)(2,1)}, u32[]{:S(2)}, u32[]{:S(2)}) collective-permute-start(bf16[2,144,1152]{2,1,0:T(8,128)(2,1)S(1)} %broadcast_select_fusion.rest_4_.rest_7_), channel_id=1, source_target_pairs={{0,16},{16,0},{1,17},{17,1},{2,18},{18,2},{3,19},{19,3},{4,20},{20... | collective-permute-start | bytes 1990664 | tf_op jit(solution)/shard_map/ppermute | solution.py:930
  108.0 39.5 %collective-permute-start.30 = (bf16[2,8,16,1152]{3,2,1,0:T(8,128)(2,1)S(1)}, bf16[2,8,16,1152]{3,2,1,0:T(8,128)(2,1)S(1)}, u32[]{:S(2)}, u32[]{:S(2)}) collective-permute-start(bf16[2,8,16,1152]{3,2,1,0:T(8,128)(2,1)S(1)} %get-tuple-element.334), channel_id=1, source_target_pairs={{0,8},{2,10},{4,12},{6,14},{8,0},{10,2},{12,4},{14,6},{1,9},{3,11}... | collective-permute-start | bytes 1769480 | tf_op jit(solution)/shard_map/ppermute | solution.py:930
  108.0 51.8 %collective-permute-start.31 = (bf16[2,8,16,1152]{3,2,1,0:T(8,128)(2,1)S(1)}, bf16[2,8,16,1152]{3,2,1,0:T(8,128)(2,1)S(1)}, u32[]{:S(2)}, u32[]{:S(2)}) collective-permute-start(bf16[2,8,16,1152]{3,2,1,0:T(8,128)(2,1)S(1)} %get-tuple-element.335), channel_id=1, source_target_pairs={{0,12},{2,14},{4,8},{6,10},{8,4},{10,6},{12,0},{14,2},{1,13},{3,15... | collective-permute-start | bytes 1769480 | tf_op jit(solution)/shard_map/ppermute | solution.py:930
  109.1 50.7 %collective-permute-start.27 = (bf16[2,144,1152]{2,1,0:T(8,128)(2,1)S(1)}, bf16[2,144,1152]{2,1,0:T(8,128)(2,1)}, u32[]{:S(2)}, u32[]{:S(2)}) collective-permute-start(bf16[2,144,1152]{2,1,0:T(8,128)(2,1)S(1)} %collective-permute-done.21.rest_1_.rest_4_), channel_id=1, source_target_pairs={{0,16},{16,0},{1,17},{17,1},{2,18},{18,2},{3,19},{19,3},{4,20},{20... | collective-permute-start | bytes 1990664 | tf_op jit(solution)/shard_map/ppermute | solution.py:930
  159.8 4.5 collective-permute-start.33
  159.9 4.4 collective-permute-start.32
  160.4 3.9 collective-permute-start.34
  164.4 42.5 %collective-permute-start.35 = (bf16[4,4,16,1152]{3,2,1,0:T(8,128)(2,1)}, bf16[4,4,16,1152]{3,2,1,0:T(8,128)(2,1)S(1)}, u32[]{:S(2)}, u32[]{:S(2)}) collective-permute-start(bf16[4,4,16,1152]{3,2,1,0:T(8,128)(2,1)} %copy-done.50), channel_id=1, source_target_pairs={{0,2},{2,0},{4,6},{6,4},{8,10},{10,8},{12,14},{14,12},{1,3},{3,1},... | collective-permute-start | bytes 1769480 | tf_op jit(solution)/shard_map/ppermute | solution.py:930
  165.9 40.9 %collective-permute-start.36 = (bf16[4,4,16,1152]{3,2,1,0:T(8,128)(2,1)}, bf16[4,4,16,1152]{3,2,1,0:T(8,128)(2,1)S(1)}, u32[]{:S(2)}, u32[]{:S(2)}) collective-permute-start(bf16[4,4,16,1152]{3,2,1,0:T(8,128)(2,1)} %copy-done.49), channel_id=1, source_target_pairs={{0,16},{16,0},{1,17},{17,1},{2,18},{18,2},{3,19},{19,3},{4,20},{20... | collective-permute-start | bytes 1769480 | tf_op jit(solution)/shard_map/ppermute | solution.py:930
  166.5 40.4 %collective-permute-start.37 = (bf16[4,4,16,1152]{3,2,1,0:T(8,128)(2,1)}, bf16[4,4,16,1152]{3,2,1,0:T(8,128)(2,1)S(1)}, u32[]{:S(2)}, u32[]{:S(2)}) collective-permute-start(bf16[4,4,16,1152]{3,2,1,0:T(8,128)(2,1)} %copy-done.48), channel_id=1, source_target_pairs={{0,18},{2,16},{4,22},{6,20},{8,26},{10,24},{12,30},{14,28},{16,2},... | collective-permute-start | bytes 1769480 | tf_op jit(solution)/shard_map/ppermute | solution.py:1004
  167.9 40.5 %collective-permute-start.38 = (bf16[2,144,1152]{2,1,0:T(8,128)(2,1)}, bf16[2,144,1152]{2,1,0:T(8,128)(2,1)S(1)}, u32[]{:S(2)}, u32[]{:S(2)}) collective-permute-start(bf16[2,144,1152]{2,1,0:T(8,128)(2,1)} %collective-permute-done.29.rest_5_.rest_8_), channel_id=1, source_target_pairs={{0,16},{16,0},{1,17},{17,1},{2,18},{18,2},{3,19},{19,3},{4,20},{20... | collective-permute-start | bytes 1990664 | tf_op jit(solution)/shard_map/ppermute | solution.py:930
  169.4 48.9 %collective-permute-start.39 = (bf16[4,8,16,1152]{3,2,1,0:T(8,128)(2,1)S(1)}, bf16[4,8,16,1152]{3,2,1,0:T(8,128)(2,1)S(1)}, u32[]{:S(2)}, u32[]{:S(2)}) collective-permute-start(bf16[4,8,16,1152]{3,2,1,0:T(8,128)(2,1)S(1)} %pad_maximum_fusion), channel_id=1, source_target_pairs={{0,2},{2,0},{4,6},{6,4},{8,10},{10,8},{12,14},{14,12},{1,3},{3,1},... | collective-permute-start | bytes 3538952 | tf_op jit(solution)/shard_map/ppermute | solution.py:930
  218.2 2.8 collective-permute-start.40
  219.3 55.8 %collective-permute-start.45 = (bf16[4,4,16,1152]{3,2,1,0:T(8,128)(2,1)S(1)}, bf16[4,4,16,1152]{3,2,1,0:T(8,128)(2,1)S(1)}, u32[]{:S(2)}, u32[]{:S(2)}) collective-permute-start(bf16[4,4,16,1152]{3,2,1,0:T(8,128)(2,1)S(1)} %pad_maximum_fusion.3), channel_id=1, source_target_pairs={{0,8},{2,10},{4,12},{6,14},{8,0},{10,2},{12,4},{14,6},{1,9},{3,11}... | collective-permute-start | bytes 1769480 | tf_op jit(solution)/shard_map/ppermute | solution.py:930
  219.6 65.8 %collective-permute-start.46 = (bf16[4,4,16,1152]{3,2,1,0:T(8,128)(2,1)S(1)}, bf16[4,4,16,1152]{3,2,1,0:T(8,128)(2,1)S(1)}, u32[]{:S(2)}, u32[]{:S(2)}) collective-permute-start(bf16[4,4,16,1152]{3,2,1,0:T(8,128)(2,1)S(1)} %pad_maximum_fusion.4), channel_id=1, source_target_pairs={{0,12},{2,14},{4,8},{6,10},{8,4},{10,6},{12,0},{14,2},{1,13},{3,15... | collective-permute-start | bytes 1769480 | tf_op jit(solution)/shard_map/ppermute | solution.py:930
  221.0 23.3 %collective-permute-start.41 = (bf16[4,4,16,1152]{3,2,1,0:T(8,128)(2,1)S(1)}, bf16[4,4,16,1152]{3,2,1,0:T(8,128)(2,1)S(1)}, u32[]{:S(2)}, u32[]{:S(2)}) collective-permute-start(bf16[4,4,16,1152]{3,2,1,0:T(8,128)(2,1)S(1)} %get-tuple-element.373), channel_id=1, source_target_pairs={{0,2},{2,0},{4,6},{6,4},{8,10},{10,8},{12,14},{14,12},{1,3},{3,1},... | collective-permute-start | bytes 1769480 | tf_op jit(solution)/shard_map/ppermute | solution.py:930
  222.0 22.3 %collective-permute-start.42 = (bf16[4,4,16,1152]{3,2,1,0:T(8,128)(2,1)S(1)}, bf16[4,4,16,1152]{3,2,1,0:T(8,128)(2,1)S(1)}, u32[]{:S(2)}, u32[]{:S(2)}) collective-permute-start(bf16[4,4,16,1152]{3,2,1,0:T(8,128)(2,1)S(1)} %get-tuple-element.374), channel_id=1, source_target_pairs={{0,16},{16,0},{1,17},{17,1},{2,18},{18,2},{3,19},{19,3},{4,20},{20... | collective-permute-start | bytes 1769480 | tf_op jit(solution)/shard_map/ppermute | solution.py:930
  222.6 27.1 %collective-permute-start.43 = (bf16[4,4,16,1152]{3,2,1,0:T(8,128)(2,1)S(1)}, bf16[4,4,16,1152]{3,2,1,0:T(8,128)(2,1)S(1)}, u32[]{:S(2)}, u32[]{:S(2)}) collective-permute-start(bf16[4,4,16,1152]{3,2,1,0:T(8,128)(2,1)S(1)} %get-tuple-element.375), channel_id=1, source_target_pairs={{0,18},{2,16},{4,22},{6,20},{8,26},{10,24},{12,30},{14,28},{16,2},... | collective-permute-start | bytes 1769480 | tf_op jit(solution)/shard_map/ppermute | solution.py:1004
  249.9 77.2 %collective-permute-start.48 = (bf16[4,4,16,1152]{3,2,1,0:T(8,128)(2,1)S(1)}, bf16[4,4,16,1152]{3,2,1,0:T(8,128)(2,1)S(1)}, u32[]{:S(2)}, u32[]{:S(2)}) collective-permute-start(bf16[4,4,16,1152]{3,2,1,0:T(8,128)(2,1)S(1)} %pad_maximum_fusion.6), channel_id=1, source_target_pairs={{0,4},{2,6},{4,0},{6,2},{8,12},{10,14},{12,8},{14,10},{1,5},{3,7},... | collective-permute-start | bytes 1769480 | tf_op jit(solution)/shard_map/ppermute | solution.py:930
  253.8 73.4 %collective-permute-start.49 = (bf16[4,4,16,1152]{3,2,1,0:T(8,128)(2,1)}, bf16[4,4,16,1152]{3,2,1,0:T(8,128)(2,1)S(1)}, u32[]{:S(2)}, u32[]{:S(2)}) collective-permute-start(bf16[4,4,16,1152]{3,2,1,0:T(8,128)(2,1)} %pad_maximum_fusion.7), channel_id=1, source_target_pairs={{0,8},{2,10},{4,12},{6,14},{8,0},{10,2},{12,4},{14,6},{1,9},{3,11}... | collective-permute-start | bytes 1769480 | tf_op jit(solution)/shard_map/ppermute | solution.py:930
  254.4 38.0 %collective-permute-start.44 = (bf16[4,4,16,1152]{3,2,1,0:T(8,128)(2,1)S(1)}, bf16[4,4,16,1152]{3,2,1,0:T(8,128)(2,1)S(1)}, u32[]{:S(2)}, u32[]{:S(2)}) collective-permute-start(bf16[4,4,16,1152]{3,2,1,0:T(8,128)(2,1)S(1)} %pad_maximum_fusion.2), channel_id=1, source_target_pairs={{0,4},{2,6},{4,0},{6,2},{8,12},{10,14},{12,8},{14,10},{1,5},{3,7},... | collective-permute-start | bytes 1769480 | tf_op jit(solution)/shard_map/ppermute | solution.py:930
  275.2 52.0 %collective-permute-start.50 = (bf16[4,4,16,1152]{3,2,1,0:T(8,128)(2,1)}, bf16[4,4,16,1152]{3,2,1,0:T(8,128)(2,1)S(1)}, u32[]{:S(2)}, u32[]{:S(2)}) collective-permute-start(bf16[4,4,16,1152]{3,2,1,0:T(8,128)(2,1)} %pad_maximum_fusion.8), channel_id=1, source_target_pairs={{0,12},{2,14},{4,8},{6,10},{8,4},{10,6},{12,0},{14,2},{1,13},{3,15... | collective-permute-start | bytes 1769480 | tf_op jit(solution)/shard_map/ppermute | solution.py:930
  292.4 34.7 %collective-permute-start.47 = (bf16[4,128,1152]{2,1,0:T(8,128)(2,1)S(1)}, bf16[4,128,1152]{2,1,0:T(8,128)(2,1)S(1)}, u32[]{:S(2)}, u32[]{:S(2)}) collective-permute-start(bf16[4,128,1152]{2,1,0:T(8,128)(2,1)S(1)} %get-tuple-element.387), channel_id=1, source_target_pairs={{0,2},{2,0},{4,6},{6,4},{8,10},{10,8},{12,14},{14,12},{1,3},{3,1},... | collective-permute-start | bytes 3538952 | tf_op jit(solution)/shard_map/ppermute | solution.py:930
  327.3 49.9 %collective-permute-start.51 = (bf16[2,128,1152]{2,1,0:T(8,128)(2,1)S(1)}, bf16[2,128,1152]{2,1,0:T(8,128)(2,1)S(1)}, u32[]{:S(2)}, u32[]{:S(2)}) collective-permute-start(bf16[2,128,1152]{2,1,0:T(8,128)(2,1)S(1)} %pad_maximum_fusion.10), channel_id=1, source_target_pairs={{0,4},{2,6},{4,0},{6,2},{8,12},{10,14},{12,8},{14,10},{1,5},{3,7},... | collective-permute-start | bytes 1769480 | tf_op jit(solution)/shard_map/ppermute | solution.py:930
  327.5 49.8 %collective-permute-start.52 = (bf16[2,128,1152]{2,1,0:T(8,128)(2,1)S(1)}, bf16[2,128,1152]{2,1,0:T(8,128)(2,1)S(1)}, u32[]{:S(2)}, u32[]{:S(2)}) collective-permute-start(bf16[2,128,1152]{2,1,0:T(8,128)(2,1)S(1)} %pad_maximum_fusion.11), channel_id=1, source_target_pairs={{0,8},{2,10},{4,12},{6,14},{8,0},{10,2},{12,4},{14,6},{1,9},{3,11}... | collective-permute-start | bytes 1769480 | tf_op jit(solution)/shard_map/ppermute | solution.py:930
  329.6 47.6 %collective-permute-start.53 = (bf16[2,128,1152]{2,1,0:T(8,128)(2,1)S(1)}, bf16[2,128,1152]{2,1,0:T(8,128)(2,1)S(1)}, u32[]{:S(2)}, u32[]{:S(2)}) collective-permute-start(bf16[2,128,1152]{2,1,0:T(8,128)(2,1)S(1)} %pad_maximum_fusion.12), channel_id=1, source_target_pairs={{0,12},{2,14},{4,8},{6,10},{8,4},{10,6},{12,0},{14,2},{1,13},{3,15... | collective-permute-start | bytes 1769480 | tf_op jit(solution)/shard_map/ppermute | solution.py:930
  377.2 6.4 %collective-permute-start.54 = (bf16[64,1152]{1,0:T(8,128)(2,1)S(1)}, bf16[64,1152]{1,0:T(8,128)(2,1)S(1)}, u32[]{:S(2)}, u32[]{:S(2)}) collective-permute-start(bf16[64,1152]{1,0:T(8,128)(2,1)S(1)} %get-tuple-element.425), channel_id=1, source_target_pairs={{0,2},{2,0},{4,6},{6,4},{8,10},{10,8},{12,14},{14,12},{1,3},{3,1},... | collective-permute-start | bytes 442376 | tf_op jit(solution)/shard_map/ppermute | solution.py:930
  377.8 9.4 %collective-permute-start.55 = (bf16[64,1152]{1,0:T(8,128)(2,1)S(1)}, bf16[64,1152]{1,0:T(8,128)(2,1)S(1)}, u32[]{:S(2)}, u32[]{:S(2)}) collective-permute-start(bf16[64,1152]{1,0:T(8,128)(2,1)S(1)} %get-tuple-element.426), channel_id=1, source_target_pairs={{0,4},{2,6},{4,0},{6,2},{8,12},{10,14},{12,8},{14,10},{1,5},{3,7},... | collective-permute-start | bytes 442376 | tf_op jit(solution)/shard_map/ppermute | solution.py:930
  378.7 53.0 %collective-permute-start.56 = (bf16[64,1152]{1,0:T(8,128)(2,1)S(1)}, bf16[64,1152]{1,0:T(8,128)(2,1)S(1)}, u32[]{:S(2)}, u32[]{:S(2)}) collective-permute-start(bf16[64,1152]{1,0:T(8,128)(2,1)S(1)} %get-tuple-element.427), channel_id=1, source_target_pairs={{0,6},{2,4},{4,2},{6,0},{8,14},{10,12},{12,10},{14,8},{1,7},{3,5},... | collective-permute-start | bytes 442376 | tf_op jit(solution)/shard_map/ppermute | solution.py:930
  380.8 51.0 %collective-permute-start.57 = (bf16[64,1152]{1,0:T(8,128)(2,1)S(1)}, bf16[64,1152]{1,0:T(8,128)(2,1)S(1)}, u32[]{:S(2)}, u32[]{:S(2)}) collective-permute-start(bf16[64,1152]{1,0:T(8,128)(2,1)S(1)} %get-tuple-element.428), channel_id=1, source_target_pairs={{0,8},{2,10},{4,12},{6,14},{8,0},{10,2},{12,4},{14,6},{1,9},{3,11}... | collective-permute-start | bytes 442376 | tf_op jit(solution)/shard_map/ppermute | solution.py:930
  381.7 50.0 %collective-permute-start.58 = (bf16[64,1152]{1,0:T(8,128)(2,1)S(1)}, bf16[64,1152]{1,0:T(8,128)(2,1)S(1)}, u32[]{:S(2)}, u32[]{:S(2)}) collective-permute-start(bf16[64,1152]{1,0:T(8,128)(2,1)S(1)} %get-tuple-element.429), channel_id=1, source_target_pairs={{0,10},{2,8},{4,14},{6,12},{8,2},{10,0},{12,6},{14,4},{1,11},{3,9}... | collective-permute-start | bytes 442376 | tf_op jit(solution)/shard_map/ppermute | solution.py:930
  383.7 48.1 %collective-permute-start.59 = (bf16[64,1152]{1,0:T(8,128)(2,1)S(1)}, bf16[64,1152]{1,0:T(8,128)(2,1)S(1)}, u32[]{:S(2)}, u32[]{:S(2)}) collective-permute-start(bf16[64,1152]{1,0:T(8,128)(2,1)S(1)} %get-tuple-element.430), channel_id=1, source_target_pairs={{0,12},{2,14},{4,8},{6,10},{8,4},{10,6},{12,0},{14,2},{1,13},{3,15... | collective-permute-start | bytes 442376 | tf_op jit(solution)/shard_map/ppermute | solution.py:930
  387.2 44.6 %collective-permute-start.60 = (bf16[64,1152]{1,0:T(8,128)(2,1)S(1)}, bf16[64,1152]{1,0:T(8,128)(2,1)S(1)}, u32[]{:S(2)}, u32[]{:S(2)}) collective-permute-start(bf16[64,1152]{1,0:T(8,128)(2,1)S(1)} %get-tuple-element.431), channel_id=1, source_target_pairs={{0,14},{2,12},{4,10},{6,8},{8,6},{10,4},{12,2},{14,0},{1,15},{3,13... | collective-permute-start | bytes 442376 | tf_op jit(solution)/shard_map/ppermute | solution.py:930
  431.8 8.1 %collective-permute-start.61 = (bf16[64,1152]{1,0:T(8,128)(2,1)S(1)}, bf16[64,1152]{1,0:T(8,128)(2,1)S(1)}, u32[]{:S(2)}, u32[]{:S(2)}) collective-permute-start(bf16[64,1152]{1,0:T(8,128)(2,1)S(1)} %get-tuple-element.441), channel_id=1, source_target_pairs={{0,2},{2,0},{4,6},{6,4},{8,10},{10,8},{12,14},{14,12},{1,3},{3,1},... | collective-permute-start | bytes 442376 | tf_op jit(solution)/shard_map/ppermute | solution.py:930
  432.7 7.9 %collective-permute-start.62 = (bf16[64,1152]{1,0:T(8,128)(2,1)S(1)}, bf16[64,1152]{1,0:T(8,128)(2,1)S(1)}, u32[]{:S(2)}, u32[]{:S(2)}) collective-permute-start(bf16[64,1152]{1,0:T(8,128)(2,1)S(1)} %get-tuple-element.442), channel_id=1, source_target_pairs={{0,4},{2,6},{4,0},{6,2},{8,12},{10,14},{12,8},{14,10},{1,5},{3,7},... | collective-permute-start | bytes 442376 | tf_op jit(solution)/shard_map/ppermute | solution.py:930
  436.1 8.6 %collective-permute-start.63 = (bf16[64,1152]{1,0:T(8,128)(2,1)S(1)}, bf16[64,1152]{1,0:T(8,128)(2,1)S(1)}, u32[]{:S(2)}, u32[]{:S(2)}) collective-permute-start(bf16[64,1152]{1,0:T(8,128)(2,1)S(1)} %get-tuple-element.443), channel_id=1, source_target_pairs={{0,6},{2,4},{4,2},{6,0},{8,14},{10,12},{12,10},{14,8},{1,7},{3,5},... | collective-permute-start | bytes 442376 | tf_op jit(solution)/shard_map/ppermute | solution.py:930
  436.7 9.9 %collective-permute-start.64 = (bf16[64,1152]{1,0:T(8,128)(2,1)S(1)}, bf16[64,1152]{1,0:T(8,128)(2,1)S(1)}, u32[]{:S(2)}, u32[]{:S(2)}) collective-permute-start(bf16[64,1152]{1,0:T(8,128)(2,1)S(1)} %get-tuple-element.444), channel_id=1, source_target_pairs={{0,8},{2,10},{4,12},{6,14},{8,0},{10,2},{12,4},{14,6},{1,9},{3,11}... | collective-permute-start | bytes 442376 | tf_op jit(solution)/shard_map/ppermute | solution.py:930
  439.2 10.6 %collective-permute-start.65 = (bf16[64,1152]{1,0:T(8,128)(2,1)S(1)}, bf16[64,1152]{1,0:T(8,128)(2,1)S(1)}, u32[]{:S(2)}, u32[]{:S(2)}) collective-permute-start(bf16[64,1152]{1,0:T(8,128)(2,1)S(1)} %get-tuple-element.445), channel_id=1, source_target_pairs={{0,10},{2,8},{4,14},{6,12},{8,2},{10,0},{12,6},{14,4},{1,11},{3,9}... | collective-permute-start | bytes 442376 | tf_op jit(solution)/shard_map/ppermute | solution.py:930
  439.9 12.8 %collective-permute-start.66 = (bf16[64,1152]{1,0:T(8,128)(2,1)S(1)}, bf16[64,1152]{1,0:T(8,128)(2,1)S(1)}, u32[]{:S(2)}, u32[]{:S(2)}) collective-permute-start(bf16[64,1152]{1,0:T(8,128)(2,1)S(1)} %get-tuple-element.446), channel_id=1, source_target_pairs={{0,12},{2,14},{4,8},{6,10},{8,4},{10,6},{12,0},{14,2},{1,13},{3,15... | collective-permute-start | bytes 442376 | tf_op jit(solution)/shard_map/ppermute | solution.py:930
  440.6 14.0 %collective-permute-start.67 = (bf16[64,1152]{1,0:T(8,128)(2,1)S(1)}, bf16[64,1152]{1,0:T(8,128)(2,1)S(1)}, u32[]{:S(2)}, u32[]{:S(2)}) collective-permute-start(bf16[64,1152]{1,0:T(8,128)(2,1)S(1)} %get-tuple-element.447), channel_id=1, source_target_pairs={{0,14},{2,12},{4,10},{6,8},{8,6},{10,4},{12,2},{14,0},{1,15},{3,13... | collective-permute-start | bytes 442376 | tf_op jit(solution)/shard_map/ppermute | solution.py:930
  (66 other events, 968.9 us)

commit v2 on v1

--- a/solution.py
+++ b/solution.py
@@ -12,10 +12,10 @@
 LANES = 128
 ROW_TILE = 16
 BLOCK = 8
-TANGENT_BLOCK = 4
-PAIR = 2
 EXPONENT_SCALE = HEAD_DIM ** (-0.5) * math.log2(math.e)
 VMEM_LIMIT = 40 * 1024 * 1024
+SPACE_VMEM_LIMIT = 26 * 1024 * 1024
+TANGENT_VMEM_LIMIT = 60 * 1024 * 1024
 
 epsilon = 1e-06
 
@@ -297,45 +297,24 @@
 
 def space_kernel(layout, pieces, targets, seat_ref, moment_ref, clean_ref, noise_ref, shift_ref, *rest):
     weight_pieces, sent_refs = rest[:pieces], rest[pieces : pieces + targets]
-    weights_ref, noisy_ref, query_ref, key_ref, value_ref, mixed_ref, sems = rest[pieces + targets :]
+    weights_ref, query_ref, key_ref, value_ref, mixed_ref, sems = rest[pieces + targets :]
     moment = moment_ref[0]
-    pair, positions, width = clean_ref.shape
+    positions, width = key_ref.shape
 
     @pl.when(pl.program_id(0) == 0)
     def _():
         wait_all(start_all(weight_copies(seat_ref, layout, weight_pieces, weights_ref, sems)))
 
     noisy = (
-        (1.0 - moment) * clean_ref[...].reshape(pair * positions, width).astype(jnp.float32)
-        + moment * noise_ref[...].reshape(pair * positions, width).astype(jnp.float32)
+        (1.0 - moment) * clean_ref[0].astype(jnp.float32)
+        + moment * noise_ref[0].astype(jnp.float32)
     ).astype(jnp.bfloat16)
-    noisy_ref[...] = noisy
     entry = noisy.astype(jnp.float32) + shift_ref[...]
     normed = (entry * inverse_rms(entry)).astype(jnp.bfloat16)
     query_ref[...] = dot_t(normed, weights_ref[0]).astype(jnp.bfloat16)
     key_ref[...] = dot_t(normed, weights_ref[1]).astype(jnp.bfloat16)
     value_ref[...] = dot_t(normed, weights_ref[2]).astype(jnp.bfloat16)
 
-    @pl.loop(0, pair)
-    def _(frame):
-        here = pl.ds(pl.multiple_of(frame * positions, positions), positions)
-        space_mix(query_ref.at[here], key_ref.at[here], value_ref.at[here], mixed_ref.at[here])
-
-    entry = noisy_ref[...].astype(jnp.float32) + shift_ref[...]
-    query_ref[...] = (entry + dot(mixed_ref[...], weights_ref[3])).astype(jnp.bfloat16)
-    lines = sent_refs[0].shape[0]
-    for index, ref in enumerate(sent_refs):
-        for line in range(lines):
-            seat = (seat_ref[0] ^ (index // 2)) * lines * 2 + (
-                seat_ref[1] ^ (line * 2 + index % 2)
-            )
-            for frame in range(pair):
-                start = pl.multiple_of(frame * positions + seat * ROW_TILE, ROW_TILE)
-                ref[line, frame] = query_ref[pl.ds(start, ROW_TILE), :]
-
-
-def space_mix(query_ref, key_ref, value_ref, mixed_ref):
-    positions, width = query_ref.shape
     weights = []
     for head in range(width // HEAD_DIM):
         low, high = head * HEAD_DIM, (head + 1) * HEAD_DIM
@@ -369,12 +348,22 @@
             )
             mixed_ref[:, pl.ds(left_edge, edge - left_edge)] = mixed.astype(jnp.bfloat16)
 
+    query_ref[...] = (entry + dot(mixed_ref[...], weights_ref[3])).astype(jnp.bfloat16)
+    lines = sent_refs[0].shape[0]
+    for index, ref in enumerate(sent_refs):
+        for line in range(lines):
+            seat = (seat_ref[0] ^ (index // 2)) * lines * 2 + (
+                seat_ref[1] ^ (line * 2 + index % 2)
+            )
+            start = pl.multiple_of(seat * ROW_TILE, ROW_TILE)
+            ref[line, 0] = query_ref[pl.ds(start, ROW_TILE), :]
+
 
 def spatial_layer(seat, moment, clean, noise, shift, weights, frames, seats):
     pieces, layout = weights
     positions, width = clean.shape[1:]
     frame_block = pl.BlockSpec(
-        (PAIR, positions, width), lambda f, seat: (seat[0] * (frames // PAIR) + f, 0, 0)
+        (1, positions, width), lambda f, seat: (seat[0] * frames + f, 0, 0)
     )
     lines = seats // 2
     piece = jax.ShapeDtypeStruct((lines, frames, ROW_TILE, width), jnp.bfloat16)
@@ -385,7 +374,7 @@
         out_shape=[piece] * 4,
         grid_spec=pltpu.PrefetchScalarGridSpec(
             num_scalar_prefetch=1,
-            grid=(frames // PAIR,),
+            grid=(frames,),
             in_specs=[
                 pl.BlockSpec(memory_space=pltpu.SMEM),
                 frame_block,
@@ -394,14 +383,14 @@
             ]
             + [pl.BlockSpec(memory_space=pl.ANY)] * len(pieces),
             out_specs=[
-                pl.BlockSpec((lines, PAIR, ROW_TILE, width), lambda f, seat: (0, f, 0, 0))
+                pl.BlockSpec((lines, 1, ROW_TILE, width), lambda f, seat: (0, f, 0, 0))
             ]
             * 4,
             scratch_shapes=[vmem(4, width, width)]
-            + [vmem(PAIR * positions, width)] * 5
+            + [vmem(positions, width)] * 4
             + [pltpu.SemaphoreType.DMA((len(layout),))],
         ),
-        compiler_params=pltpu.CompilerParams(vmem_limit_bytes=VMEM_LIMIT),
+        compiler_params=pltpu.CompilerParams(vmem_limit_bytes=SPACE_VMEM_LIMIT),
         cost_estimate=pl.CostEstimate(
             flops=14 * rows * width * width,
             bytes_accessed=8 * width * width + 6 * rows * width,
@@ -749,10 +738,10 @@
 ANYWHERE = pl.BlockSpec(memory_space=pl.ANY)
 
 
-def time_call(kernel, passes, rows, width, **settings):
+def time_call(kernel, passes, rows, width, limit=VMEM_LIMIT, **settings):
     return pl.pallas_call(
         kernel,
-        compiler_params=pltpu.CompilerParams(vmem_limit_bytes=VMEM_LIMIT),
+        compiler_params=pltpu.CompilerParams(vmem_limit_bytes=limit),
         cost_estimate=pl.CostEstimate(
             flops=int(12 * passes * rows * width * width),
             bytes_accessed=8 * width * width + 8 * rows * width,
@@ -861,7 +850,7 @@
     rows = frames * ROW_TILE // 2
     piece = jax.ShapeDtypeStruct((rows // seats, width), jnp.bfloat16)
     vmem = lambda *shape: pltpu.VMEM(shape, jnp.bfloat16)
-    chunk = TANGENT_BLOCK * frames
+    chunk = BLOCK * frames
     steps = rows // chunk
     part = 0 if first else steps
     half = pl.BlockSpec((chunk, width), lambda i: (part + i, 0))
@@ -873,6 +862,7 @@
         1,
         rows,
         width,
+        TANGENT_VMEM_LIMIT,
         grid=(steps,),
         out_shape=[piece] * seats + [other] * first,
         in_specs=[IN_SMEM] * 2
@@ -1140,12 +1130,20 @@
     rows, primal = student_rows(seat, cond_shift, down, up, time_weights, noisy_in, frames)
     rows, primal, low, across, both, lines = together(rows, primal, low, across, both, lines)
     near_line = flip(lines[1], "seq", 2)
-    uncond = along_line([kept, low, across, both])
+    uncond = [
+        jnp.stack([given[line] for given in (kept, low, across, both)])
+        for line in range(seats // 2)
+    ]
+    uncond_last = flip(uncond[-1], "seq", seats - 2)
     student_kept, student_low = student_mix(
         seat, cond_shift, rows, primal, time_weights, frames, seats
     )
     cond = [lines[0], near_line, *far_lines]
-    student_kept, student_low, cond = together(student_kept, student_low, cond)
+    student_kept, student_low, cond, uncond = together(student_kept, student_low, cond, uncond)
+    uncond = [
+        flip(line, "seq", 2 * index) if index > 0 else line
+        for index, line in enumerate(uncond[:-1])
+    ] + [uncond_last]
     velocity = teacher_velocity(seat, time_weights, cond, frames)
     student_low, velocity, uncond = together(flip(student_low, "seq", 1), velocity, uncond)
     student_back = along_line([student_kept, student_low])
@@ -1170,7 +1168,6 @@
         and mesh.shape["clip"] == 2
         and seats == 4 * sides
         and frames % (groups * ROW_TILE // 4) == 0
-        and frames // groups % PAIR == 0
         and positions == groups * ROW_TILE
         and 2 * frames == LANES
         and width % LANES == 0

time: 461 us -> 464 us (level); the launches traced: 457 us -> 454 us
  Pallas kernels: 225 us -> 210 us
  waiting for transfers between devices: 121 us -> 129 us
    pallas_call x2, Pallas kernels: 60.4 us -> 51.9 us  [spatial_layer(): pl.pallas_call(functools.partial(space_kernel, layout, len(pieces), 4), o...]
    pallas_call x2, Pallas kernels: 87.2 us -> 79.8 us  [student_tangent(): time_call(functools.partial(tangent_kernel, layout, (len(weights), len(pi...]
    ppermute x62, waiting for transfers between devices: 103 us -> 110 us  [flip(): return lax.ppermute(value, axis, pairs)]
    unnamed x118 -> x156, local copies, waits for them, and re-layouts: 23.4 us -> 26.1 us
  transfers between devices with their start and end apart: 68 -> 68, of which waited for: 26 -> 28; matrix products, arithmetic and copies ran while one was open for 3% -> 2% of each run, Pallas kernels for 49% -> 46%
where the time goes in v2:
time: 464 us; the launch traced here: 454 us
  Pallas kernels  210 us (45%)
  waiting for transfers between devices  129 us (28%)
  starting transfers between devices  74.2 us (16%)
  local copies, waits for them, and re-layouts  31.1 us (7%)
  other arithmetic  7.26 us (2%)
    ppermute x62, waiting for transfers between devices, flip(): return lax.ppermute(value, axis, pairs)  110 us
    pallas_call x2, Pallas kernels, student_tangent(): time_call(functools.partial(tangent_kernel, layout, (len(weights), len(pi...  79.8 us
    ppermute x62, starting transfers between devices, flip(): return lax.ppermute(value, axis, pairs)  60.2 us
    pallas_call x2, Pallas kernels, spatial_layer(): pl.pallas_call(functools.partial(space_kernel, layout, len(pieces), 4), o...  51.9 us
    pallas_call x1, Pallas kernels, teacher_velocity(): time_call(functools.partial(teacher_kernel, layout, (len(weights), len(pi...  33.1 us
    unnamed x156, local copies, waits for them, and re-layouts  26.1 us
    pallas_call x1, Pallas kernels, student_rows(): time_call(functools.partial(student_rows_kernel, layout, (len(weights), l...  19.8 us
    pallas_call x1, Pallas kernels, student_mix(): time_call(functools.partial(student_mix_kernel, layout, frames), 0.6, row...  18.3 us
  transfers between devices with their start and end apart: 68, of which 28 were waited for; matrix products, arithmetic and copies ran while one was open for 2% of the time, Pallas kernels for 46%

profile of v2, /device:TPU:8, one launch (start us, length us, event | category | flops | bytes accessed | tf_op | source)
XLA Modules:
  0.0 454.5 jit_solution(16748453555981475719)
XLA Ops:
  3.0 8.4 %collective-permute-done = bf16[2,72,1152]{2,1,0:T(8,128)(2,1)S(1)} collective-permute-done((bf16[2,72,1152]{2,1,0:T(8,128)(2,1)S(1)}, bf16[2,72,1152]{2,1,0:T(8,128)(2,1)S(1)}, u32[]{:S(2)}, u32[]{:S(2)}) %collective-permute-start) | collective-permute-done | bytes 331808 | tf_op jit(solution)/shard_map/ppermute | solution.py:920
  11.6 3.5 collective-permute-start.4
  15.2 1.6 collective-permute-start.2
  16.7 1.5 collective-permute-start.1
  18.2 9.6 %collective-permute-done.5 = bf16[2,72,1152]{2,1,0:T(8,128)(2,1)S(1)} collective-permute-done((bf16[2,72,1152]{2,1,0:T(8,128)(2,1)S(1)}, bf16[2,72,1152]{2,1,0:T(8,128)(2,1)S(1)}, u32[]{:S(2)}, u32[]{:S(2)}) %collective-permute-start.5) | collective-permute-done | bytes 331808 | tf_op jit(solution)/shard_map/ppermute | solution.py:920
  28.0 1.3 collective-permute-done.4
  30.2 2.4 collective-permute-done.2.rest_2_
  34.5 2.1 collective-permute-start.7
  37.2 3.6 collective-permute-start.10
  40.9 1.6 collective-permute-start.6
  46.1 2.3 copy-done
  48.4 2.3 copy-done.2
  50.8 2.6 shard_map.140
  53.4 1.4 broadcast_select_fusion.1.rest_4_
  54.9 2.9 collective-permute-done.6.rest_3_
  57.8 1.3 collective-permute-start.16
  59.2 1.6 collective-permute-start.13
  60.7 1.5 collective-permute-start.12
  62.3 12.3 %collective-permute-done.16 = bf16[2,144,1152]{2,1,0:T(8,128)(2,1)S(1)} collective-permute-done((bf16[2,144,1152]{2,1,0:T(8,128)(2,1)}, bf16[2,144,1152]{2,1,0:T(8,128)(2,1)S(1)}, u32[]{:S(2)}, u32[]{:S(2)}) %collective-permute-start.16) | collective-permute-done | bytes 663584 | tf_op jit(solution)/shard_map/ppermute | solution.py:954
  77.8 2.1 collective-permute-done.18.rest_12_
  80.1 2.0 collective-permute-done.19.rest_13_
  82.7 1.5 collective-permute-start.21
  84.7 15.4 %collective-permute-done.23.rest_17_ = bf16[2,8,16,1152]{3,2,1,0:T(8,128)(2,1)S(1)} collective-permute-done((bf16[2,8,16,1152]{3,2,1,0:T(8,128)(2,1)S(1)}, bf16[2,8,16,1152]{3,2,1,0:T(8,128)(2,1)S(1)}, u32[]{:S(2)}, u32[]{:S(2)}) %collective-permute-start.23) | collective-permute-done | bytes 589856 | tf_op jit(solution)/shard_map/ppermute | solution.py:920
  100.8 1.5 collective-permute-done.24.rest_15_
  104.2 1.3 collective-permute-start.29
  107.9 1.4 collective-permute-start.27
  109.3 2.3 copy-done.3
  111.7 25.8 %shard_map.141 = (bf16[4,4,16,1152]{3,2,1,0:T(8,128)(2,1)S(1)}, bf16[4,4,16,1152]{3,2,1,0:T(8,128)(2,1)S(1)}, bf16[4,4,16,1152]{3,2,1,0:T(8,128)(2,1)S(1)}, bf16[4,4,16,1152]{3,2,1,0:T(8,128)(2,1)S(1)}) custom-call(s32[3]{0:T(128)S(1)} %pad_add_fusion.seat_ref, f32[1]{0:T(128)} %copy.20.moment_ref, bf16[8,256,1152]{2,1,0:T(8,128)(2,1)S(1)} %bitcast.15, ...), custom_call_target="tpu_custom_call" | custom-call | flops 19025362944 | bytes 17694720 | tf_op jit(solution)/shard_map/pallas_call | solution.py:372
  140.9 4.8 %collective-permute-done.30.rest_18_ = bf16[2,8,16,1152]{3,2,1,0:T(8,128)(2,1)S(1)} collective-permute-done((bf16[2,8,16,1152]{3,2,1,0:T(8,128)(2,1)S(1)}, bf16[2,8,16,1152]{3,2,1,0:T(8,128)(2,1)S(1)}, u32[]{:S(2)}, u32[]{:S(2)}) %collective-permute-start.30) | collective-permute-done | bytes 589856 | tf_op jit(solution)/shard_map/ppermute | solution.py:920
  145.7 12.9 %collective-permute-done.31.rest_19_ = bf16[2,8,16,1152]{3,2,1,0:T(8,128)(2,1)S(1)} collective-permute-done((bf16[2,8,16,1152]{3,2,1,0:T(8,128)(2,1)S(1)}, bf16[2,8,16,1152]{3,2,1,0:T(8,128)(2,1)S(1)}, u32[]{:S(2)}, u32[]{:S(2)}) %collective-permute-start.31) | collective-permute-done | bytes 589856 | tf_op jit(solution)/shard_map/ppermute | solution.py:920
  163.1 1.5 collective-permute-start.35
  165.1 1.4 collective-permute-start.37
  166.5 1.4 collective-permute-start.38
  168.7 2.3 copy-done.1
  171.0 2.3 copy-done.4
  179.9 26.0 %shard_map.142 = (bf16[4,4,16,1152]{3,2,1,0:T(8,128)(2,1)S(1)}, bf16[4,4,16,1152]{3,2,1,0:T(8,128)(2,1)S(1)}, bf16[4,4,16,1152]{3,2,1,0:T(8,128)(2,1)S(1)}, bf16[4,4,16,1152]{3,2,1,0:T(8,128)(2,1)S(1)}) custom-call(s32[3]{0:T(128)S(1)} %pad_add_fusion.seat_ref, f32[1]{0:T(128)} %copy.20.moment_ref, bf16[8,256,1152]{2,1,0:T(8,128)(2,1)S(1)} %copy-done.1, ...), custom_call_target="tpu_custom_call" | custom-call | flops 19025362944 | bytes 17694720 | tf_op jit(solution)/shard_map/pallas_call | solution.py:372
  206.8 9.8 %collective-permute-done.39.rest_20_ = bf16[4,8,16,1152]{3,2,1,0:T(8,128)(2,1)S(1)} collective-permute-done((bf16[4,8,16,1152]{3,2,1,0:T(8,128)(2,1)S(1)}, bf16[4,8,16,1152]{3,2,1,0:T(8,128)(2,1)S(1)}, u32[]{:S(2)}, u32[]{:S(2)}) %collective-permute-start.39) | collective-permute-done | bytes 1179680 | tf_op jit(solution)/shard_map/ppermute | solution.py:920
  220.9 1.9 collective-permute-start.43
  222.9 19.8 %shard_map.143 = (bf16[1024,1152]{1,0:T(8,128)(2,1)}, bf16[3,1024,1152]{2,1,0:T(8,128)(2,1)}) custom-call(s32[3]{0:T(128)S(1)} %pad_add_fusion.seat_ref, f32[1,1152]{1,0:T(1,128)S(1)} %broadcast_in_dim.12.shift_ref, bf16[128,1152]{1,0:T(8,128)(2,1)S(1)} %bitcast.18, bf16[128,1152]{1,0:T(8,128)(2,1)S(1)} %copy.17.up_ref, ...), custom_call_target="tpu_custom_call" | custom-call | flops 9784472576 | bytes 20054016 | tf_op jit(solution)/shard_map/pallas_call | solution.py:760
  242.8 5.1 %collective-permute-done.43 = bf16[4,4,16,1152]{3,2,1,0:T(8,128)(2,1)S(1)} collective-permute-done((bf16[4,4,16,1152]{3,2,1,0:T(8,128)(2,1)S(1)}, bf16[4,4,16,1152]{3,2,1,0:T(8,128)(2,1)S(1)}, u32[]{:S(2)}, u32[]{:S(2)}) %collective-permute-start.43) | collective-permute-done | bytes 589856 | tf_op jit(solution)/shard_map/ppermute | solution.py:994
  249.3 3.9 collective-permute-start.44
  254.3 18.3 %shard_map.144 = (bf16[4,128,1152]{2,1,0:T(8,128)(2,1)S(1)}, bf16[4,128,1152]{2,1,0:T(8,128)(2,1)S(1)}) custom-call(s32[3]{0:T(128)S(1)} %pad_add_fusion.seat_ref, f32[1,1152]{1,0:T(1,128)S(1)} %broadcast_in_dim.12.shift_ref, bf16[1024,1152]{1,0:T(8,128)(2,1)} %get-tuple-element.383.rows_ref.rest_1_, ...), custom_call_target="tpu_custom_call" | custom-call | flops 9784472576 | bytes 20054016 | tf_op jit(solution)/shard_map/pallas_call | solution.py:792
  272.6 11.0 %collective-permute-done.46.rest_19_ = bf16[4,4,16,1152]{3,2,1,0:T(8,128)(2,1)S(1)} collective-permute-done((bf16[4,4,16,1152]{3,2,1,0:T(8,128)(2,1)S(1)}, bf16[4,4,16,1152]{3,2,1,0:T(8,128)(2,1)S(1)}, u32[]{:S(2)}, u32[]{:S(2)}) %collective-permute-start.46) | collective-permute-done | bytes 589856 | tf_op jit(solution)/shard_map/ppermute | solution.py:920
  284.1 1.9 collective-permute-start.49
  286.0 1.5 collective-permute-start.47
  287.5 33.1 %shard_map.145.rest_0_ = bf16[1024,1152]{1,0:T(8,128)(2,1)} custom-call(s32[3]{0:T(128)S(1)} %pad_add_fusion.seat_ref, bf16[2,144,1152]{2,1,0:T(8,128)(2,1)S(1)} %maximum_select_fusion.1.rest_0_.rest_3_, bf16[2,144,1152]{2,1,0:T(8,128)(2,1)S(1)} %copy-done.29, bf16[2,144,1152]{2,1,0:T(8,128)(2,1)S(1)} %copy-done.25, ...), custom_call_target="tpu_custom_call" | custom-call | flops 16307453952 | bytes 20054016 | tf_op jit(solution)/shard_map/pallas_call | solution.py:822
  324.2 1.5 collective-permute-start.53
  325.8 41.0 %shard_map.146 = (bf16[64,1152]{1,0:T(8,128)(2,1)}, bf16[64,1152]{1,0:T(8,128)(2,1)}, bf16[64,1152]{1,0:T(8,128)(2,1)}, bf16[64,1152]{1,0:T(8,128)(2,1)}, bf16[6...) custom-call(s32[3]{0:T(128)} %copy-done.20, ...), custom_call_target="tpu_custom_call" | custom-call | flops 8153726976 | bytes 15335424 | tf_op jit(solution)/shard_map/pallas_call | solution.py:860
  366.9 8.0 %collective-permute-done.53.rest_3_ = bf16[2,128,1152]{2,1,0:T(8,128)(2,1)S(1)} collective-permute-done((bf16[2,128,1152]{2,1,0:T(8,128)(2,1)S(1)}, bf16[2,128,1152]{2,1,0:T(8,128)(2,1)S(1)}, u32[]{:S(2)}, u32[]{:S(2)}) %collective-permute-start.53) | collective-permute-done | bytes 589856 | tf_op jit(solution)/shard_map/ppermute | solution.py:920
  375.9 2.5 collective-permute-start.56
  378.8 2.9 collective-permute-start.58
  381.7 1.4 collective-permute-start.59
  384.3 38.8 %shard_map.148 = (bf16[64,1152]{1,0:T(8,128)(2,1)}, bf16[64,1152]{1,0:T(8,128)(2,1)}, bf16[64,1152]{1,0:T(8,128)(2,1)}, bf16[64,1152]{1,0:T(8,128)(2,1)}, bf16[6...) custom-call(s32[3]{0:T(128)} %copy-done.20, ...), custom_call_target="tpu_custom_call" | custom-call | flops 8153726976 | bytes 15335424 | tf_op jit(solution)/shard_map/pallas_call | solution.py:860
  423.1 1.6 collective-permute-start.61
  424.7 2.9 collective-permute-start.62
  428.0 1.7 collective-permute-start.64
  429.7 1.7 collective-permute-start.65
  432.6 4.6 %collective-permute-start.67 = (bf16[64,1152]{1,0:T(8,128)(2,1)}, bf16[64,1152]{1,0:T(8,128)(2,1)S(1)}, u32[]{:S(2)}, u32[]{:S(2)}) collective-permute-start(bf16[64,1152]{1,0:T(8,128)(2,1)} %get-tuple-element.453), channel_id=1, source_target_pairs={{0,14},{2,12},{4,10},{6,8},{8,6},{10,4},{12,2},{14,0},{1,15},{3,13... | collective-permute-start | bytes 442376 | tf_op jit(solution)/shard_map/ppermute | solution.py:920
  437.2 2.1 shard_map.147
  439.4 1.8 collective-permute-done.64.rest_12_
  441.1 4.7 %collective-permute-done.65.rest_13_ = bf16[64,1152]{1,0:T(8,128)(2,1)S(1)} collective-permute-done((bf16[64,1152]{1,0:T(8,128)(2,1)}, bf16[64,1152]{1,0:T(8,128)(2,1)S(1)}, u32[]{:S(2)}, u32[]{:S(2)}) %collective-permute-start.65) | collective-permute-done | bytes 147488 | tf_op jit(solution)/shard_map/ppermute | solution.py:920
  445.9 3.6 collective-permute-done.66.rest_14_
  449.5 2.4 collective-permute-done.67.rest_15_
  451.9 2.1 shard_map.149
  (280 shorter events, 49.1 us)
Async XLA Ops:
  1.8 9.6 %collective-permute-start = (bf16[2,72,1152]{2,1,0:T(8,128)(2,1)S(1)}, bf16[2,72,1152]{2,1,0:T(8,128)(2,1)S(1)}, u32[]{:S(2)}, u32[]{:S(2)}) collective-permute-start(bf16[2,72,1152]{2,1,0:T(8,128)(2,1)S(1)} %fusion.1), channel_id=1, source_target_pairs={{0,4},{2,6},{4,0},{6,2},{8,12},{10,14},{12,8},{14,10},{1,5},{3,7},... | collective-permute-start | bytes 995336 | tf_op jit(solution)/shard_map/ppermute | solution.py:920
  11.6 17.7 %collective-permute-start.4 = (bf16[2,144,1152]{2,1,0:T(8,128)(2,1)S(1)}, bf16[2,144,1152]{2,1,0:T(8,128)(2,1)}, u32[]{:S(2)}, u32[]{:S(2)}) collective-permute-start(bf16[2,144,1152]{2,1,0:T(8,128)(2,1)S(1)} %maximum_select_fusion.rest_0_), channel_id=1, source_target_pairs={{4,8},{8,4},{6,10},{10,6},{5,9},{9,5},{7,11},{11,7},{20,24},{24,20... | collective-permute-start | bytes 1990664 | tf_op jit(solution)/shard_map/ppermute | solution.py:944
  15.1 14.3 %collective-permute-start.3 = (bf16[2,144,1152]{2,1,0:T(8,128)(2,1)S(1)}, bf16[2,144,1152]{2,1,0:T(8,128)(2,1)S(1)}, u32[]{:S(2)}, u32[]{:S(2)}) collective-permute-start(bf16[2,144,1152]{2,1,0:T(8,128)(2,1)S(1)} %maximum_select_fusion.rest_0_), channel_id=1, source_target_pairs={{0,1},{1,0},{2,3},{3,2},{4,5},{5,4},{6,7},{7,6},{8,9},{9,8},{10,11... | collective-permute-start | bytes 1990664 | tf_op jit(solution)/shard_map/ppermute | solution.py:920
  15.2 17.4 %collective-permute-start.2 = (bf16[2,144,1152]{2,1,0:T(8,128)(2,1)S(1)}, bf16[2,144,1152]{2,1,0:T(8,128)(2,1)}, u32[]{:S(2)}, u32[]{:S(2)}) collective-permute-start(bf16[2,144,1152]{2,1,0:T(8,128)(2,1)S(1)} %maximum_select_fusion.rest_0_), channel_id=1, source_target_pairs={{0,16},{16,0},{1,17},{17,1},{2,18},{18,2},{3,19},{19,3},{4,20},{20... | collective-permute-start | bytes 1990664 | tf_op jit(solution)/shard_map/ppermute | solution.py:920
  16.7 17.0 %collective-permute-start.1 = (bf16[2,144,1152]{2,1,0:T(8,128)(2,1)S(1)}, bf16[2,144,1152]{2,1,0:T(8,128)(2,1)S(1)}, u32[]{:S(2)}, u32[]{:S(2)}) collective-permute-start(bf16[2,144,1152]{2,1,0:T(8,128)(2,1)S(1)} %maximum_select_fusion.rest_0_), channel_id=1, source_target_pairs={{0,2},{2,0},{4,6},{6,4},{8,10},{10,8},{12,14},{14,12},{1,3},{3,1},... | collective-permute-start | bytes 1990664 | tf_op jit(solution)/shard_map/ppermute | solution.py:920
  18.2 9.6 %collective-permute-start.5 = (bf16[2,72,1152]{2,1,0:T(8,128)(2,1)S(1)}, bf16[2,72,1152]{2,1,0:T(8,128)(2,1)S(1)}, u32[]{:S(2)}, u32[]{:S(2)}) collective-permute-start(bf16[2,72,1152]{2,1,0:T(8,128)(2,1)S(1)} %fusion), channel_id=1, source_target_pairs={{0,4},{2,6},{4,0},{6,2},{8,12},{10,14},{12,8},{14,10},{1,5},{3,7},... | collective-permute-start | bytes 995336 | tf_op jit(solution)/shard_map/ppermute | solution.py:920
  33.7 8.8 %collective-permute-start.8 = (bf16[2,144,1152]{2,1,0:T(8,128)(2,1)S(1)}, bf16[2,144,1152]{2,1,0:T(8,128)(2,1)S(1)}, u32[]{:S(2)}, u32[]{:S(2)}) collective-permute-start(bf16[2,144,1152]{2,1,0:T(8,128)(2,1)S(1)} %collective-permute-done.1.rest_1_), channel_id=1, source_target_pairs={{0,1},{1,0},{2,3},{3,2},{4,5},{5,4},{6,7},{7,6},{8,9},{9,8},{10,11... | collective-permute-start | bytes 1990664 | tf_op jit(solution)/shard_map/ppermute | solution.py:920
  34.5 18.9 %collective-permute-start.7 = (bf16[2,144,1152]{2,1,0:T(8,128)(2,1)}, bf16[2,144,1152]{2,1,0:T(8,128)(2,1)}, u32[]{:S(2)}, u32[]{:S(2)}) collective-permute-start(bf16[2,144,1152]{2,1,0:T(8,128)(2,1)} %collective-permute-done.4), channel_id=1, source_target_pairs={{4,0},{8,12},{6,2},{10,14},{5,1},{9,13},{7,3},{11,15},{20,16},{24,... | collective-permute-start | bytes 1990664 | tf_op jit(solution)/shard_map/ppermute | solution.py:954
  36.7 21.0 %collective-permute-start.11 = (bf16[2,144,1152]{2,1,0:T(8,128)(2,1)S(1)}, bf16[2,144,1152]{2,1,0:T(8,128)(2,1)S(1)}, u32[]{:S(2)}, u32[]{:S(2)}) collective-permute-start(bf16[2,144,1152]{2,1,0:T(8,128)(2,1)S(1)} %maximum_select_fusion.1.rest_0_.rest_3_), channel_id=1, source_target_pairs={{0,16},{16,0},{1,17},{17,1},{2,18},{18,2},{3,19},{19,3},{4,20},{20... | collective-permute-start | bytes 1990664 | tf_op jit(solution)/shard_map/ppermute | solution.py:920
  37.2 20.5 %collective-permute-start.10 = (bf16[2,144,1152]{2,1,0:T(8,128)(2,1)S(1)}, bf16[2,144,1152]{2,1,0:T(8,128)(2,1)}, u32[]{:S(2)}, u32[]{:S(2)}) collective-permute-start(bf16[2,144,1152]{2,1,0:T(8,128)(2,1)S(1)} %maximum_select_fusion.1.rest_0_.rest_3_), channel_id=1, source_target_pairs={{4,8},{8,4},{6,10},{10,6},{5,9},{9,5},{7,11},{11,7},{20,24},{24,20... | collective-permute-start | bytes 1990664 | tf_op jit(solution)/shard_map/ppermute | solution.py:944
  40.9 16.9 %collective-permute-start.6 = (bf16[2,144,1152]{2,1,0:T(8,128)(2,1)}, bf16[2,144,1152]{2,1,0:T(8,128)(2,1)}, u32[]{:S(2)}, u32[]{:S(2)}) collective-permute-start(bf16[2,144,1152]{2,1,0:T(8,128)(2,1)} %collective-permute-done.2.rest_2_), channel_id=1, source_target_pairs={{0,2},{2,0},{4,6},{6,4},{8,10},{10,8},{12,14},{14,12},{1,3},{3,1},... | collective-permute-start | bytes 1990664 | tf_op jit(solution)/shard_map/ppermute | solution.py:920
  43.3 14.4 %collective-permute-start.9 = (bf16[2,144,1152]{2,1,0:T(8,128)(2,1)}, bf16[2,144,1152]{2,1,0:T(8,128)(2,1)}, u32[]{:S(2)}, u32[]{:S(2)}) collective-permute-start(bf16[2,144,1152]{2,1,0:T(8,128)(2,1)} %collective-permute-done.2.rest_2_), channel_id=1, source_target_pairs={{0,1},{1,0},{2,3},{3,2},{4,5},{5,4},{6,7},{7,6},{8,9},{9,8},{10,11... | collective-permute-start | bytes 1990664 | tf_op jit(solution)/shard_map/ppermute | solution.py:920
  57.7 4.5 collective-permute-start.14
  57.8 16.7 %collective-permute-start.16 = (bf16[2,144,1152]{2,1,0:T(8,128)(2,1)}, bf16[2,144,1152]{2,1,0:T(8,128)(2,1)S(1)}, u32[]{:S(2)}, u32[]{:S(2)}) collective-permute-start(bf16[2,144,1152]{2,1,0:T(8,128)(2,1)} %collective-permute-done.10), channel_id=1, source_target_pairs={{4,0},{8,12},{6,2},{10,14},{5,1},{9,13},{7,3},{11,15},{20,16},{24,... | collective-permute-start | bytes 1990664 | tf_op jit(solution)/shard_map/ppermute | solution.py:954
  59.2 17.4 %collective-permute-start.13 = (bf16[2,144,1152]{2,1,0:T(8,128)(2,1)S(1)}, bf16[2,144,1152]{2,1,0:T(8,128)(2,1)S(1)}, u32[]{:S(2)}, u32[]{:S(2)}) collective-permute-start(bf16[2,144,1152]{2,1,0:T(8,128)(2,1)S(1)} %broadcast_select_fusion.1.rest_4_), channel_id=1, source_target_pairs={{0,16},{16,0},{1,17},{17,1},{2,18},{18,2},{3,19},{19,3},{4,20},{20... | collective-permute-start | bytes 1990664 | tf_op jit(solution)/shard_map/ppermute | solution.py:920
  60.7 17.0 %collective-permute-start.12 = (bf16[2,144,1152]{2,1,0:T(8,128)(2,1)S(1)}, bf16[2,144,1152]{2,1,0:T(8,128)(2,1)S(1)}, u32[]{:S(2)}, u32[]{:S(2)}) collective-permute-start(bf16[2,144,1152]{2,1,0:T(8,128)(2,1)S(1)} %broadcast_select_fusion.1.rest_4_), channel_id=1, source_target_pairs={{0,2},{2,0},{4,6},{6,4},{8,10},{10,8},{12,14},{14,12},{1,3},{3,1},... | collective-permute-start | bytes 1990664 | tf_op jit(solution)/shard_map/ppermute | solution.py:920
  62.2 15.5 %collective-permute-start.15 = (bf16[2,144,1152]{2,1,0:T(8,128)(2,1)S(1)}, bf16[2,144,1152]{2,1,0:T(8,128)(2,1)S(1)}, u32[]{:S(2)}, u32[]{:S(2)}) collective-permute-start(bf16[2,144,1152]{2,1,0:T(8,128)(2,1)S(1)} %maximum_select_fusion.1.rest_0_.rest_3_), channel_id=1, source_target_pairs={{0,1},{1,0},{2,3},{3,2},{4,5},{5,4},{6,7},{7,6},{8,9},{9,8},{10,11... | collective-permute-start | bytes 1990664 | tf_op jit(solution)/shard_map/ppermute | solution.py:920
  82.2 17.9 %collective-permute-start.17 = (bf16[2,144,1152]{2,1,0:T(8,128)(2,1)S(1)}, bf16[2,144,1152]{2,1,0:T(8,128)(2,1)S(1)}, u32[]{:S(2)}, u32[]{:S(2)}) collective-permute-start(bf16[2,144,1152]{2,1,0:T(8,128)(2,1)S(1)} %collective-permute-done.12.rest_5_), channel_id=1, source_target_pairs={{0,16},{16,0},{1,17},{17,1},{2,18},{18,2},{3,19},{19,3},{4,20},{20... | collective-permute-start | bytes 1990664 | tf_op jit(solution)/shard_map/ppermute | solution.py:920
  82.7 17.4 %collective-permute-start.21 = (bf16[2,144,1152]{2,1,0:T(8,128)(2,1)S(1)}, bf16[2,144,1152]{2,1,0:T(8,128)(2,1)S(1)}, u32[]{:S(2)}, u32[]{:S(2)}) collective-permute-start(bf16[2,144,1152]{2,1,0:T(8,128)(2,1)S(1)} %maximum_select_fusion.1.rest_0_.rest_3_), channel_id=1, source_target_pairs={{0,2},{2,0},{4,6},{6,4},{8,10},{10,8},{12,14},{14,12},{1,3},{3,1},... | collective-permute-start | bytes 1990664 | tf_op jit(solution)/shard_map/ppermute | solution.py:920
  84.2 15.8 %collective-permute-start.22 = (bf16[2,144,1152]{2,1,0:T(8,128)(2,1)S(1)}, bf16[2,144,1152]{2,1,0:T(8,128)(2,1)S(1)}, u32[]{:S(2)}, u32[]{:S(2)}) collective-permute-start(bf16[2,144,1152]{2,1,0:T(8,128)(2,1)S(1)} %copy-done.24), channel_id=1, source_target_pairs={{0,1},{1,0},{2,3},{3,2},{4,5},{5,4},{6,7},{7,6},{8,9},{9,8},{10,11... | collective-permute-start | bytes 1990664 | tf_op jit(solution)/shard_map/ppermute | solution.py:920
  84.3 15.7 %collective-permute-start.23 = (bf16[2,8,16,1152]{3,2,1,0:T(8,128)(2,1)S(1)}, bf16[2,8,16,1152]{3,2,1,0:T(8,128)(2,1)S(1)}, u32[]{:S(2)}, u32[]{:S(2)}) collective-permute-start(bf16[2,8,16,1152]{3,2,1,0:T(8,128)(2,1)S(1)} %get-tuple-element.283), channel_id=1, source_target_pairs={{0,4},{2,6},{4,0},{6,2},{8,12},{10,14},{12,8},{14,10},{1,5},{3,7},... | collective-permute-start | bytes 1769480 | tf_op jit(solution)/shard_map/ppermute | solution.py:920
  100.2 3.0 collective-permute-start.26
  100.7 3.5 collective-permute-start.25
  104.2 54.4 %collective-permute-start.29 = (bf16[2,144,1152]{2,1,0:T(8,128)(2,1)S(1)}, bf16[2,144,1152]{2,1,0:T(8,128)(2,1)}, u32[]{:S(2)}, u32[]{:S(2)}) collective-permute-start(bf16[2,144,1152]{2,1,0:T(8,128)(2,1)S(1)} %broadcast_select_fusion.rest_4_.rest_7_), channel_id=1, source_target_pairs={{0,2},{2,0},{4,6},{6,4},{8,10},{10,8},{12,14},{14,12},{1,3},{3,1},... | collective-permute-start | bytes 1990664 | tf_op jit(solution)/shard_map/ppermute | solution.py:920
  105.5 53.1 %collective-permute-start.28 = (bf16[2,144,1152]{2,1,0:T(8,128)(2,1)S(1)}, bf16[2,144,1152]{2,1,0:T(8,128)(2,1)}, u32[]{:S(2)}, u32[]{:S(2)}) collective-permute-start(bf16[2,144,1152]{2,1,0:T(8,128)(2,1)S(1)} %broadcast_select_fusion.rest_4_.rest_7_), channel_id=1, source_target_pairs={{0,16},{16,0},{1,17},{17,1},{2,18},{18,2},{3,19},{19,3},{4,20},{20... | collective-permute-start | bytes 1990664 | tf_op jit(solution)/shard_map/ppermute | solution.py:920
  106.7 39.0 %collective-permute-start.30 = (bf16[2,8,16,1152]{3,2,1,0:T(8,128)(2,1)S(1)}, bf16[2,8,16,1152]{3,2,1,0:T(8,128)(2,1)S(1)}, u32[]{:S(2)}, u32[]{:S(2)}) collective-permute-start(bf16[2,8,16,1152]{3,2,1,0:T(8,128)(2,1)S(1)} %get-tuple-element.337), channel_id=1, source_target_pairs={{0,8},{2,10},{4,12},{6,14},{8,0},{10,2},{12,4},{14,6},{1,9},{3,11}... | collective-permute-start | bytes 1769480 | tf_op jit(solution)/shard_map/ppermute | solution.py:920
  106.7 51.9 %collective-permute-start.31 = (bf16[2,8,16,1152]{3,2,1,0:T(8,128)(2,1)S(1)}, bf16[2,8,16,1152]{3,2,1,0:T(8,128)(2,1)S(1)}, u32[]{:S(2)}, u32[]{:S(2)}) collective-permute-start(bf16[2,8,16,1152]{3,2,1,0:T(8,128)(2,1)S(1)} %get-tuple-element.338), channel_id=1, source_target_pairs={{0,12},{2,14},{4,8},{6,10},{8,4},{10,6},{12,0},{14,2},{1,13},{3,15... | collective-permute-start | bytes 1769480 | tf_op jit(solution)/shard_map/ppermute | solution.py:920
  107.9 50.7 %collective-permute-start.27 = (bf16[2,144,1152]{2,1,0:T(8,128)(2,1)S(1)}, bf16[2,144,1152]{2,1,0:T(8,128)(2,1)}, u32[]{:S(2)}, u32[]{:S(2)}) collective-permute-start(bf16[2,144,1152]{2,1,0:T(8,128)(2,1)S(1)} %collective-permute-done.21.rest_1_.rest_4_), channel_id=1, source_target_pairs={{0,16},{16,0},{1,17},{17,1},{2,18},{18,2},{3,19},{19,3},{4,20},{20... | collective-permute-start | bytes 1990664 | tf_op jit(solution)/shard_map/ppermute | solution.py:920
  158.6 4.0 collective-permute-start.33
  158.7 3.9 collective-permute-start.32
  159.2 3.8 collective-permute-start.34
  163.1 42.9 %collective-permute-start.35 = (bf16[4,4,16,1152]{3,2,1,0:T(8,128)(2,1)}, bf16[4,4,16,1152]{3,2,1,0:T(8,128)(2,1)S(1)}, u32[]{:S(2)}, u32[]{:S(2)}) collective-permute-start(bf16[4,4,16,1152]{3,2,1,0:T(8,128)(2,1)} %copy-done.65), channel_id=1, source_target_pairs={{0,2},{2,0},{4,6},{6,4},{8,10},{10,8},{12,14},{14,12},{1,3},{3,1},... | collective-permute-start | bytes 1769480 | tf_op jit(solution)/shard_map/ppermute | solution.py:920
  164.6 41.4 %collective-permute-start.36 = (bf16[4,4,16,1152]{3,2,1,0:T(8,128)(2,1)}, bf16[4,4,16,1152]{3,2,1,0:T(8,128)(2,1)S(1)}, u32[]{:S(2)}, u32[]{:S(2)}) collective-permute-start(bf16[4,4,16,1152]{3,2,1,0:T(8,128)(2,1)} %copy-done.64), channel_id=1, source_target_pairs={{0,16},{16,0},{1,17},{17,1},{2,18},{18,2},{3,19},{19,3},{4,20},{20... | collective-permute-start | bytes 1769480 | tf_op jit(solution)/shard_map/ppermute | solution.py:920
  165.1 40.8 %collective-permute-start.37 = (bf16[4,4,16,1152]{3,2,1,0:T(8,128)(2,1)}, bf16[4,4,16,1152]{3,2,1,0:T(8,128)(2,1)S(1)}, u32[]{:S(2)}, u32[]{:S(2)}) collective-permute-start(bf16[4,4,16,1152]{3,2,1,0:T(8,128)(2,1)} %copy-done.63), channel_id=1, source_target_pairs={{0,18},{2,16},{4,22},{6,20},{8,26},{10,24},{12,30},{14,28},{16,2},... | collective-permute-start | bytes 1769480 | tf_op jit(solution)/shard_map/ppermute | solution.py:994
  166.5 40.2 %collective-permute-start.38 = (bf16[2,144,1152]{2,1,0:T(8,128)(2,1)}, bf16[2,144,1152]{2,1,0:T(8,128)(2,1)S(1)}, u32[]{:S(2)}, u32[]{:S(2)}) collective-permute-start(bf16[2,144,1152]{2,1,0:T(8,128)(2,1)} %collective-permute-done.29.rest_5_.rest_8_), channel_id=1, source_target_pairs={{0,16},{16,0},{1,17},{17,1},{2,18},{18,2},{3,19},{19,3},{4,20},{20... | collective-permute-start | bytes 1990664 | tf_op jit(solution)/shard_map/ppermute | solution.py:920
  167.9 48.6 %collective-permute-start.39 = (bf16[4,8,16,1152]{3,2,1,0:T(8,128)(2,1)S(1)}, bf16[4,8,16,1152]{3,2,1,0:T(8,128)(2,1)S(1)}, u32[]{:S(2)}, u32[]{:S(2)}) collective-permute-start(bf16[4,8,16,1152]{3,2,1,0:T(8,128)(2,1)S(1)} %pad_maximum_fusion), channel_id=1, source_target_pairs={{0,2},{2,0},{4,6},{6,4},{8,10},{10,8},{12,14},{14,12},{1,3},{3,1},... | collective-permute-start | bytes 3538952 | tf_op jit(solution)/shard_map/ppermute | solution.py:920
  216.6 2.7 collective-permute-start.40
  217.7 54.9 %collective-permute-start.45 = (bf16[4,4,16,1152]{3,2,1,0:T(8,128)(2,1)S(1)}, bf16[4,4,16,1152]{3,2,1,0:T(8,128)(2,1)S(1)}, u32[]{:S(2)}, u32[]{:S(2)}) collective-permute-start(bf16[4,4,16,1152]{3,2,1,0:T(8,128)(2,1)S(1)} %pad_maximum_fusion.3), channel_id=1, source_target_pairs={{0,8},{2,10},{4,12},{6,14},{8,0},{10,2},{12,4},{14,6},{1,9},{3,11}... | collective-permute-start | bytes 1769480 | tf_op jit(solution)/shard_map/ppermute | solution.py:920
  217.9 65.7 %collective-permute-start.46 = (bf16[4,4,16,1152]{3,2,1,0:T(8,128)(2,1)S(1)}, bf16[4,4,16,1152]{3,2,1,0:T(8,128)(2,1)S(1)}, u32[]{:S(2)}, u32[]{:S(2)}) collective-permute-start(bf16[4,4,16,1152]{3,2,1,0:T(8,128)(2,1)S(1)} %pad_maximum_fusion.4), channel_id=1, source_target_pairs={{0,12},{2,14},{4,8},{6,10},{8,4},{10,6},{12,0},{14,2},{1,13},{3,15... | collective-permute-start | bytes 1769480 | tf_op jit(solution)/shard_map/ppermute | solution.py:920
  219.3 23.5 %collective-permute-start.41 = (bf16[4,4,16,1152]{3,2,1,0:T(8,128)(2,1)S(1)}, bf16[4,4,16,1152]{3,2,1,0:T(8,128)(2,1)S(1)}, u32[]{:S(2)}, u32[]{:S(2)}) collective-permute-start(bf16[4,4,16,1152]{3,2,1,0:T(8,128)(2,1)S(1)} %get-tuple-element.376), channel_id=1, source_target_pairs={{0,2},{2,0},{4,6},{6,4},{8,10},{10,8},{12,14},{14,12},{1,3},{3,1},... | collective-permute-start | bytes 1769480 | tf_op jit(solution)/shard_map/ppermute | solution.py:920
  220.3 22.5 %collective-permute-start.42 = (bf16[4,4,16,1152]{3,2,1,0:T(8,128)(2,1)S(1)}, bf16[4,4,16,1152]{3,2,1,0:T(8,128)(2,1)S(1)}, u32[]{:S(2)}, u32[]{:S(2)}) collective-permute-start(bf16[4,4,16,1152]{3,2,1,0:T(8,128)(2,1)S(1)} %get-tuple-element.377), channel_id=1, source_target_pairs={{0,16},{16,0},{1,17},{17,1},{2,18},{18,2},{3,19},{19,3},{4,20},{20... | collective-permute-start | bytes 1769480 | tf_op jit(solution)/shard_map/ppermute | solution.py:920
  220.9 27.0 %collective-permute-start.43 = (bf16[4,4,16,1152]{3,2,1,0:T(8,128)(2,1)S(1)}, bf16[4,4,16,1152]{3,2,1,0:T(8,128)(2,1)S(1)}, u32[]{:S(2)}, u32[]{:S(2)}) collective-permute-start(bf16[4,4,16,1152]{3,2,1,0:T(8,128)(2,1)S(1)} %get-tuple-element.378), channel_id=1, source_target_pairs={{0,18},{2,16},{4,22},{6,20},{8,26},{10,24},{12,30},{14,28},{16,2},... | collective-permute-start | bytes 1769480 | tf_op jit(solution)/shard_map/ppermute | solution.py:994
  248.2 72.6 %collective-permute-start.50 = (bf16[4,4,16,1152]{3,2,1,0:T(8,128)(2,1)S(1)}, bf16[4,4,16,1152]{3,2,1,0:T(8,128)(2,1)S(1)}, u32[]{:S(2)}, u32[]{:S(2)}) collective-permute-start(bf16[4,4,16,1152]{3,2,1,0:T(8,128)(2,1)S(1)} %pad_maximum_fusion.8), channel_id=1, source_target_pairs={{0,12},{2,14},{4,8},{6,10},{8,4},{10,6},{12,0},{14,2},{1,13},{3,15... | collective-permute-start | bytes 1769480 | tf_op jit(solution)/shard_map/ppermute | solution.py:920
  249.3 34.3 %collective-permute-start.44 = (bf16[4,4,16,1152]{3,2,1,0:T(8,128)(2,1)S(1)}, bf16[4,4,16,1152]{3,2,1,0:T(8,128)(2,1)S(1)}, u32[]{:S(2)}, u32[]{:S(2)}) collective-permute-start(bf16[4,4,16,1152]{3,2,1,0:T(8,128)(2,1)S(1)} %pad_maximum_fusion.2), channel_id=1, source_target_pairs={{0,4},{2,6},{4,0},{6,2},{8,12},{10,14},{12,8},{14,10},{1,5},{3,7},... | collective-permute-start | bytes 1769480 | tf_op jit(solution)/shard_map/ppermute | solution.py:920
  283.6 37.1 %collective-permute-start.48 = (bf16[4,4,16,1152]{3,2,1,0:T(8,128)(2,1)S(1)}, bf16[4,4,16,1152]{3,2,1,0:T(8,128)(2,1)S(1)}, u32[]{:S(2)}, u32[]{:S(2)}) collective-permute-start(bf16[4,4,16,1152]{3,2,1,0:T(8,128)(2,1)S(1)} %pad_maximum_fusion.6), channel_id=1, source_target_pairs={{0,4},{2,6},{4,0},{6,2},{8,12},{10,14},{12,8},{14,10},{1,5},{3,7},... | collective-permute-start | bytes 1769480 | tf_op jit(solution)/shard_map/ppermute | solution.py:920
  284.1 36.6 %collective-permute-start.49 = (bf16[4,4,16,1152]{3,2,1,0:T(8,128)(2,1)S(1)}, bf16[4,4,16,1152]{3,2,1,0:T(8,128)(2,1)S(1)}, u32[]{:S(2)}, u32[]{:S(2)}) collective-permute-start(bf16[4,4,16,1152]{3,2,1,0:T(8,128)(2,1)S(1)} %pad_maximum_fusion.7), channel_id=1, source_target_pairs={{0,8},{2,10},{4,12},{6,14},{8,0},{10,2},{12,4},{14,6},{1,9},{3,11}... | collective-permute-start | bytes 1769480 | tf_op jit(solution)/shard_map/ppermute | solution.py:920
  286.0 34.8 %collective-permute-start.47 = (bf16[4,128,1152]{2,1,0:T(8,128)(2,1)S(1)}, bf16[4,128,1152]{2,1,0:T(8,128)(2,1)S(1)}, u32[]{:S(2)}, u32[]{:S(2)}) collective-permute-start(bf16[4,128,1152]{2,1,0:T(8,128)(2,1)S(1)} %get-tuple-element.394), channel_id=1, source_target_pairs={{0,2},{2,0},{4,6},{6,4},{8,10},{10,8},{12,14},{14,12},{1,3},{3,1},... | collective-permute-start | bytes 3538952 | tf_op jit(solution)/shard_map/ppermute | solution.py:920
  322.0 44.9 %collective-permute-start.51 = (bf16[2,128,1152]{2,1,0:T(8,128)(2,1)S(1)}, bf16[2,128,1152]{2,1,0:T(8,128)(2,1)S(1)}, u32[]{:S(2)}, u32[]{:S(2)}) collective-permute-start(bf16[2,128,1152]{2,1,0:T(8,128)(2,1)S(1)} %pad_maximum_fusion.10), channel_id=1, source_target_pairs={{0,4},{2,6},{4,0},{6,2},{8,12},{10,14},{12,8},{14,10},{1,5},{3,7},... | collective-permute-start | bytes 1769480 | tf_op jit(solution)/shard_map/ppermute | solution.py:920
  323.0 43.9 %collective-permute-start.52 = (bf16[2,128,1152]{2,1,0:T(8,128)(2,1)S(1)}, bf16[2,128,1152]{2,1,0:T(8,128)(2,1)S(1)}, u32[]{:S(2)}, u32[]{:S(2)}) collective-permute-start(bf16[2,128,1152]{2,1,0:T(8,128)(2,1)S(1)} %pad_maximum_fusion.11), channel_id=1, source_target_pairs={{0,8},{2,10},{4,12},{6,14},{8,0},{10,2},{12,4},{14,6},{1,9},{3,11}... | collective-permute-start | bytes 1769480 | tf_op jit(solution)/shard_map/ppermute | solution.py:920
  324.2 50.7 %collective-permute-start.53 = (bf16[2,128,1152]{2,1,0:T(8,128)(2,1)S(1)}, bf16[2,128,1152]{2,1,0:T(8,128)(2,1)S(1)}, u32[]{:S(2)}, u32[]{:S(2)}) collective-permute-start(bf16[2,128,1152]{2,1,0:T(8,128)(2,1)S(1)} %pad_maximum_fusion.12), channel_id=1, source_target_pairs={{0,12},{2,14},{4,8},{6,10},{8,4},{10,6},{12,0},{14,2},{1,13},{3,15... | collective-permute-start | bytes 1769480 | tf_op jit(solution)/shard_map/ppermute | solution.py:920
  374.9 6.8 %collective-permute-start.54 = (bf16[64,1152]{1,0:T(8,128)(2,1)}, bf16[64,1152]{1,0:T(8,128)(2,1)S(1)}, u32[]{:S(2)}, u32[]{:S(2)}) collective-permute-start(bf16[64,1152]{1,0:T(8,128)(2,1)} %get-tuple-element.431), channel_id=1, source_target_pairs={{0,2},{2,0},{4,6},{6,4},{8,10},{10,8},{12,14},{14,12},{1,3},{3,1},... | collective-permute-start | bytes 442376 | tf_op jit(solution)/shard_map/ppermute | solution.py:920
  375.9 7.3 %collective-permute-start.55 = (bf16[64,1152]{1,0:T(8,128)(2,1)}, bf16[64,1152]{1,0:T(8,128)(2,1)S(1)}, u32[]{:S(2)}, u32[]{:S(2)}) collective-permute-start(bf16[64,1152]{1,0:T(8,128)(2,1)} %get-tuple-element.432), channel_id=1, source_target_pairs={{0,4},{2,6},{4,0},{6,2},{8,12},{10,14},{12,8},{14,10},{1,5},{3,7},... | collective-permute-start | bytes 442376 | tf_op jit(solution)/shard_map/ppermute | solution.py:920
  375.9 47.2 %collective-permute-start.56 = (bf16[64,1152]{1,0:T(8,128)(2,1)}, bf16[64,1152]{1,0:T(8,128)(2,1)S(1)}, u32[]{:S(2)}, u32[]{:S(2)}) collective-permute-start(bf16[64,1152]{1,0:T(8,128)(2,1)} %get-tuple-element.433), channel_id=1, source_target_pairs={{0,6},{2,4},{4,2},{6,0},{8,14},{10,12},{12,10},{14,8},{1,7},{3,5},... | collective-permute-start | bytes 442376 | tf_op jit(solution)/shard_map/ppermute | solution.py:920
  378.4 44.7 %collective-permute-start.57 = (bf16[64,1152]{1,0:T(8,128)(2,1)}, bf16[64,1152]{1,0:T(8,128)(2,1)S(1)}, u32[]{:S(2)}, u32[]{:S(2)}) collective-permute-start(bf16[64,1152]{1,0:T(8,128)(2,1)} %get-tuple-element.434), channel_id=1, source_target_pairs={{0,8},{2,10},{4,12},{6,14},{8,0},{10,2},{12,4},{14,6},{1,9},{3,11}... | collective-permute-start | bytes 442376 | tf_op jit(solution)/shard_map/ppermute | solution.py:920
  378.8 44.3 %collective-permute-start.58 = (bf16[64,1152]{1,0:T(8,128)(2,1)}, bf16[64,1152]{1,0:T(8,128)(2,1)S(1)}, u32[]{:S(2)}, u32[]{:S(2)}) collective-permute-start(bf16[64,1152]{1,0:T(8,128)(2,1)} %get-tuple-element.435), channel_id=1, source_target_pairs={{0,10},{2,8},{4,14},{6,12},{8,2},{10,0},{12,6},{14,4},{1,11},{3,9}... | collective-permute-start | bytes 442376 | tf_op jit(solution)/shard_map/ppermute | solution.py:920
  381.7 41.3 %collective-permute-start.59 = (bf16[64,1152]{1,0:T(8,128)(2,1)}, bf16[64,1152]{1,0:T(8,128)(2,1)S(1)}, u32[]{:S(2)}, u32[]{:S(2)}) collective-permute-start(bf16[64,1152]{1,0:T(8,128)(2,1)} %get-tuple-element.436), channel_id=1, source_target_pairs={{0,12},{2,14},{4,8},{6,10},{8,4},{10,6},{12,0},{14,2},{1,13},{3,15... | collective-permute-start | bytes 442376 | tf_op jit(solution)/shard_map/ppermute | solution.py:920
  383.2 39.9 %collective-permute-start.60 = (bf16[64,1152]{1,0:T(8,128)(2,1)}, bf16[64,1152]{1,0:T(8,128)(2,1)S(1)}, u32[]{:S(2)}, u32[]{:S(2)}) collective-permute-start(bf16[64,1152]{1,0:T(8,128)(2,1)} %get-tuple-element.437), channel_id=1, source_target_pairs={{0,14},{2,12},{4,10},{6,8},{8,6},{10,4},{12,2},{14,0},{1,15},{3,13... | collective-permute-start | bytes 442376 | tf_op jit(solution)/shard_map/ppermute | solution.py:920
  423.1 8.3 %collective-permute-start.61 = (bf16[64,1152]{1,0:T(8,128)(2,1)}, bf16[64,1152]{1,0:T(8,128)(2,1)S(1)}, u32[]{:S(2)}, u32[]{:S(2)}) collective-permute-start(bf16[64,1152]{1,0:T(8,128)(2,1)} %get-tuple-element.447), channel_id=1, source_target_pairs={{0,2},{2,0},{4,6},{6,4},{8,10},{10,8},{12,14},{14,12},{1,3},{3,1},... | collective-permute-start | bytes 442376 | tf_op jit(solution)/shard_map/ppermute | solution.py:920
  424.7 7.9 %collective-permute-start.62 = (bf16[64,1152]{1,0:T(8,128)(2,1)}, bf16[64,1152]{1,0:T(8,128)(2,1)S(1)}, u32[]{:S(2)}, u32[]{:S(2)}) collective-permute-start(bf16[64,1152]{1,0:T(8,128)(2,1)} %get-tuple-element.448), channel_id=1, source_target_pairs={{0,4},{2,6},{4,0},{6,2},{8,12},{10,14},{12,8},{14,10},{1,5},{3,7},... | collective-permute-start | bytes 442376 | tf_op jit(solution)/shard_map/ppermute | solution.py:920
  427.6 11.7 %collective-permute-start.63 = (bf16[64,1152]{1,0:T(8,128)(2,1)}, bf16[64,1152]{1,0:T(8,128)(2,1)S(1)}, u32[]{:S(2)}, u32[]{:S(2)}) collective-permute-start(bf16[64,1152]{1,0:T(8,128)(2,1)} %get-tuple-element.449), channel_id=1, source_target_pairs={{0,6},{2,4},{4,2},{6,0},{8,14},{10,12},{12,10},{14,8},{1,7},{3,5},... | collective-permute-start | bytes 442376 | tf_op jit(solution)/shard_map/ppermute | solution.py:920
  428.0 13.2 %collective-permute-start.64 = (bf16[64,1152]{1,0:T(8,128)(2,1)}, bf16[64,1152]{1,0:T(8,128)(2,1)S(1)}, u32[]{:S(2)}, u32[]{:S(2)}) collective-permute-start(bf16[64,1152]{1,0:T(8,128)(2,1)} %get-tuple-element.450), channel_id=1, source_target_pairs={{0,8},{2,10},{4,12},{6,14},{8,0},{10,2},{12,4},{14,6},{1,9},{3,11}... | collective-permute-start | bytes 442376 | tf_op jit(solution)/shard_map/ppermute | solution.py:920
  429.7 16.2 %collective-permute-start.65 = (bf16[64,1152]{1,0:T(8,128)(2,1)}, bf16[64,1152]{1,0:T(8,128)(2,1)S(1)}, u32[]{:S(2)}, u32[]{:S(2)}) collective-permute-start(bf16[64,1152]{1,0:T(8,128)(2,1)} %get-tuple-element.451), channel_id=1, source_target_pairs={{0,10},{2,8},{4,14},{6,12},{8,2},{10,0},{12,6},{14,4},{1,11},{3,9}... | collective-permute-start | bytes 442376 | tf_op jit(solution)/shard_map/ppermute | solution.py:920
  431.5 18.0 %collective-permute-start.66 = (bf16[64,1152]{1,0:T(8,128)(2,1)}, bf16[64,1152]{1,0:T(8,128)(2,1)S(1)}, u32[]{:S(2)}, u32[]{:S(2)}) collective-permute-start(bf16[64,1152]{1,0:T(8,128)(2,1)} %get-tuple-element.452), channel_id=1, source_target_pairs={{0,12},{2,14},{4,8},{6,10},{8,4},{10,6},{12,0},{14,2},{1,13},{3,15... | collective-permute-start | bytes 442376 | tf_op jit(solution)/shard_map/ppermute | solution.py:920
  432.6 19.3 %collective-permute-start.67 = (bf16[64,1152]{1,0:T(8,128)(2,1)}, bf16[64,1152]{1,0:T(8,128)(2,1)S(1)}, u32[]{:S(2)}, u32[]{:S(2)}) collective-permute-start(bf16[64,1152]{1,0:T(8,128)(2,1)} %get-tuple-element.453), channel_id=1, source_target_pairs={{0,14},{2,12},{4,10},{6,8},{8,6},{10,4},{12,2},{14,0},{1,15},{3,13... | collective-permute-start | bytes 442376 | tf_op jit(solution)/shard_map/ppermute | solution.py:920
  (85 other events, 2638.6 us)

commit v3 on v2

--- a/solution.py
+++ b/solution.py
@@ -15,7 +15,7 @@
 EXPONENT_SCALE = HEAD_DIM ** (-0.5) * math.log2(math.e)
 VMEM_LIMIT = 40 * 1024 * 1024
 SPACE_VMEM_LIMIT = 26 * 1024 * 1024
-TANGENT_VMEM_LIMIT = 60 * 1024 * 1024
+FULL_VMEM_LIMIT = 60 * 1024 * 1024
 
 epsilon = 1e-06
 
@@ -359,7 +359,7 @@
             ref[line, 0] = query_ref[pl.ds(start, ROW_TILE), :]
 
 
-def spatial_layer(seat, moment, clean, noise, shift, weights, frames, seats):
+def spatial_layer(seat, moment, clean, noise, shift, limit, weights, frames, seats):
     pieces, layout = weights
     positions, width = clean.shape[1:]
     frame_block = pl.BlockSpec(
@@ -390,7 +390,7 @@
             + [vmem(positions, width)] * 4
             + [pltpu.SemaphoreType.DMA((len(layout),))],
         ),
-        compiler_params=pltpu.CompilerParams(vmem_limit_bytes=SPACE_VMEM_LIMIT),
+        compiler_params=pltpu.CompilerParams(vmem_limit_bytes=limit),
         cost_estimate=pl.CostEstimate(
             flops=14 * rows * width * width,
             bytes_accessed=8 * width * width + 6 * rows * width,
@@ -593,10 +593,14 @@
     @pl.when(pl.program_id(0) == 0)
     def _():
         weights = weight_copies(seat_ref, layout, weight_pieces, weights_ref, weight_sems)
-        lines = piece_count - 1
+        lines = piece_count - 2
         copies = []
         for index in range(2 * lines):
-            piece = pieces[lines].at[index // 2] if index % 2 else pieces[index // 2].at[0]
+            if index % 2:
+                part, line = divmod(index // 2, lines // 2)
+                piece = pieces[lines + part].at[line]
+            else:
+                piece = pieces[index // 2].at[0]
             count = piece.shape[0]
             copies.append(
                 pltpu.make_async_copy(
@@ -862,7 +866,7 @@
         1,
         rows,
         width,
-        TANGENT_VMEM_LIMIT,
+        FULL_VMEM_LIMIT,
         grid=(steps,),
         out_shape=[piece] * seats + [other] * first,
         in_specs=[IN_SMEM] * 2
@@ -1085,10 +1089,12 @@
     )
     cond, uncond = [
         functools.partial(
-            spatial_layer, seat, timestep, clean, noise, shift,
+            spatial_layer, seat, timestep, clean, noise, shift, limit,
             frames=clean.shape[0] // sides, seats=seats,
         )
-        for shift in (cond_shift, uncond_shift)
+        for shift, limit in (
+            (cond_shift, SPACE_VMEM_LIMIT), (uncond_shift, FULL_VMEM_LIMIT)
+        )
     ]
     time_xy = flip(time_y, "cfg", 1)
     time_far_x = flip(time_far, "cfg", 1)
@@ -1101,18 +1107,23 @@
         cond, time_xy, time_far_x, time_far_y, noisy_came
     )
     time_late = [flip(piece, "clip", 1) for piece in (time_xy, time_far_y, time_far_x)]
-    noisy_low = jnp.stack([line[1] for line in noisy_came])
-    cond, time_far_y, time_late, noisy_low = together(cond, time_far_y, time_late, noisy_low)
+    half = len(noisy_came) // 2
+    noisy_low = jnp.stack([line[1] for line in noisy_came[:half]])
+    noisy_last = jnp.stack([line[1] for line in noisy_came[half:]])
+    cond, time_far_y, time_late, noisy_low, noisy_last = together(
+        cond, time_far_y, time_late, noisy_low, noisy_last
+    )
     uncond = uncond(weights=space_weights)
     time_far_xy = flip(time_far_y, "cfg", 1)
     noisy_low = flip(noisy_low, "seq", 1)
-    cond, uncond, time_far_xy, noisy_low = together(
-        to_neighbours(*cond), uncond, time_far_xy, noisy_low
-    )
+    cond, uncond, time_far_xy, noisy_low, noisy_last = together(
+        to_neighbours(*cond), uncond, time_far_xy, noisy_low, noisy_last
+    )
+    noisy_last = flip(noisy_last, "seq", 1)
     lines = [jnp.stack([given[line] for given in cond]) for line in range(seats // 2)]
     far_lines = [flip(lines[i], "seq", 2 * i) for i in range(2, seats // 2)]
     time_last = flip(time_far_xy, "clip", 1)
-    uncond, time_last = together(uncond, time_last)
+    uncond, time_last, noisy_last = together(uncond, time_last, noisy_last)
     time_weights = (
         [time_near, time_y, time_x, time_xy, time_far, time_far_y, time_far_x, time_far_xy]
         + list(time_other) + list(time_late) + [time_last],
@@ -1124,7 +1135,7 @@
             )
         ],
     )
-    noisy_in = list(noisy_came) + [noisy_low]
+    noisy_in = list(noisy_came) + [noisy_low, noisy_last]
     kept, low, across, both = uncond
     low, across, both = flip(low, "seq", 1), flip(across, "cfg", 1), over_both(both)
     rows, primal = student_rows(seat, cond_shift, down, up, time_weights, noisy_in, frames)

time: 464 us -> 457 us (0.985); the launches traced: 454 us -> 453 us
  local copies, waits for them, and re-layouts: 31.1 us -> 23 us
  starting transfers between devices: 74.2 us -> 68.2 us
  waiting for transfers between devices: 129 us -> 134 us
    unnamed x156 -> x146, local copies, waits for them, and re-layouts: 26.1 us -> 13.6 us
    ppermute x62 -> x63, waiting for transfers between devices: 110 us -> 118 us  [flip(): return lax.ppermute(value, axis, pairs)]
    ppermute x62 -> x63, starting transfers between devices: 60.2 us -> 54.6 us  [flip(): return lax.ppermute(value, axis, pairs)]
    pallas_call x2, Pallas kernels: 51.9 us -> 56.8 us  [spatial_layer(): pl.pallas_call(functools.partial(space_kernel, layout, len(pieces), 4), o...]
  transfers between devices with their start and end apart: 68 -> 69, of which waited for: 28 -> 29; matrix products, arithmetic and copies ran while one was open for 2% -> 3% of each run, Pallas kernels for 46% -> 47%
where the time goes in v3:
time: 457 us; the launch traced here: 453 us
  Pallas kernels  214 us (47%)
  waiting for transfers between devices  134 us (29%)
  starting transfers between devices  68.2 us (15%)
  local copies, waits for them, and re-layouts  23 us (5%)
  other arithmetic  9.92 us (2%)
    ppermute x63, waiting for transfers between devices, flip(): return lax.ppermute(value, axis, pairs)  118 us
    pallas_call x2, Pallas kernels, student_tangent(): time_call(functools.partial(tangent_kernel, layout, (len(weights), len(pi...  79.8 us
    pallas_call x2, Pallas kernels, spatial_layer(): pl.pallas_call(functools.partial(space_kernel, layout, len(pieces), 4), o...  56.8 us
    ppermute x63, starting transfers between devices, flip(): return lax.ppermute(value, axis, pairs)  54.6 us
    pallas_call x1, Pallas kernels, teacher_velocity(): time_call(functools.partial(teacher_kernel, layout, (len(weights), len(pi...  32.8 us
    pallas_call x1, Pallas kernels, student_rows(): time_call(functools.partial(student_rows_kernel, layout, (len(weights), l...  19.6 us
    pallas_call x1, Pallas kernels, student_mix(): time_call(functools.partial(student_mix_kernel, layout, frames), 0.6, row...  18 us
    unnamed x146, local copies, waits for them, and re-layouts  13.6 us
  transfers between devices with their start and end apart: 69, of which 29 were waited for; matrix products, arithmetic and copies ran while one was open for 3% of the time, Pallas kernels for 47%

profile of v3, /device:TPU:8, one launch (start us, length us, event | category | flops | bytes accessed | tf_op | source)
XLA Modules:
  0.0 452.7 jit_solution(5594800373102204041)
XLA Ops:
  3.0 8.4 %collective-permute-done = bf16[2,72,1152]{2,1,0:T(8,128)(2,1)S(1)} collective-permute-done((bf16[2,72,1152]{2,1,0:T(8,128)(2,1)S(1)}, bf16[2,72,1152]{2,1,0:T(8,128)(2,1)S(1)}, u32[]{:S(2)}, u32[]{:S(2)}) %collective-permute-start) | collective-permute-done | bytes 331808 | tf_op jit(solution)/shard_map/ppermute | solution.py:924
  11.6 3.5 collective-permute-start.4
  15.2 1.6 collective-permute-start.2
  16.7 1.5 collective-permute-start.1
  18.2 9.6 %collective-permute-done.5 = bf16[2,72,1152]{2,1,0:T(8,128)(2,1)S(1)} collective-permute-done((bf16[2,72,1152]{2,1,0:T(8,128)(2,1)S(1)}, bf16[2,72,1152]{2,1,0:T(8,128)(2,1)S(1)}, u32[]{:S(2)}, u32[]{:S(2)}) %collective-permute-start.5) | collective-permute-done | bytes 331808 | tf_op jit(solution)/shard_map/ppermute | solution.py:924
  28.0 1.3 collective-permute-done.4
  30.2 2.4 collective-permute-done.2.rest_2_
  34.5 2.1 collective-permute-start.7
  37.2 3.6 collective-permute-start.10
  40.9 1.6 collective-permute-start.6
  46.1 2.3 copy-done
  48.4 2.3 copy-done.1
  50.8 2.6 shard_map.140
  53.4 1.4 broadcast_select_fusion.1.rest_4_
  54.9 2.9 collective-permute-done.6.rest_3_
  57.8 1.3 collective-permute-start.16
  59.2 1.6 collective-permute-start.13
  60.7 1.5 collective-permute-start.12
  62.2 12.3 %collective-permute-done.16 = bf16[2,144,1152]{2,1,0:T(8,128)(2,1)S(1)} collective-permute-done((bf16[2,144,1152]{2,1,0:T(8,128)(2,1)}, bf16[2,144,1152]{2,1,0:T(8,128)(2,1)S(1)}, u32[]{:S(2)}, u32[]{:S(2)}) %collective-permute-start.16) | collective-permute-done | bytes 663584 | tf_op jit(solution)/shard_map/ppermute | solution.py:958
  77.8 2.1 collective-permute-done.18.rest_12_
  80.0 2.0 collective-permute-done.19.rest_13_
  82.7 1.5 collective-permute-start.21
  84.7 15.4 %collective-permute-done.23.rest_17_ = bf16[2,8,16,1152]{3,2,1,0:T(8,128)(2,1)S(1)} collective-permute-done((bf16[2,8,16,1152]{3,2,1,0:T(8,128)(2,1)S(1)}, bf16[2,8,16,1152]{3,2,1,0:T(8,128)(2,1)S(1)}, u32[]{:S(2)}, u32[]{:S(2)}) %collective-permute-start.23) | collective-permute-done | bytes 589856 | tf_op jit(solution)/shard_map/ppermute | solution.py:924
  100.8 1.5 collective-permute-done.24.rest_15_
  104.2 1.3 collective-permute-start.29
  107.9 1.4 collective-permute-start.27
  109.3 2.3 copy-done.2
  111.7 26.7 %shard_map.141 = (bf16[4,4,16,1152]{3,2,1,0:T(8,128)(2,1)S(1)}, bf16[4,4,16,1152]{3,2,1,0:T(8,128)(2,1)}, bf16[4,4,16,1152]{3,2,1,0:T(8,128)(2,1)}, bf16[4,4,16,1152]{3,2,1,0:T(8,128)(2,1)}) custom-call(s32[3]{0:T(128)S(1)} %pad_add_fusion.seat_ref, f32[1]{0:T(128)} %copy.20.moment_ref, bf16[8,256,1152]{2,1,0:T(8,128)(2,1)S(1)} %bitcast.15, ...), custom_call_target="tpu_custom_call" | custom-call | flops 19025362944 | bytes 17694720 | tf_op jit(solution)/shard_map/pallas_call | solution.py:372
  139.4 6.3 %collective-permute-done.30.rest_18_ = bf16[2,8,16,1152]{3,2,1,0:T(8,128)(2,1)S(1)} collective-permute-done((bf16[2,8,16,1152]{3,2,1,0:T(8,128)(2,1)S(1)}, bf16[2,8,16,1152]{3,2,1,0:T(8,128)(2,1)S(1)}, u32[]{:S(2)}, u32[]{:S(2)}) %collective-permute-start.30) | collective-permute-done | bytes 589856 | tf_op jit(solution)/shard_map/ppermute | solution.py:924
  145.7 12.9 %collective-permute-done.31.rest_19_ = bf16[2,8,16,1152]{3,2,1,0:T(8,128)(2,1)S(1)} collective-permute-done((bf16[2,8,16,1152]{3,2,1,0:T(8,128)(2,1)S(1)}, bf16[2,8,16,1152]{3,2,1,0:T(8,128)(2,1)S(1)}, u32[]{:S(2)}, u32[]{:S(2)}) %collective-permute-start.31) | collective-permute-done | bytes 589856 | tf_op jit(solution)/shard_map/ppermute | solution.py:924
  165.0 1.6 collective-permute-start.35
  167.1 1.4 collective-permute-start.37
  168.5 1.5 collective-permute-start.39
  170.6 30.1 %shard_map.142 = (bf16[4,4,16,1152]{3,2,1,0:T(8,128)(2,1)}, bf16[4,4,16,1152]{3,2,1,0:T(8,128)(2,1)}, bf16[4,4,16,1152]{3,2,1,0:T(8,128)(2,1)}, bf16[4,4,16,1152]{3,2,1,0:T(8,128)(2,1)}) custom-call(s32[3]{0:T(128)} %copy-done.20, f32[1]{0:T(128)} %copy.20.moment_ref, bf16[8,256,1152]{2,1,0:T(8,128)(2,1)} %clean_ref.5, bf16[8,256,1152]{2,1,0:T(8,128)(2,1)} %noise_ref.5, ...), custom_call_target="tpu_custom_call" | custom-call | flops 19025362944 | bytes 17694720 | tf_op jit(solution)/shard_map/pallas_call | solution.py:372
  200.7 5.5 %collective-permute-done.39.rest_20_ = bf16[2,8,16,1152]{3,2,1,0:T(8,128)(2,1)S(1)} collective-permute-done((bf16[2,8,16,1152]{3,2,1,0:T(8,128)(2,1)}, bf16[2,8,16,1152]{3,2,1,0:T(8,128)(2,1)S(1)}, u32[]{:S(2)}, u32[]{:S(2)}) %collective-permute-start.39) | collective-permute-done | bytes 589856 | tf_op jit(solution)/shard_map/ppermute | solution.py:924
  206.2 2.9 collective-permute-done.38.rest_7_.rest_10_
  209.2 1.4 fusion.9
  217.1 10.9 %collective-permute-done.41.rest_21_ = bf16[2,8,16,1152]{3,2,1,0:T(8,128)(2,1)S(1)} collective-permute-done((bf16[2,8,16,1152]{3,2,1,0:T(8,128)(2,1)S(1)}, bf16[2,8,16,1152]{3,2,1,0:T(8,128)(2,1)S(1)}, u32[]{:S(2)}, u32[]{:S(2)}) %collective-permute-start.41) | collective-permute-done | bytes 589856 | tf_op jit(solution)/shard_map/ppermute | solution.py:924
  228.6 1.4 collective-permute-start.43
  230.0 1.6 collective-permute-start.44
  232.8 19.6 %shard_map.143 = (bf16[1024,1152]{1,0:T(8,128)(2,1)}, bf16[3,1024,1152]{2,1,0:T(8,128)(2,1)}) custom-call(s32[3]{0:T(128)S(1)} %copy-done.21, f32[1,1152]{1,0:T(1,128)S(1)} %broadcast_in_dim.12.shift_ref, bf16[128,1152]{1,0:T(8,128)(2,1)S(1)} %bitcast.18, bf16[128,1152]{1,0:T(8,128)(2,1)S(1)} %copy.17.up_ref, ...), custom_call_target="tpu_custom_call" | custom-call | flops 9784472576 | bytes 20054016 | tf_op jit(solution)/shard_map/pallas_call | solution.py:764
  252.5 3.1 collective-permute-done.44
  256.5 3.2 collective-permute-start.45
  260.8 18.0 %shard_map.144 = (bf16[4,128,1152]{2,1,0:T(8,128)(2,1)S(1)}, bf16[4,128,1152]{2,1,0:T(8,128)(2,1)S(1)}) custom-call(s32[3]{0:T(128)S(1)} %copy-done.21, f32[1,1152]{1,0:T(1,128)S(1)} %broadcast_in_dim.12.shift_ref, bf16[1024,1152]{1,0:T(8,128)(2,1)} %get-tuple-element.389.rows_ref.rest_1_, bf16[3,1024,1152]{2,1,0:T(8,128)(2,1)} %get-tuple-element.390.primal_ref.rest_2_, ...), custom_call_target="tpu_custom_call" | custom-call | flops 9784472576 | bytes 20054016 | tf_op jit(solution)/shard_map/pallas_call | solution.py:796
  278.8 3.6 collective-permute-done.45.rest_17_
  282.4 1.5 collective-permute-start.49
  285.5 32.8 %shard_map.145.rest_0_ = bf16[1024,1152]{1,0:T(8,128)(2,1)} custom-call(s32[3]{0:T(128)S(1)} %copy-done.21, bf16[2,144,1152]{2,1,0:T(8,128)(2,1)S(1)} %maximum_select_fusion.1.rest_0_.rest_3_, bf16[2,144,1152]{2,1,0:T(8,128)(2,1)S(1)} %copy-done.30, bf16[2,144,1152]{2,1,0:T(8,128)(2,1)S(1)} %copy-done.26, ...), custom_call_target="tpu_custom_call" | custom-call | flops 16307453952 | bytes 20054016 | tf_op jit(solution)/shard_map/pallas_call | solution.py:826
  319.7 1.9 collective-permute-start.52
  323.6 41.1 %shard_map.146 = (bf16[64,1152]{1,0:T(8,128)(2,1)}, bf16[64,1152]{1,0:T(8,128)(2,1)}, bf16[64,1152]{1,0:T(8,128)(2,1)}, bf16[64,1152]{1,0:T(8,128)(2,1)}, bf16[6...) custom-call(s32[3]{0:T(128)} %copy-done.20, ...), custom_call_target="tpu_custom_call" | custom-call | flops 8153726976 | bytes 15335424 | tf_op jit(solution)/shard_map/pallas_call | solution.py:864
  364.6 8.9 %collective-permute-done.54.rest_3_ = bf16[2,128,1152]{2,1,0:T(8,128)(2,1)S(1)} collective-permute-done((bf16[2,128,1152]{2,1,0:T(8,128)(2,1)S(1)}, bf16[2,128,1152]{2,1,0:T(8,128)(2,1)S(1)}, u32[]{:S(2)}, u32[]{:S(2)}) %collective-permute-start.54) | collective-permute-done | bytes 589856 | tf_op jit(solution)/shard_map/ppermute | solution.py:924
  374.2 2.8 collective-permute-start.57
  377.3 2.7 collective-permute-start.59
  381.5 1.4 collective-permute-start.61
  382.9 38.7 %shard_map.148 = (bf16[64,1152]{1,0:T(8,128)(2,1)}, bf16[64,1152]{1,0:T(8,128)(2,1)}, bf16[64,1152]{1,0:T(8,128)(2,1)}, bf16[64,1152]{1,0:T(8,128)(2,1)}, bf16[6...) custom-call(s32[3]{0:T(128)} %copy-done.20, ...), custom_call_target="tpu_custom_call" | custom-call | flops 8153726976 | bytes 15335424 | tf_op jit(solution)/shard_map/pallas_call | solution.py:864
  423.0 2.9 collective-permute-start.63
  425.9 2.6 collective-permute-start.65
  429.7 1.3 collective-permute-start.67
  431.0 4.1 collective-permute-done.63.rest_10_
  435.2 2.1 shard_map.147
  437.4 4.3 collective-permute-done.65.rest_12_
  441.7 3.3 collective-permute-done.66.rest_13_
  445.0 3.7 collective-permute-done.67.rest_14_
  448.7 1.6 collective-permute-done.68.rest_15_
  450.3 2.1 shard_map.149
  (274 shorter events, 46.4 us)
Async XLA Ops:
  1.8 9.6 %collective-permute-start = (bf16[2,72,1152]{2,1,0:T(8,128)(2,1)S(1)}, bf16[2,72,1152]{2,1,0:T(8,128)(2,1)S(1)}, u32[]{:S(2)}, u32[]{:S(2)}) collective-permute-start(bf16[2,72,1152]{2,1,0:T(8,128)(2,1)S(1)} %fusion.1), channel_id=1, source_target_pairs={{0,4},{2,6},{4,0},{6,2},{8,12},{10,14},{12,8},{14,10},{1,5},{3,7},... | collective-permute-start | bytes 995336 | tf_op jit(solution)/shard_map/ppermute | solution.py:924
  11.6 17.7 %collective-permute-start.4 = (bf16[2,144,1152]{2,1,0:T(8,128)(2,1)S(1)}, bf16[2,144,1152]{2,1,0:T(8,128)(2,1)}, u32[]{:S(2)}, u32[]{:S(2)}) collective-permute-start(bf16[2,144,1152]{2,1,0:T(8,128)(2,1)S(1)} %maximum_select_fusion.rest_0_), channel_id=1, source_target_pairs={{4,8},{8,4},{6,10},{10,6},{5,9},{9,5},{7,11},{11,7},{20,24},{24,20... | collective-permute-start | bytes 1990664 | tf_op jit(solution)/shard_map/ppermute | solution.py:948
  15.1 14.3 %collective-permute-start.3 = (bf16[2,144,1152]{2,1,0:T(8,128)(2,1)S(1)}, bf16[2,144,1152]{2,1,0:T(8,128)(2,1)S(1)}, u32[]{:S(2)}, u32[]{:S(2)}) collective-permute-start(bf16[2,144,1152]{2,1,0:T(8,128)(2,1)S(1)} %maximum_select_fusion.rest_0_), channel_id=1, source_target_pairs={{0,1},{1,0},{2,3},{3,2},{4,5},{5,4},{6,7},{7,6},{8,9},{9,8},{10,11... | collective-permute-start | bytes 1990664 | tf_op jit(solution)/shard_map/ppermute | solution.py:924
  15.2 17.4 %collective-permute-start.2 = (bf16[2,144,1152]{2,1,0:T(8,128)(2,1)S(1)}, bf16[2,144,1152]{2,1,0:T(8,128)(2,1)}, u32[]{:S(2)}, u32[]{:S(2)}) collective-permute-start(bf16[2,144,1152]{2,1,0:T(8,128)(2,1)S(1)} %maximum_select_fusion.rest_0_), channel_id=1, source_target_pairs={{0,16},{16,0},{1,17},{17,1},{2,18},{18,2},{3,19},{19,3},{4,20},{20... | collective-permute-start | bytes 1990664 | tf_op jit(solution)/shard_map/ppermute | solution.py:924
  16.7 17.0 %collective-permute-start.1 = (bf16[2,144,1152]{2,1,0:T(8,128)(2,1)S(1)}, bf16[2,144,1152]{2,1,0:T(8,128)(2,1)S(1)}, u32[]{:S(2)}, u32[]{:S(2)}) collective-permute-start(bf16[2,144,1152]{2,1,0:T(8,128)(2,1)S(1)} %maximum_select_fusion.rest_0_), channel_id=1, source_target_pairs={{0,2},{2,0},{4,6},{6,4},{8,10},{10,8},{12,14},{14,12},{1,3},{3,1},... | collective-permute-start | bytes 1990664 | tf_op jit(solution)/shard_map/ppermute | solution.py:924
  18.2 9.6 %collective-permute-start.5 = (bf16[2,72,1152]{2,1,0:T(8,128)(2,1)S(1)}, bf16[2,72,1152]{2,1,0:T(8,128)(2,1)S(1)}, u32[]{:S(2)}, u32[]{:S(2)}) collective-permute-start(bf16[2,72,1152]{2,1,0:T(8,128)(2,1)S(1)} %fusion), channel_id=1, source_target_pairs={{0,4},{2,6},{4,0},{6,2},{8,12},{10,14},{12,8},{14,10},{1,5},{3,7},... | collective-permute-start | bytes 995336 | tf_op jit(solution)/shard_map/ppermute | solution.py:924
  33.7 8.7 %collective-permute-start.8 = (bf16[2,144,1152]{2,1,0:T(8,128)(2,1)S(1)}, bf16[2,144,1152]{2,1,0:T(8,128)(2,1)S(1)}, u32[]{:S(2)}, u32[]{:S(2)}) collective-permute-start(bf16[2,144,1152]{2,1,0:T(8,128)(2,1)S(1)} %collective-permute-done.1.rest_1_), channel_id=1, source_target_pairs={{0,1},{1,0},{2,3},{3,2},{4,5},{5,4},{6,7},{7,6},{8,9},{9,8},{10,11... | collective-permute-start | bytes 1990664 | tf_op jit(solution)/shard_map/ppermute | solution.py:924
  34.5 18.8 %collective-permute-start.7 = (bf16[2,144,1152]{2,1,0:T(8,128)(2,1)}, bf16[2,144,1152]{2,1,0:T(8,128)(2,1)}, u32[]{:S(2)}, u32[]{:S(2)}) collective-permute-start(bf16[2,144,1152]{2,1,0:T(8,128)(2,1)} %collective-permute-done.4), channel_id=1, source_target_pairs={{4,0},{8,12},{6,2},{10,14},{5,1},{9,13},{7,3},{11,15},{20,16},{24,... | collective-permute-start | bytes 1990664 | tf_op jit(solution)/shard_map/ppermute | solution.py:958
  36.7 21.0 %collective-permute-start.11 = (bf16[2,144,1152]{2,1,0:T(8,128)(2,1)S(1)}, bf16[2,144,1152]{2,1,0:T(8,128)(2,1)S(1)}, u32[]{:S(2)}, u32[]{:S(2)}) collective-permute-start(bf16[2,144,1152]{2,1,0:T(8,128)(2,1)S(1)} %maximum_select_fusion.1.rest_0_.rest_3_), channel_id=1, source_target_pairs={{0,16},{16,0},{1,17},{17,1},{2,18},{18,2},{3,19},{19,3},{4,20},{20... | collective-permute-start | bytes 1990664 | tf_op jit(solution)/shard_map/ppermute | solution.py:924
  37.2 20.5 %collective-permute-start.10 = (bf16[2,144,1152]{2,1,0:T(8,128)(2,1)S(1)}, bf16[2,144,1152]{2,1,0:T(8,128)(2,1)}, u32[]{:S(2)}, u32[]{:S(2)}) collective-permute-start(bf16[2,144,1152]{2,1,0:T(8,128)(2,1)S(1)} %maximum_select_fusion.1.rest_0_.rest_3_), channel_id=1, source_target_pairs={{4,8},{8,4},{6,10},{10,6},{5,9},{9,5},{7,11},{11,7},{20,24},{24,20... | collective-permute-start | bytes 1990664 | tf_op jit(solution)/shard_map/ppermute | solution.py:948
  40.9 16.9 %collective-permute-start.6 = (bf16[2,144,1152]{2,1,0:T(8,128)(2,1)}, bf16[2,144,1152]{2,1,0:T(8,128)(2,1)}, u32[]{:S(2)}, u32[]{:S(2)}) collective-permute-start(bf16[2,144,1152]{2,1,0:T(8,128)(2,1)} %collective-permute-done.2.rest_2_), channel_id=1, source_target_pairs={{0,2},{2,0},{4,6},{6,4},{8,10},{10,8},{12,14},{14,12},{1,3},{3,1},... | collective-permute-start | bytes 1990664 | tf_op jit(solution)/shard_map/ppermute | solution.py:924
  43.3 14.5 %collective-permute-start.9 = (bf16[2,144,1152]{2,1,0:T(8,128)(2,1)}, bf16[2,144,1152]{2,1,0:T(8,128)(2,1)}, u32[]{:S(2)}, u32[]{:S(2)}) collective-permute-start(bf16[2,144,1152]{2,1,0:T(8,128)(2,1)} %collective-permute-done.2.rest_2_), channel_id=1, source_target_pairs={{0,1},{1,0},{2,3},{3,2},{4,5},{5,4},{6,7},{7,6},{8,9},{9,8},{10,11... | collective-permute-start | bytes 1990664 | tf_op jit(solution)/shard_map/ppermute | solution.py:924
  57.7 4.5 collective-permute-start.14
  57.8 16.7 %collective-permute-start.16 = (bf16[2,144,1152]{2,1,0:T(8,128)(2,1)}, bf16[2,144,1152]{2,1,0:T(8,128)(2,1)S(1)}, u32[]{:S(2)}, u32[]{:S(2)}) collective-permute-start(bf16[2,144,1152]{2,1,0:T(8,128)(2,1)} %collective-permute-done.10), channel_id=1, source_target_pairs={{4,0},{8,12},{6,2},{10,14},{5,1},{9,13},{7,3},{11,15},{20,16},{24,... | collective-permute-start | bytes 1990664 | tf_op jit(solution)/shard_map/ppermute | solution.py:958
  59.2 17.4 %collective-permute-start.13 = (bf16[2,144,1152]{2,1,0:T(8,128)(2,1)S(1)}, bf16[2,144,1152]{2,1,0:T(8,128)(2,1)S(1)}, u32[]{:S(2)}, u32[]{:S(2)}) collective-permute-start(bf16[2,144,1152]{2,1,0:T(8,128)(2,1)S(1)} %broadcast_select_fusion.1.rest_4_), channel_id=1, source_target_pairs={{0,16},{16,0},{1,17},{17,1},{2,18},{18,2},{3,19},{19,3},{4,20},{20... | collective-permute-start | bytes 1990664 | tf_op jit(solution)/shard_map/ppermute | solution.py:924
  60.7 17.0 %collective-permute-start.12 = (bf16[2,144,1152]{2,1,0:T(8,128)(2,1)S(1)}, bf16[2,144,1152]{2,1,0:T(8,128)(2,1)S(1)}, u32[]{:S(2)}, u32[]{:S(2)}) collective-permute-start(bf16[2,144,1152]{2,1,0:T(8,128)(2,1)S(1)} %broadcast_select_fusion.1.rest_4_), channel_id=1, source_target_pairs={{0,2},{2,0},{4,6},{6,4},{8,10},{10,8},{12,14},{14,12},{1,3},{3,1},... | collective-permute-start | bytes 1990664 | tf_op jit(solution)/shard_map/ppermute | solution.py:924
  62.2 15.5 %collective-permute-start.15 = (bf16[2,144,1152]{2,1,0:T(8,128)(2,1)S(1)}, bf16[2,144,1152]{2,1,0:T(8,128)(2,1)S(1)}, u32[]{:S(2)}, u32[]{:S(2)}) collective-permute-start(bf16[2,144,1152]{2,1,0:T(8,128)(2,1)S(1)} %maximum_select_fusion.1.rest_0_.rest_3_), channel_id=1, source_target_pairs={{0,1},{1,0},{2,3},{3,2},{4,5},{5,4},{6,7},{7,6},{8,9},{9,8},{10,11... | collective-permute-start | bytes 1990664 | tf_op jit(solution)/shard_map/ppermute | solution.py:924
  82.2 17.9 %collective-permute-start.17 = (bf16[2,144,1152]{2,1,0:T(8,128)(2,1)S(1)}, bf16[2,144,1152]{2,1,0:T(8,128)(2,1)S(1)}, u32[]{:S(2)}, u32[]{:S(2)}) collective-permute-start(bf16[2,144,1152]{2,1,0:T(8,128)(2,1)S(1)} %collective-permute-done.12.rest_5_), channel_id=1, source_target_pairs={{0,16},{16,0},{1,17},{17,1},{2,18},{18,2},{3,19},{19,3},{4,20},{20... | collective-permute-start | bytes 1990664 | tf_op jit(solution)/shard_map/ppermute | solution.py:924
  82.7 17.4 %collective-permute-start.21 = (bf16[2,144,1152]{2,1,0:T(8,128)(2,1)S(1)}, bf16[2,144,1152]{2,1,0:T(8,128)(2,1)S(1)}, u32[]{:S(2)}, u32[]{:S(2)}) collective-permute-start(bf16[2,144,1152]{2,1,0:T(8,128)(2,1)S(1)} %maximum_select_fusion.1.rest_0_.rest_3_), channel_id=1, source_target_pairs={{0,2},{2,0},{4,6},{6,4},{8,10},{10,8},{12,14},{14,12},{1,3},{3,1},... | collective-permute-start | bytes 1990664 | tf_op jit(solution)/shard_map/ppermute | solution.py:924
  84.2 15.8 %collective-permute-start.22 = (bf16[2,144,1152]{2,1,0:T(8,128)(2,1)S(1)}, bf16[2,144,1152]{2,1,0:T(8,128)(2,1)S(1)}, u32[]{:S(2)}, u32[]{:S(2)}) collective-permute-start(bf16[2,144,1152]{2,1,0:T(8,128)(2,1)S(1)} %copy-done.25), channel_id=1, source_target_pairs={{0,1},{1,0},{2,3},{3,2},{4,5},{5,4},{6,7},{7,6},{8,9},{9,8},{10,11... | collective-permute-start | bytes 1990664 | tf_op jit(solution)/shard_map/ppermute | solution.py:924
  84.3 15.7 %collective-permute-start.23 = (bf16[2,8,16,1152]{3,2,1,0:T(8,128)(2,1)S(1)}, bf16[2,8,16,1152]{3,2,1,0:T(8,128)(2,1)S(1)}, u32[]{:S(2)}, u32[]{:S(2)}) collective-permute-start(bf16[2,8,16,1152]{3,2,1,0:T(8,128)(2,1)S(1)} %get-tuple-element.286), channel_id=1, source_target_pairs={{0,4},{2,6},{4,0},{6,2},{8,12},{10,14},{12,8},{14,10},{1,5},{3,7},... | collective-permute-start | bytes 1769480 | tf_op jit(solution)/shard_map/ppermute | solution.py:924
  100.7 3.5 collective-permute-start.25
  104.2 54.4 %collective-permute-start.29 = (bf16[2,144,1152]{2,1,0:T(8,128)(2,1)S(1)}, bf16[2,144,1152]{2,1,0:T(8,128)(2,1)}, u32[]{:S(2)}, u32[]{:S(2)}) collective-permute-start(bf16[2,144,1152]{2,1,0:T(8,128)(2,1)S(1)} %broadcast_select_fusion.rest_4_.rest_7_), channel_id=1, source_target_pairs={{0,2},{2,0},{4,6},{6,4},{8,10},{10,8},{12,14},{14,12},{1,3},{3,1},... | collective-permute-start | bytes 1990664 | tf_op jit(solution)/shard_map/ppermute | solution.py:924
  105.5 53.1 %collective-permute-start.28 = (bf16[2,144,1152]{2,1,0:T(8,128)(2,1)S(1)}, bf16[2,144,1152]{2,1,0:T(8,128)(2,1)}, u32[]{:S(2)}, u32[]{:S(2)}) collective-permute-start(bf16[2,144,1152]{2,1,0:T(8,128)(2,1)S(1)} %broadcast_select_fusion.rest_4_.rest_7_), channel_id=1, source_target_pairs={{0,16},{16,0},{1,17},{17,1},{2,18},{18,2},{3,19},{19,3},{4,20},{20... | collective-permute-start | bytes 1990664 | tf_op jit(solution)/shard_map/ppermute | solution.py:924
  106.7 39.0 %collective-permute-start.30 = (bf16[2,8,16,1152]{3,2,1,0:T(8,128)(2,1)S(1)}, bf16[2,8,16,1152]{3,2,1,0:T(8,128)(2,1)S(1)}, u32[]{:S(2)}, u32[]{:S(2)}) collective-permute-start(bf16[2,8,16,1152]{3,2,1,0:T(8,128)(2,1)S(1)} %get-tuple-element.340), channel_id=1, source_target_pairs={{0,8},{2,10},{4,12},{6,14},{8,0},{10,2},{12,4},{14,6},{1,9},{3,11}... | collective-permute-start | bytes 1769480 | tf_op jit(solution)/shard_map/ppermute | solution.py:924
  106.7 51.9 %collective-permute-start.31 = (bf16[2,8,16,1152]{3,2,1,0:T(8,128)(2,1)S(1)}, bf16[2,8,16,1152]{3,2,1,0:T(8,128)(2,1)S(1)}, u32[]{:S(2)}, u32[]{:S(2)}) collective-permute-start(bf16[2,8,16,1152]{3,2,1,0:T(8,128)(2,1)S(1)} %get-tuple-element.341), channel_id=1, source_target_pairs={{0,12},{2,14},{4,8},{6,10},{8,4},{10,6},{12,0},{14,2},{1,13},{3,15... | collective-permute-start | bytes 1769480 | tf_op jit(solution)/shard_map/ppermute | solution.py:924
  107.9 50.7 %collective-permute-start.27 = (bf16[2,144,1152]{2,1,0:T(8,128)(2,1)S(1)}, bf16[2,144,1152]{2,1,0:T(8,128)(2,1)}, u32[]{:S(2)}, u32[]{:S(2)}) collective-permute-start(bf16[2,144,1152]{2,1,0:T(8,128)(2,1)S(1)} %collective-permute-done.21.rest_1_.rest_4_), channel_id=1, source_target_pairs={{0,16},{16,0},{1,17},{17,1},{2,18},{18,2},{3,19},{19,3},{4,20},{20... | collective-permute-start | bytes 1990664 | tf_op jit(solution)/shard_map/ppermute | solution.py:924
  158.6 5.5 %collective-permute-start.33 = (bf16[2,144,1152]{2,1,0:T(8,128)(2,1)}, bf16[2,144,1152]{2,1,0:T(8,128)(2,1)S(1)}, u32[]{:S(2)}, u32[]{:S(2)}) collective-permute-start(bf16[2,144,1152]{2,1,0:T(8,128)(2,1)} %collective-permute-done.29.rest_5_.rest_8_), channel_id=1, source_target_pairs={{0,1},{1,0},{2,3},{3,2},{4,5},{5,4},{6,7},{7,6},{8,9},{9,8},{10,11... | collective-permute-start | bytes 1990664 | tf_op jit(solution)/shard_map/ppermute | solution.py:924
  158.7 6.3 %collective-permute-start.32 = (bf16[2,144,1152]{2,1,0:T(8,128)(2,1)}, bf16[2,144,1152]{2,1,0:T(8,128)(2,1)}, u32[]{:S(2)}, u32[]{:S(2)}) collective-permute-start(bf16[2,144,1152]{2,1,0:T(8,128)(2,1)} %collective-permute-done.27.rest_3_.rest_6_), channel_id=1, source_target_pairs={{0,1},{1,0},{2,3},{3,2},{4,5},{5,4},{6,7},{7,6},{8,9},{9,8},{10,11... | collective-permute-start | bytes 1990664 | tf_op jit(solution)/shard_map/ppermute | solution.py:924
  159.2 5.8 %collective-permute-start.34 = (bf16[2,144,1152]{2,1,0:T(8,128)(2,1)}, bf16[2,144,1152]{2,1,0:T(8,128)(2,1)}, u32[]{:S(2)}, u32[]{:S(2)}) collective-permute-start(bf16[2,144,1152]{2,1,0:T(8,128)(2,1)} %collective-permute-done.28.rest_6_.rest_9_), channel_id=1, source_target_pairs={{0,1},{1,0},{2,3},{3,2},{4,5},{5,4},{6,7},{7,6},{8,9},{9,8},{10,11... | collective-permute-start | bytes 1990664 | tf_op jit(solution)/shard_map/ppermute | solution.py:924
  165.0 35.7 %collective-permute-start.35 = (bf16[4,4,16,1152]{3,2,1,0:T(8,128)(2,1)}, bf16[4,4,16,1152]{3,2,1,0:T(8,128)(2,1)}, u32[]{:S(2)}, u32[]{:S(2)}) collective-permute-start(bf16[4,4,16,1152]{3,2,1,0:T(8,128)(2,1)} %get-tuple-element.355), channel_id=1, source_target_pairs={{0,2},{2,0},{4,6},{6,4},{8,10},{10,8},{12,14},{14,12},{1,3},{3,1},... | collective-permute-start | bytes 1769480 | tf_op jit(solution)/shard_map/ppermute | solution.py:924
  166.6 34.2 %collective-permute-start.36 = (bf16[4,4,16,1152]{3,2,1,0:T(8,128)(2,1)}, bf16[4,4,16,1152]{3,2,1,0:T(8,128)(2,1)}, u32[]{:S(2)}, u32[]{:S(2)}) collective-permute-start(bf16[4,4,16,1152]{3,2,1,0:T(8,128)(2,1)} %get-tuple-element.356), channel_id=1, source_target_pairs={{0,16},{16,0},{1,17},{17,1},{2,18},{18,2},{3,19},{19,3},{4,20},{20... | collective-permute-start | bytes 1769480 | tf_op jit(solution)/shard_map/ppermute | solution.py:924
  167.1 33.6 %collective-permute-start.37 = (bf16[4,4,16,1152]{3,2,1,0:T(8,128)(2,1)}, bf16[4,4,16,1152]{3,2,1,0:T(8,128)(2,1)}, u32[]{:S(2)}, u32[]{:S(2)}) collective-permute-start(bf16[4,4,16,1152]{3,2,1,0:T(8,128)(2,1)} %get-tuple-element.357), channel_id=1, source_target_pairs={{0,18},{2,16},{4,22},{6,20},{8,26},{10,24},{12,30},{14,28},{16,2},... | collective-permute-start | bytes 1769480 | tf_op jit(solution)/shard_map/ppermute | solution.py:998
  168.5 37.7 %collective-permute-start.39 = (bf16[2,8,16,1152]{3,2,1,0:T(8,128)(2,1)}, bf16[2,8,16,1152]{3,2,1,0:T(8,128)(2,1)S(1)}, u32[]{:S(2)}, u32[]{:S(2)}) collective-permute-start(bf16[2,8,16,1152]{3,2,1,0:T(8,128)(2,1)} %get-tuple-element.362), channel_id=1, source_target_pairs={{0,2},{2,0},{4,6},{6,4},{8,10},{10,8},{12,14},{14,12},{1,3},{3,1},... | collective-permute-start | bytes 1769480 | tf_op jit(solution)/shard_map/ppermute | solution.py:924
  170.1 39.0 %collective-permute-start.38 = (bf16[2,144,1152]{2,1,0:T(8,128)(2,1)}, bf16[2,144,1152]{2,1,0:T(8,128)(2,1)S(1)}, u32[]{:S(2)}, u32[]{:S(2)}) collective-permute-start(bf16[2,144,1152]{2,1,0:T(8,128)(2,1)} %collective-permute-done.29.rest_5_.rest_8_), channel_id=1, source_target_pairs={{0,16},{16,0},{1,17},{17,1},{2,18},{18,2},{3,19},{19,3},{4,20},{20... | collective-permute-start | bytes 1990664 | tf_op jit(solution)/shard_map/ppermute | solution.py:924
  213.3 65.4 %collective-permute-start.46 = (bf16[4,4,16,1152]{3,2,1,0:T(8,128)(2,1)S(1)}, bf16[4,4,16,1152]{3,2,1,0:T(8,128)(2,1)S(1)}, u32[]{:S(2)}, u32[]{:S(2)}) collective-permute-start(bf16[4,4,16,1152]{3,2,1,0:T(8,128)(2,1)S(1)} %pad_maximum_fusion.4), channel_id=1, source_target_pairs={{0,8},{2,10},{4,12},{6,14},{8,0},{10,2},{12,4},{14,6},{1,9},{3,11}... | collective-permute-start | bytes 1769480 | tf_op jit(solution)/shard_map/ppermute | solution.py:924
  213.4 14.6 %collective-permute-start.41 = (bf16[2,8,16,1152]{3,2,1,0:T(8,128)(2,1)S(1)}, bf16[2,8,16,1152]{3,2,1,0:T(8,128)(2,1)S(1)}, u32[]{:S(2)}, u32[]{:S(2)}) collective-permute-start(bf16[2,8,16,1152]{3,2,1,0:T(8,128)(2,1)S(1)} %copy-done.60), channel_id=1, source_target_pairs={{0,2},{2,0},{4,6},{6,4},{8,10},{10,8},{12,14},{14,12},{1,3},{3,1},... | collective-permute-start | bytes 1769480 | tf_op jit(solution)/shard_map/ppermute | solution.py:924
  214.0 14.1 %collective-permute-start.40 = (bf16[2,144,1152]{2,1,0:T(8,128)(2,1)S(1)}, bf16[2,144,1152]{2,1,0:T(8,128)(2,1)S(1)}, u32[]{:S(2)}, u32[]{:S(2)}) collective-permute-start(bf16[2,144,1152]{2,1,0:T(8,128)(2,1)S(1)} %collective-permute-done.38.rest_7_.rest_10_), channel_id=1, source_target_pairs={{0,1},{1,0},{2,3},{3,2},{4,5},{5,4},{6,7},{7,6},{8,9},{9,8},{10,11... | collective-permute-start | bytes 1990664 | tf_op jit(solution)/shard_map/ppermute | solution.py:924
  214.9 63.8 %collective-permute-start.47 = (bf16[4,4,16,1152]{3,2,1,0:T(8,128)(2,1)}, bf16[4,4,16,1152]{3,2,1,0:T(8,128)(2,1)S(1)}, u32[]{:S(2)}, u32[]{:S(2)}) collective-permute-start(bf16[4,4,16,1152]{3,2,1,0:T(8,128)(2,1)} %pad_maximum_fusion.5), channel_id=1, source_target_pairs={{0,12},{2,14},{4,8},{6,10},{8,4},{10,6},{12,0},{14,2},{1,13},{3,15... | collective-permute-start | bytes 1769480 | tf_op jit(solution)/shard_map/ppermute | solution.py:924
  228.1 24.4 %collective-permute-start.42 = (bf16[4,4,16,1152]{3,2,1,0:T(8,128)(2,1)}, bf16[4,4,16,1152]{3,2,1,0:T(8,128)(2,1)S(1)}, u32[]{:S(2)}, u32[]{:S(2)}) collective-permute-start(bf16[4,4,16,1152]{3,2,1,0:T(8,128)(2,1)} %get-tuple-element.382), channel_id=1, source_target_pairs={{0,2},{2,0},{4,6},{6,4},{8,10},{10,8},{12,14},{14,12},{1,3},{3,1},... | collective-permute-start | bytes 1769480 | tf_op jit(solution)/shard_map/ppermute | solution.py:924
  228.6 23.9 %collective-permute-start.43 = (bf16[4,4,16,1152]{3,2,1,0:T(8,128)(2,1)S(1)}, bf16[4,4,16,1152]{3,2,1,0:T(8,128)(2,1)S(1)}, u32[]{:S(2)}, u32[]{:S(2)}) collective-permute-start(bf16[4,4,16,1152]{3,2,1,0:T(8,128)(2,1)S(1)} %copy-done.67), channel_id=1, source_target_pairs={{0,16},{16,0},{1,17},{17,1},{2,18},{18,2},{3,19},{19,3},{4,20},{20... | collective-permute-start | bytes 1769480 | tf_op jit(solution)/shard_map/ppermute | solution.py:924
  230.0 25.6 %collective-permute-start.44 = (bf16[4,4,16,1152]{3,2,1,0:T(8,128)(2,1)S(1)}, bf16[4,4,16,1152]{3,2,1,0:T(8,128)(2,1)S(1)}, u32[]{:S(2)}, u32[]{:S(2)}) collective-permute-start(bf16[4,4,16,1152]{3,2,1,0:T(8,128)(2,1)S(1)} %copy-done.66), channel_id=1, source_target_pairs={{0,18},{2,16},{4,22},{6,20},{8,26},{10,24},{12,30},{14,28},{16,2},... | collective-permute-start | bytes 1769480 | tf_op jit(solution)/shard_map/ppermute | solution.py:998
  255.8 62.7 %collective-permute-start.51 = (bf16[4,4,16,1152]{3,2,1,0:T(8,128)(2,1)S(1)}, bf16[4,4,16,1152]{3,2,1,0:T(8,128)(2,1)S(1)}, u32[]{:S(2)}, u32[]{:S(2)}) collective-permute-start(bf16[4,4,16,1152]{3,2,1,0:T(8,128)(2,1)S(1)} %pad_maximum_fusion.9), channel_id=1, source_target_pairs={{0,12},{2,14},{4,8},{6,10},{8,4},{10,6},{12,0},{14,2},{1,13},{3,15... | collective-permute-start | bytes 1769480 | tf_op jit(solution)/shard_map/ppermute | solution.py:924
  256.5 26.0 %collective-permute-start.45 = (bf16[4,4,16,1152]{3,2,1,0:T(8,128)(2,1)}, bf16[4,4,16,1152]{3,2,1,0:T(8,128)(2,1)S(1)}, u32[]{:S(2)}, u32[]{:S(2)}) collective-permute-start(bf16[4,4,16,1152]{3,2,1,0:T(8,128)(2,1)} %pad_maximum_fusion.3), channel_id=1, source_target_pairs={{0,4},{2,6},{4,0},{6,2},{8,12},{10,14},{12,8},{14,10},{1,5},{3,7},... | collective-permute-start | bytes 1769480 | tf_op jit(solution)/shard_map/ppermute | solution.py:924
  282.4 36.1 %collective-permute-start.49 = (bf16[4,4,16,1152]{3,2,1,0:T(8,128)(2,1)S(1)}, bf16[4,4,16,1152]{3,2,1,0:T(8,128)(2,1)S(1)}, u32[]{:S(2)}, u32[]{:S(2)}) collective-permute-start(bf16[4,4,16,1152]{3,2,1,0:T(8,128)(2,1)S(1)} %pad_maximum_fusion.7), channel_id=1, source_target_pairs={{0,4},{2,6},{4,0},{6,2},{8,12},{10,14},{12,8},{14,10},{1,5},{3,7},... | collective-permute-start | bytes 1769480 | tf_op jit(solution)/shard_map/ppermute | solution.py:924
  284.0 34.5 %collective-permute-start.50 = (bf16[4,4,16,1152]{3,2,1,0:T(8,128)(2,1)S(1)}, bf16[4,4,16,1152]{3,2,1,0:T(8,128)(2,1)S(1)}, u32[]{:S(2)}, u32[]{:S(2)}) collective-permute-start(bf16[4,4,16,1152]{3,2,1,0:T(8,128)(2,1)S(1)} %pad_maximum_fusion.8), channel_id=1, source_target_pairs={{0,8},{2,10},{4,12},{6,14},{8,0},{10,2},{12,4},{14,6},{1,9},{3,11}... | collective-permute-start | bytes 1769480 | tf_op jit(solution)/shard_map/ppermute | solution.py:924
  284.5 34.0 %collective-permute-start.48 = (bf16[4,128,1152]{2,1,0:T(8,128)(2,1)S(1)}, bf16[4,128,1152]{2,1,0:T(8,128)(2,1)S(1)}, u32[]{:S(2)}, u32[]{:S(2)}) collective-permute-start(bf16[4,128,1152]{2,1,0:T(8,128)(2,1)S(1)} %get-tuple-element.400), channel_id=1, source_target_pairs={{0,2},{2,0},{4,6},{6,4},{8,10},{10,8},{12,14},{14,12},{1,3},{3,1},... | collective-permute-start | bytes 3538952 | tf_op jit(solution)/shard_map/ppermute | solution.py:924
  319.7 44.9 %collective-permute-start.52 = (bf16[2,128,1152]{2,1,0:T(8,128)(2,1)S(1)}, bf16[2,128,1152]{2,1,0:T(8,128)(2,1)S(1)}, u32[]{:S(2)}, u32[]{:S(2)}) collective-permute-start(bf16[2,128,1152]{2,1,0:T(8,128)(2,1)S(1)} %pad_maximum_fusion.11), channel_id=1, source_target_pairs={{0,4},{2,6},{4,0},{6,2},{8,12},{10,14},{12,8},{14,10},{1,5},{3,7},... | collective-permute-start | bytes 1769480 | tf_op jit(solution)/shard_map/ppermute | solution.py:924
  321.7 43.0 %collective-permute-start.53 = (bf16[2,128,1152]{2,1,0:T(8,128)(2,1)S(1)}, bf16[2,128,1152]{2,1,0:T(8,128)(2,1)S(1)}, u32[]{:S(2)}, u32[]{:S(2)}) collective-permute-start(bf16[2,128,1152]{2,1,0:T(8,128)(2,1)S(1)} %pad_maximum_fusion.12), channel_id=1, source_target_pairs={{0,8},{2,10},{4,12},{6,14},{8,0},{10,2},{12,4},{14,6},{1,9},{3,11}... | collective-permute-start | bytes 1769480 | tf_op jit(solution)/shard_map/ppermute | solution.py:924
  322.4 51.2 %collective-permute-start.54 = (bf16[2,128,1152]{2,1,0:T(8,128)(2,1)S(1)}, bf16[2,128,1152]{2,1,0:T(8,128)(2,1)S(1)}, u32[]{:S(2)}, u32[]{:S(2)}) collective-permute-start(bf16[2,128,1152]{2,1,0:T(8,128)(2,1)S(1)} %pad_maximum_fusion.13), channel_id=1, source_target_pairs={{0,12},{2,14},{4,8},{6,10},{8,4},{10,6},{12,0},{14,2},{1,13},{3,15... | collective-permute-start | bytes 1769480 | tf_op jit(solution)/shard_map/ppermute | solution.py:924
  373.6 6.9 %collective-permute-start.55 = (bf16[64,1152]{1,0:T(8,128)(2,1)}, bf16[64,1152]{1,0:T(8,128)(2,1)S(1)}, u32[]{:S(2)}, u32[]{:S(2)}) collective-permute-start(bf16[64,1152]{1,0:T(8,128)(2,1)} %get-tuple-element.437), channel_id=1, source_target_pairs={{0,2},{2,0},{4,6},{6,4},{8,10},{10,8},{12,14},{14,12},{1,3},{3,1},... | collective-permute-start | bytes 442376 | tf_op jit(solution)/shard_map/ppermute | solution.py:924
  374.2 7.3 %collective-permute-start.56 = (bf16[64,1152]{1,0:T(8,128)(2,1)}, bf16[64,1152]{1,0:T(8,128)(2,1)S(1)}, u32[]{:S(2)}, u32[]{:S(2)}) collective-permute-start(bf16[64,1152]{1,0:T(8,128)(2,1)} %get-tuple-element.438), channel_id=1, source_target_pairs={{0,4},{2,6},{4,0},{6,2},{8,12},{10,14},{12,8},{14,10},{1,5},{3,7},... | collective-permute-start | bytes 442376 | tf_op jit(solution)/shard_map/ppermute | solution.py:924
  374.2 47.4 %collective-permute-start.57 = (bf16[64,1152]{1,0:T(8,128)(2,1)}, bf16[64,1152]{1,0:T(8,128)(2,1)S(1)}, u32[]{:S(2)}, u32[]{:S(2)}) collective-permute-start(bf16[64,1152]{1,0:T(8,128)(2,1)} %get-tuple-element.439), channel_id=1, source_target_pairs={{0,6},{2,4},{4,2},{6,0},{8,14},{10,12},{12,10},{14,8},{1,7},{3,5},... | collective-permute-start | bytes 442376 | tf_op jit(solution)/shard_map/ppermute | solution.py:924
  377.0 44.6 %collective-permute-start.58 = (bf16[64,1152]{1,0:T(8,128)(2,1)}, bf16[64,1152]{1,0:T(8,128)(2,1)S(1)}, u32[]{:S(2)}, u32[]{:S(2)}) collective-permute-start(bf16[64,1152]{1,0:T(8,128)(2,1)} %get-tuple-element.440), channel_id=1, source_target_pairs={{0,8},{2,10},{4,12},{6,14},{8,0},{10,2},{12,4},{14,6},{1,9},{3,11}... | collective-permute-start | bytes 442376 | tf_op jit(solution)/shard_map/ppermute | solution.py:924
  377.3 44.3 %collective-permute-start.59 = (bf16[64,1152]{1,0:T(8,128)(2,1)}, bf16[64,1152]{1,0:T(8,128)(2,1)S(1)}, u32[]{:S(2)}, u32[]{:S(2)}) collective-permute-start(bf16[64,1152]{1,0:T(8,128)(2,1)} %get-tuple-element.441), channel_id=1, source_target_pairs={{0,10},{2,8},{4,14},{6,12},{8,2},{10,0},{12,6},{14,4},{1,11},{3,9}... | collective-permute-start | bytes 442376 | tf_op jit(solution)/shard_map/ppermute | solution.py:924
  380.4 41.2 %collective-permute-start.60 = (bf16[64,1152]{1,0:T(8,128)(2,1)}, bf16[64,1152]{1,0:T(8,128)(2,1)S(1)}, u32[]{:S(2)}, u32[]{:S(2)}) collective-permute-start(bf16[64,1152]{1,0:T(8,128)(2,1)} %get-tuple-element.442), channel_id=1, source_target_pairs={{0,12},{2,14},{4,8},{6,10},{8,4},{10,6},{12,0},{14,2},{1,13},{3,15... | collective-permute-start | bytes 442376 | tf_op jit(solution)/shard_map/ppermute | solution.py:924
  381.5 40.1 %collective-permute-start.61 = (bf16[64,1152]{1,0:T(8,128)(2,1)}, bf16[64,1152]{1,0:T(8,128)(2,1)S(1)}, u32[]{:S(2)}, u32[]{:S(2)}) collective-permute-start(bf16[64,1152]{1,0:T(8,128)(2,1)} %get-tuple-element.443), channel_id=1, source_target_pairs={{0,14},{2,12},{4,10},{6,8},{8,6},{10,4},{12,2},{14,0},{1,15},{3,13... | collective-permute-start | bytes 442376 | tf_op jit(solution)/shard_map/ppermute | solution.py:924
  421.7 8.0 %collective-permute-start.62 = (bf16[64,1152]{1,0:T(8,128)(2,1)}, bf16[64,1152]{1,0:T(8,128)(2,1)S(1)}, u32[]{:S(2)}, u32[]{:S(2)}) collective-permute-start(bf16[64,1152]{1,0:T(8,128)(2,1)} %get-tuple-element.453), channel_id=1, source_target_pairs={{0,2},{2,0},{4,6},{6,4},{8,10},{10,8},{12,14},{14,12},{1,3},{3,1},... | collective-permute-start | bytes 442376 | tf_op jit(solution)/shard_map/ppermute | solution.py:924
  423.0 12.1 %collective-permute-start.63 = (bf16[64,1152]{1,0:T(8,128)(2,1)}, bf16[64,1152]{1,0:T(8,128)(2,1)S(1)}, u32[]{:S(2)}, u32[]{:S(2)}) collective-permute-start(bf16[64,1152]{1,0:T(8,128)(2,1)} %get-tuple-element.454), channel_id=1, source_target_pairs={{0,4},{2,6},{4,0},{6,2},{8,12},{10,14},{12,8},{14,10},{1,5},{3,7},... | collective-permute-start | bytes 442376 | tf_op jit(solution)/shard_map/ppermute | solution.py:924
  425.8 11.5 %collective-permute-start.64 = (bf16[64,1152]{1,0:T(8,128)(2,1)}, bf16[64,1152]{1,0:T(8,128)(2,1)S(1)}, u32[]{:S(2)}, u32[]{:S(2)}) collective-permute-start(bf16[64,1152]{1,0:T(8,128)(2,1)} %get-tuple-element.455), channel_id=1, source_target_pairs={{0,6},{2,4},{4,2},{6,0},{8,14},{10,12},{12,10},{14,8},{1,7},{3,5},... | collective-permute-start | bytes 442376 | tf_op jit(solution)/shard_map/ppermute | solution.py:924
  425.9 15.8 %collective-permute-start.65 = (bf16[64,1152]{1,0:T(8,128)(2,1)}, bf16[64,1152]{1,0:T(8,128)(2,1)S(1)}, u32[]{:S(2)}, u32[]{:S(2)}) collective-permute-start(bf16[64,1152]{1,0:T(8,128)(2,1)} %get-tuple-element.456), channel_id=1, source_target_pairs={{0,8},{2,10},{4,12},{6,14},{8,0},{10,2},{12,4},{14,6},{1,9},{3,11}... | collective-permute-start | bytes 442376 | tf_op jit(solution)/shard_map/ppermute | solution.py:924
  428.4 16.6 %collective-permute-start.66 = (bf16[64,1152]{1,0:T(8,128)(2,1)}, bf16[64,1152]{1,0:T(8,128)(2,1)S(1)}, u32[]{:S(2)}, u32[]{:S(2)}) collective-permute-start(bf16[64,1152]{1,0:T(8,128)(2,1)} %get-tuple-element.457), channel_id=1, source_target_pairs={{0,10},{2,8},{4,14},{6,12},{8,2},{10,0},{12,6},{14,4},{1,11},{3,9}... | collective-permute-start | bytes 442376 | tf_op jit(solution)/shard_map/ppermute | solution.py:924
  429.7 19.0 %collective-permute-start.67 = (bf16[64,1152]{1,0:T(8,128)(2,1)}, bf16[64,1152]{1,0:T(8,128)(2,1)S(1)}, u32[]{:S(2)}, u32[]{:S(2)}) collective-permute-start(bf16[64,1152]{1,0:T(8,128)(2,1)} %get-tuple-element.458), channel_id=1, source_target_pairs={{0,12},{2,14},{4,8},{6,10},{8,4},{10,6},{12,0},{14,2},{1,13},{3,15... | collective-permute-start | bytes 442376 | tf_op jit(solution)/shard_map/ppermute | solution.py:924
  435.0 15.2 %collective-permute-start.68 = (bf16[64,1152]{1,0:T(8,128)(2,1)}, bf16[64,1152]{1,0:T(8,128)(2,1)S(1)}, u32[]{:S(2)}, u32[]{:S(2)}) collective-permute-start(bf16[64,1152]{1,0:T(8,128)(2,1)} %get-tuple-element.459), channel_id=1, source_target_pairs={{0,14},{2,12},{4,10},{6,8},{8,6},{10,4},{12,2},{14,0},{1,15},{3,13... | collective-permute-start | bytes 442376 | tf_op jit(solution)/shard_map/ppermute | solution.py:924
  (81 other events, 2800.9 us)

commit v4 on v3

--- a/solution.py
+++ b/solution.py
@@ -16,6 +16,7 @@
 VMEM_LIMIT = 40 * 1024 * 1024
 SPACE_VMEM_LIMIT = 26 * 1024 * 1024
 FULL_VMEM_LIMIT = 60 * 1024 * 1024
+TANGENT_VMEM_LIMIT = 50 * 1024 * 1024
 
 epsilon = 1e-06
 
@@ -866,7 +867,7 @@
         1,
         rows,
         width,
-        FULL_VMEM_LIMIT,
+        TANGENT_VMEM_LIMIT,
         grid=(steps,),
         out_shape=[piece] * seats + [other] * first,
         in_specs=[IN_SMEM] * 2
@@ -1059,8 +1060,10 @@
     space += [space_far_y, space_far_x]
     space_other += [space_xy_other]
     time_other = [time_near_other]
-    space, space_other, time_other, time_far, time_near, time_x, noisy_lines = together(
-        space, space_other, time_other, time_far, time_near, time_x, noisy_lines
+    middle = noisy_lines[2].shape[1] // 2
+    noisy_2 = flip(noisy_lines[2][:, :middle], "seq", 4)
+    space, space_other, time_other, time_far, time_near, time_x, noisy_lines, noisy_2 = together(
+        space, space_other, time_other, time_far, time_near, time_x, noisy_lines, noisy_2
     )
 
     space_far_xy = flip(space[5], "cfg", 1)
@@ -1099,8 +1102,9 @@
     time_xy = flip(time_y, "cfg", 1)
     time_far_x = flip(time_far, "cfg", 1)
     time_far_y = flip(time_far, "seq", 1)
+    noisy_2 = [noisy_2, flip(noisy_came[2][:, middle:], "seq", 4)]
     noisy_came = list(noisy_came[:2]) + [
-        flip(line, "seq", 2 * index) for index, line in enumerate(noisy_came) if index > 1
+        jnp.concatenate(noisy_2, axis=1), flip(noisy_came[3], "seq", 6)
     ]
     cond = cond(weights=space_weights)
     cond, time_xy, time_far_x, time_far_y, noisy_came = together(

time: 457 us -> 447 us (0.978)
  waiting for transfers between devices: 134 us -> 120 us
  starting transfers between devices: 68.2 us -> 75.9 us
    ppermute x63 -> x64, waiting for transfers between devices: 118 us -> 96 us  [flip(): return lax.ppermute(value, axis, pairs)]
    ppermute x63 -> x64, starting transfers between devices: 54.6 us -> 63 us  [flip(): return lax.ppermute(value, axis, pairs)]
    ppermute x2, waiting for transfers between devices: 12.3 us -> 18.4 us  [to_ends(): outside = lax.ppermute(inside, 'seq', pairs)]
    unnamed x146 -> x128, local copies, waits for them, and re-layouts: 13.6 us -> 11.3 us
  transfers between devices with their start and end apart: 69 -> 70, of which waited for: 29 -> 27; matrix products, arithmetic and copies ran while one was open for 3% -> 2% of each run, Pallas kernels for 47% -> 48%
where the time goes in v4:
time: 447 us; the launch traced here: 443 us
  Pallas kernels  217 us (49%)
  waiting for transfers between devices  120 us (27%)
  starting transfers between devices  75.9 us (17%)
  local copies, waits for them, and re-layouts  19.4 us (4%)
  other arithmetic  7.49 us (2%)
    ppermute x64, waiting for transfers between devices, flip(): return lax.ppermute(value, axis, pairs)  96 us
    pallas_call x2, Pallas kernels, student_tangent(): time_call(functools.partial(tangent_kernel, layout, (len(weights), len(pi...  82.8 us
    ppermute x64, starting transfers between devices, flip(): return lax.ppermute(value, axis, pairs)  63 us
    pallas_call x2, Pallas kernels, spatial_layer(): pl.pallas_call(functools.partial(space_kernel, layout, len(pieces), 4), o...  56.8 us
    pallas_call x1, Pallas kernels, teacher_velocity(): time_call(functools.partial(teacher_kernel, layout, (len(weights), len(pi...  32.8 us
    pallas_call x1, Pallas kernels, student_rows(): time_call(functools.partial(student_rows_kernel, layout, (len(weights), l...  19.8 us
    ppermute x2, waiting for transfers between devices, to_ends(): outside = lax.ppermute(inside, 'seq', pairs)  18.4 us
    pallas_call x1, Pallas kernels, student_mix(): time_call(functools.partial(student_mix_kernel, layout, frames), 0.6, row...  17.7 us
  transfers between devices with their start and end apart: 70, of which 27 were waited for; matrix products, arithmetic and copies ran while one was open for 2% of the time, Pallas kernels for 48%

profile of v4, /device:TPU:8, one launch (start us, length us, event | category | flops | bytes accessed | tf_op | source)
XLA Modules:
  0.0 442.8 jit_solution(5732758390597124794)
XLA Ops:
  3.0 8.4 %collective-permute-done = bf16[2,72,1152]{2,1,0:T(8,128)(2,1)S(1)} collective-permute-done((bf16[2,72,1152]{2,1,0:T(8,128)(2,1)S(1)}, bf16[2,72,1152]{2,1,0:T(8,128)(2,1)S(1)}, u32[]{:S(2)}, u32[]{:S(2)}) %collective-permute-start) | collective-permute-done | bytes 331808 | tf_op jit(solution)/shard_map/ppermute | solution.py:925
  11.6 3.5 collective-permute-start.4
  15.2 1.6 collective-permute-start.2
  16.7 1.5 collective-permute-start.1
  18.2 9.6 %collective-permute-done.5 = bf16[2,72,1152]{2,1,0:T(8,128)(2,1)S(1)} collective-permute-done((bf16[2,72,1152]{2,1,0:T(8,128)(2,1)S(1)}, bf16[2,72,1152]{2,1,0:T(8,128)(2,1)S(1)}, u32[]{:S(2)}, u32[]{:S(2)}) %collective-permute-start.5) | collective-permute-done | bytes 331808 | tf_op jit(solution)/shard_map/ppermute | solution.py:925
  28.0 1.3 collective-permute-done.4
  30.2 2.4 collective-permute-done.2.rest_2_
  34.5 2.1 collective-permute-start.7
  37.2 3.6 collective-permute-start.10
  40.8 1.6 collective-permute-start.6
  46.1 2.3 copy-done
  48.4 2.3 copy-done.1
  50.8 2.6 shard_map.140
  53.4 1.4 broadcast_select_fusion.1.rest_4_
  54.9 2.9 collective-permute-done.6.rest_3_
  57.8 1.3 collective-permute-start.16
  59.1 1.6 collective-permute-start.13
  60.7 1.5 collective-permute-start.12
  62.4 18.4 %collective-permute-done.16 = bf16[2,144,1152]{2,1,0:T(8,128)(2,1)S(1)} collective-permute-done((bf16[2,144,1152]{2,1,0:T(8,128)(2,1)}, bf16[2,144,1152]{2,1,0:T(8,128)(2,1)S(1)}, u32[]{:S(2)}, u32[]{:S(2)}) %collective-permute-start.16) | collective-permute-done | bytes 663584 | tf_op jit(solution)/shard_map/ppermute | solution.py:959
  82.3 2.1 collective-permute-done.19.rest_12_
  84.5 2.0 collective-permute-done.20.rest_13_
  86.6 1.5 collective-permute-start.18
  88.1 1.5 collective-permute-start.22
  91.0 14.5 %collective-permute-done.24.rest_17_ = bf16[2,8,16,1152]{3,2,1,0:T(8,128)(2,1)S(1)} collective-permute-done((bf16[2,8,16,1152]{3,2,1,0:T(8,128)(2,1)S(1)}, bf16[2,8,16,1152]{3,2,1,0:T(8,128)(2,1)S(1)}, u32[]{:S(2)}, u32[]{:S(2)}) %collective-permute-start.24) | collective-permute-done | bytes 589856 | tf_op jit(solution)/shard_map/ppermute | solution.py:925
  106.2 1.5 collective-permute-done.25.rest_15_
  112.8 1.4 collective-permute-start.32
  115.5 2.3 copy-done.2
  117.8 26.7 %shard_map.141 = (bf16[4,4,16,1152]{3,2,1,0:T(8,128)(2,1)S(1)}, bf16[4,4,16,1152]{3,2,1,0:T(8,128)(2,1)}, bf16[4,4,16,1152]{3,2,1,0:T(8,128)(2,1)}, bf16[4,4,16,1152]{3,2,1,0:T(8,128)(2,1)}) custom-call(s32[3]{0:T(128)S(1)} %pad_add_fusion.seat_ref, f32[1]{0:T(128)} %copy.20.moment_ref, bf16[8,256,1152]{2,1,0:T(8,128)(2,1)S(1)} %bitcast.15, ...), custom_call_target="tpu_custom_call" | custom-call | flops 19025362944 | bytes 17694720 | tf_op jit(solution)/shard_map/pallas_call | solution.py:373
  144.8 7.6 %collective-permute-done.32.rest_19_ = bf16[2,8,16,1152]{3,2,1,0:T(8,128)(2,1)S(1)} collective-permute-done((bf16[2,8,16,1152]{3,2,1,0:T(8,128)(2,1)S(1)}, bf16[2,8,16,1152]{3,2,1,0:T(8,128)(2,1)S(1)}, u32[]{:S(2)}, u32[]{:S(2)}) %collective-permute-start.32) | collective-permute-done | bytes 589856 | tf_op jit(solution)/shard_map/ppermute | solution.py:925
  157.5 1.5 collective-permute-start.37
  159.0 1.3 collective-permute-start.38
  161.0 1.5 collective-permute-start.39
  162.5 30.1 %shard_map.142 = (bf16[4,4,16,1152]{3,2,1,0:T(8,128)(2,1)}, bf16[4,4,16,1152]{3,2,1,0:T(8,128)(2,1)}, bf16[4,4,16,1152]{3,2,1,0:T(8,128)(2,1)}, bf16[4,4,16,1152]{3,2,1,0:T(8,128)(2,1)}) custom-call(s32[3]{0:T(128)} %copy-done.16, f32[1]{0:T(128)} %copy.20.moment_ref, bf16[8,256,1152]{2,1,0:T(8,128)(2,1)} %clean_ref.5, bf16[8,256,1152]{2,1,0:T(8,128)(2,1)} %noise_ref.5, ...), custom_call_target="tpu_custom_call" | custom-call | flops 19025362944 | bytes 17694720 | tf_op jit(solution)/shard_map/pallas_call | solution.py:373
  192.6 5.4 %collective-permute-done.40.rest_20_ = bf16[2,8,16,1152]{3,2,1,0:T(8,128)(2,1)} collective-permute-done((bf16[2,8,16,1152]{3,2,1,0:T(8,128)(2,1)}, bf16[2,8,16,1152]{3,2,1,0:T(8,128)(2,1)}, u32[]{:S(2)}, u32[]{:S(2)}) %collective-permute-start.40) | collective-permute-done | bytes 589856 | tf_op jit(solution)/shard_map/ppermute | solution.py:925
  198.1 2.0 collective-permute-done.39.rest_7_.rest_10_
  204.2 1.4 collective-permute-start.42
  206.6 12.2 %collective-permute-done.42.rest_21_ = bf16[2,8,16,1152]{3,2,1,0:T(8,128)(2,1)S(1)} collective-permute-done((bf16[2,8,16,1152]{3,2,1,0:T(8,128)(2,1)S(1)}, bf16[2,8,16,1152]{3,2,1,0:T(8,128)(2,1)S(1)}, u32[]{:S(2)}, u32[]{:S(2)}) %collective-permute-start.42) | collective-permute-done | bytes 589856 | tf_op jit(solution)/shard_map/ppermute | solution.py:925
  218.9 1.4 collective-permute-start.43
  222.5 19.8 %shard_map.143 = (bf16[1024,1152]{1,0:T(8,128)(2,1)}, bf16[3,1024,1152]{2,1,0:T(8,128)(2,1)}) custom-call(s32[3]{0:T(128)S(1)} %copy-done.17, f32[1,1152]{1,0:T(1,128)S(1)} %broadcast_in_dim.12.shift_ref, bf16[128,1152]{1,0:T(8,128)(2,1)S(1)} %bitcast.16, bf16[128,1152]{1,0:T(8,128)(2,1)S(1)} %copy.17.up_ref, ...), custom_call_target="tpu_custom_call" | custom-call | flops 9784472576 | bytes 20054016 | tf_op jit(solution)/shard_map/pallas_call | solution.py:765
  242.4 4.0 collective-permute-done.45
  247.3 3.2 collective-permute-start.46
  251.6 17.7 %shard_map.144 = (bf16[4,128,1152]{2,1,0:T(8,128)(2,1)S(1)}, bf16[4,128,1152]{2,1,0:T(8,128)(2,1)S(1)}) custom-call(s32[3]{0:T(128)S(1)} %copy-done.17, f32[1,1152]{1,0:T(1,128)S(1)} %broadcast_in_dim.12.shift_ref, bf16[1024,1152]{1,0:T(8,128)(2,1)} %get-tuple-element.391.rows_ref.rest_1_, bf16[3,1024,1152]{2,1,0:T(8,128)(2,1)} %get-tuple-element.392.primal_ref.rest_2_, ...), custom_call_target="tpu_custom_call" | custom-call | flops 9784472576 | bytes 20054016 | tf_op jit(solution)/shard_map/pallas_call | solution.py:797
  269.6 3.7 collective-permute-done.46.rest_17_
  273.3 1.5 collective-permute-start.50
  275.4 1.3 collective-permute-start.49
  276.7 32.8 %shard_map.145.rest_0_ = bf16[1024,1152]{1,0:T(8,128)(2,1)} custom-call(s32[3]{0:T(128)S(1)} %copy-done.17, bf16[2,144,1152]{2,1,0:T(8,128)(2,1)S(1)} %maximum_select_fusion.1.rest_0_.rest_3_, bf16[2,144,1152]{2,1,0:T(8,128)(2,1)S(1)} %copy-done.25, bf16[2,144,1152]{2,1,0:T(8,128)(2,1)S(1)} %copy-done.20, ...), custom_call_target="tpu_custom_call" | custom-call | flops 16307453952 | bytes 20054016 | tf_op jit(solution)/shard_map/pallas_call | solution.py:827
  310.5 1.7 collective-permute-start.53
  314.3 43.8 %shard_map.146 = (bf16[64,1152]{1,0:T(8,128)(2,1)S(1)}, bf16[64,1152]{1,0:T(8,128)(2,1)S(1)}, bf16[64,1152]{1,0:T(8,128)(2,1)S(1)}, bf16[64,1152]{1,0:T(8,128)(2...) custom-call(s32[3]{0:T(128)S(1)} %copy-done.17, ...), custom_call_target="tpu_custom_call" | custom-call | flops 8153726976 | bytes 15335424 | tf_op jit(solution)/shard_map/pallas_call | solution.py:865
  358.2 5.7 %collective-permute-done.55.rest_3_ = bf16[2,128,1152]{2,1,0:T(8,128)(2,1)S(1)} collective-permute-done((bf16[2,128,1152]{2,1,0:T(8,128)(2,1)S(1)}, bf16[2,128,1152]{2,1,0:T(8,128)(2,1)S(1)}, u32[]{:S(2)}, u32[]{:S(2)}) %collective-permute-start.55) | collective-permute-done | bytes 589856 | tf_op jit(solution)/shard_map/ppermute | solution.py:925
  364.6 2.8 collective-permute-start.58
  368.3 2.1 collective-permute-start.60
  370.4 1.5 collective-permute-start.61
  371.9 1.7 collective-permute-start.62
  373.6 39.0 %shard_map.148 = (bf16[64,1152]{1,0:T(8,128)(2,1)S(1)}, bf16[64,1152]{1,0:T(8,128)(2,1)S(1)}, bf16[64,1152]{1,0:T(8,128)(2,1)S(1)}, bf16[64,1152]{1,0:T(8,128)(2...) custom-call(s32[3]{0:T(128)S(1)} %copy-done.17, ...), custom_call_target="tpu_custom_call" | custom-call | flops 8153726976 | bytes 15335424 | tf_op jit(solution)/shard_map/pallas_call | solution.py:865
  413.4 3.0 collective-permute-start.64
  416.6 1.9 collective-permute-start.66
  418.5 1.7 collective-permute-start.67
  421.1 4.8 %collective-permute-start.69 = (bf16[64,1152]{1,0:T(8,128)(2,1)S(1)}, bf16[64,1152]{1,0:T(8,128)(2,1)S(1)}, u32[]{:S(2)}, u32[]{:S(2)}) collective-permute-start(bf16[64,1152]{1,0:T(8,128)(2,1)S(1)} %get-tuple-element.461), channel_id=1, source_target_pairs={{0,14},{2,12},{4,10},{6,8},{8,6},{10,4},{12,2},{14,0},{1,15},{3,13... | collective-permute-start | bytes 442376 | tf_op jit(solution)/shard_map/ppermute | solution.py:925
  426.0 2.1 shard_map.147
  428.1 2.0 collective-permute-done.66.rest_12_
  430.1 4.6 %collective-permute-done.67.rest_13_ = bf16[64,1152]{1,0:T(8,128)(2,1)S(1)} collective-permute-done((bf16[64,1152]{1,0:T(8,128)(2,1)S(1)}, bf16[64,1152]{1,0:T(8,128)(2,1)S(1)}, u32[]{:S(2)}, u32[]{:S(2)}) %collective-permute-start.67) | collective-permute-done | bytes 147488 | tf_op jit(solution)/shard_map/ppermute | solution.py:925
  434.7 3.9 collective-permute-done.68.rest_14_
  438.7 1.8 collective-permute-done.69.rest_15_
  440.4 2.1 shard_map.149
  (260 shorter events, 41.0 us)
Async XLA Ops:
  1.8 9.6 %collective-permute-start = (bf16[2,72,1152]{2,1,0:T(8,128)(2,1)S(1)}, bf16[2,72,1152]{2,1,0:T(8,128)(2,1)S(1)}, u32[]{:S(2)}, u32[]{:S(2)}) collective-permute-start(bf16[2,72,1152]{2,1,0:T(8,128)(2,1)S(1)} %fusion.1), channel_id=1, source_target_pairs={{0,4},{2,6},{4,0},{6,2},{8,12},{10,14},{12,8},{14,10},{1,5},{3,7},... | collective-permute-start | bytes 995336 | tf_op jit(solution)/shard_map/ppermute | solution.py:925
  11.6 17.7 %collective-permute-start.4 = (bf16[2,144,1152]{2,1,0:T(8,128)(2,1)S(1)}, bf16[2,144,1152]{2,1,0:T(8,128)(2,1)}, u32[]{:S(2)}, u32[]{:S(2)}) collective-permute-start(bf16[2,144,1152]{2,1,0:T(8,128)(2,1)S(1)} %maximum_select_fusion.rest_0_), channel_id=1, source_target_pairs={{4,8},{8,4},{6,10},{10,6},{5,9},{9,5},{7,11},{11,7},{20,24},{24,20... | collective-permute-start | bytes 1990664 | tf_op jit(solution)/shard_map/ppermute | solution.py:949
  15.1 14.3 %collective-permute-start.3 = (bf16[2,144,1152]{2,1,0:T(8,128)(2,1)S(1)}, bf16[2,144,1152]{2,1,0:T(8,128)(2,1)S(1)}, u32[]{:S(2)}, u32[]{:S(2)}) collective-permute-start(bf16[2,144,1152]{2,1,0:T(8,128)(2,1)S(1)} %maximum_select_fusion.rest_0_), channel_id=1, source_target_pairs={{0,1},{1,0},{2,3},{3,2},{4,5},{5,4},{6,7},{7,6},{8,9},{9,8},{10,11... | collective-permute-start | bytes 1990664 | tf_op jit(solution)/shard_map/ppermute | solution.py:925
  15.2 17.4 %collective-permute-start.2 = (bf16[2,144,1152]{2,1,0:T(8,128)(2,1)S(1)}, bf16[2,144,1152]{2,1,0:T(8,128)(2,1)}, u32[]{:S(2)}, u32[]{:S(2)}) collective-permute-start(bf16[2,144,1152]{2,1,0:T(8,128)(2,1)S(1)} %maximum_select_fusion.rest_0_), channel_id=1, source_target_pairs={{0,16},{16,0},{1,17},{17,1},{2,18},{18,2},{3,19},{19,3},{4,20},{20... | collective-permute-start | bytes 1990664 | tf_op jit(solution)/shard_map/ppermute | solution.py:925
  16.7 17.0 %collective-permute-start.1 = (bf16[2,144,1152]{2,1,0:T(8,128)(2,1)S(1)}, bf16[2,144,1152]{2,1,0:T(8,128)(2,1)S(1)}, u32[]{:S(2)}, u32[]{:S(2)}) collective-permute-start(bf16[2,144,1152]{2,1,0:T(8,128)(2,1)S(1)} %maximum_select_fusion.rest_0_), channel_id=1, source_target_pairs={{0,2},{2,0},{4,6},{6,4},{8,10},{10,8},{12,14},{14,12},{1,3},{3,1},... | collective-permute-start | bytes 1990664 | tf_op jit(solution)/shard_map/ppermute | solution.py:925
  18.2 9.6 %collective-permute-start.5 = (bf16[2,72,1152]{2,1,0:T(8,128)(2,1)S(1)}, bf16[2,72,1152]{2,1,0:T(8,128)(2,1)S(1)}, u32[]{:S(2)}, u32[]{:S(2)}) collective-permute-start(bf16[2,72,1152]{2,1,0:T(8,128)(2,1)S(1)} %fusion), channel_id=1, source_target_pairs={{0,4},{2,6},{4,0},{6,2},{8,12},{10,14},{12,8},{14,10},{1,5},{3,7},... | collective-permute-start | bytes 995336 | tf_op jit(solution)/shard_map/ppermute | solution.py:925
  33.7 8.7 %collective-permute-start.8 = (bf16[2,144,1152]{2,1,0:T(8,128)(2,1)S(1)}, bf16[2,144,1152]{2,1,0:T(8,128)(2,1)S(1)}, u32[]{:S(2)}, u32[]{:S(2)}) collective-permute-start(bf16[2,144,1152]{2,1,0:T(8,128)(2,1)S(1)} %collective-permute-done.1.rest_1_), channel_id=1, source_target_pairs={{0,1},{1,0},{2,3},{3,2},{4,5},{5,4},{6,7},{7,6},{8,9},{9,8},{10,11... | collective-permute-start | bytes 1990664 | tf_op jit(solution)/shard_map/ppermute | solution.py:925
  34.5 18.8 %collective-permute-start.7 = (bf16[2,144,1152]{2,1,0:T(8,128)(2,1)}, bf16[2,144,1152]{2,1,0:T(8,128)(2,1)}, u32[]{:S(2)}, u32[]{:S(2)}) collective-permute-start(bf16[2,144,1152]{2,1,0:T(8,128)(2,1)} %collective-permute-done.4), channel_id=1, source_target_pairs={{4,0},{8,12},{6,2},{10,14},{5,1},{9,13},{7,3},{11,15},{20,16},{24,... | collective-permute-start | bytes 1990664 | tf_op jit(solution)/shard_map/ppermute | solution.py:959
  36.7 21.0 %collective-permute-start.11 = (bf16[2,144,1152]{2,1,0:T(8,128)(2,1)S(1)}, bf16[2,144,1152]{2,1,0:T(8,128)(2,1)S(1)}, u32[]{:S(2)}, u32[]{:S(2)}) collective-permute-start(bf16[2,144,1152]{2,1,0:T(8,128)(2,1)S(1)} %maximum_select_fusion.1.rest_0_.rest_3_), channel_id=1, source_target_pairs={{0,16},{16,0},{1,17},{17,1},{2,18},{18,2},{3,19},{19,3},{4,20},{20... | collective-permute-start | bytes 1990664 | tf_op jit(solution)/shard_map/ppermute | solution.py:925
  37.2 20.5 %collective-permute-start.10 = (bf16[2,144,1152]{2,1,0:T(8,128)(2,1)S(1)}, bf16[2,144,1152]{2,1,0:T(8,128)(2,1)}, u32[]{:S(2)}, u32[]{:S(2)}) collective-permute-start(bf16[2,144,1152]{2,1,0:T(8,128)(2,1)S(1)} %maximum_select_fusion.1.rest_0_.rest_3_), channel_id=1, source_target_pairs={{4,8},{8,4},{6,10},{10,6},{5,9},{9,5},{7,11},{11,7},{20,24},{24,20... | collective-permute-start | bytes 1990664 | tf_op jit(solution)/shard_map/ppermute | solution.py:949
  40.8 16.9 %collective-permute-start.6 = (bf16[2,144,1152]{2,1,0:T(8,128)(2,1)}, bf16[2,144,1152]{2,1,0:T(8,128)(2,1)}, u32[]{:S(2)}, u32[]{:S(2)}) collective-permute-start(bf16[2,144,1152]{2,1,0:T(8,128)(2,1)} %collective-permute-done.2.rest_2_), channel_id=1, source_target_pairs={{0,2},{2,0},{4,6},{6,4},{8,10},{10,8},{12,14},{14,12},{1,3},{3,1},... | collective-permute-start | bytes 1990664 | tf_op jit(solution)/shard_map/ppermute | solution.py:925
  43.3 14.4 %collective-permute-start.9 = (bf16[2,144,1152]{2,1,0:T(8,128)(2,1)}, bf16[2,144,1152]{2,1,0:T(8,128)(2,1)}, u32[]{:S(2)}, u32[]{:S(2)}) collective-permute-start(bf16[2,144,1152]{2,1,0:T(8,128)(2,1)} %collective-permute-done.2.rest_2_), channel_id=1, source_target_pairs={{0,1},{1,0},{2,3},{3,2},{4,5},{5,4},{6,7},{7,6},{8,9},{9,8},{10,11... | collective-permute-start | bytes 1990664 | tf_op jit(solution)/shard_map/ppermute | solution.py:925
  57.7 4.5 %collective-permute-start.14 = (bf16[2,144,1152]{2,1,0:T(8,128)(2,1)}, bf16[2,144,1152]{2,1,0:T(8,128)(2,1)S(1)}, u32[]{:S(2)}, u32[]{:S(2)}) collective-permute-start(bf16[2,144,1152]{2,1,0:T(8,128)(2,1)} %collective-permute-done.6.rest_3_), channel_id=1, source_target_pairs={{0,1},{1,0},{2,3},{3,2},{4,5},{5,4},{6,7},{7,6},{8,9},{9,8},{10,11... | collective-permute-start | bytes 1990664 | tf_op jit(solution)/shard_map/ppermute | solution.py:925
  57.8 23.0 %collective-permute-start.16 = (bf16[2,144,1152]{2,1,0:T(8,128)(2,1)}, bf16[2,144,1152]{2,1,0:T(8,128)(2,1)S(1)}, u32[]{:S(2)}, u32[]{:S(2)}) collective-permute-start(bf16[2,144,1152]{2,1,0:T(8,128)(2,1)} %collective-permute-done.10), channel_id=1, source_target_pairs={{4,0},{8,12},{6,2},{10,14},{5,1},{9,13},{7,3},{11,15},{20,16},{24,... | collective-permute-start | bytes 1990664 | tf_op jit(solution)/shard_map/ppermute | solution.py:959
  59.1 23.0 %collective-permute-start.13 = (bf16[2,144,1152]{2,1,0:T(8,128)(2,1)S(1)}, bf16[2,144,1152]{2,1,0:T(8,128)(2,1)S(1)}, u32[]{:S(2)}, u32[]{:S(2)}) collective-permute-start(bf16[2,144,1152]{2,1,0:T(8,128)(2,1)S(1)} %broadcast_select_fusion.1.rest_4_), channel_id=1, source_target_pairs={{0,16},{16,0},{1,17},{17,1},{2,18},{18,2},{3,19},{19,3},{4,20},{20... | collective-permute-start | bytes 1990664 | tf_op jit(solution)/shard_map/ppermute | solution.py:925
  60.7 21.4 %collective-permute-start.12 = (bf16[2,144,1152]{2,1,0:T(8,128)(2,1)S(1)}, bf16[2,144,1152]{2,1,0:T(8,128)(2,1)S(1)}, u32[]{:S(2)}, u32[]{:S(2)}) collective-permute-start(bf16[2,144,1152]{2,1,0:T(8,128)(2,1)S(1)} %broadcast_select_fusion.1.rest_4_), channel_id=1, source_target_pairs={{0,2},{2,0},{4,6},{6,4},{8,10},{10,8},{12,14},{14,12},{1,3},{3,1},... | collective-permute-start | bytes 1990664 | tf_op jit(solution)/shard_map/ppermute | solution.py:925
  62.2 19.9 %collective-permute-start.15 = (bf16[2,144,1152]{2,1,0:T(8,128)(2,1)S(1)}, bf16[2,144,1152]{2,1,0:T(8,128)(2,1)S(1)}, u32[]{:S(2)}, u32[]{:S(2)}) collective-permute-start(bf16[2,144,1152]{2,1,0:T(8,128)(2,1)S(1)} %maximum_select_fusion.1.rest_0_.rest_3_), channel_id=1, source_target_pairs={{0,1},{1,0},{2,3},{3,2},{4,5},{5,4},{6,7},{7,6},{8,9},{9,8},{10,11... | collective-permute-start | bytes 1990664 | tf_op jit(solution)/shard_map/ppermute | solution.py:925
  62.3 19.8 %collective-permute-start.17 = (bf16[2,4,16,1152]{3,2,1,0:T(8,128)(2,1)S(1)}, bf16[2,4,16,1152]{3,2,1,0:T(8,128)(2,1)S(1)}, u32[]{:S(2)}, u32[]{:S(2)}) collective-permute-start(bf16[2,4,16,1152]{3,2,1,0:T(8,128)(2,1)S(1)} %slice.138), channel_id=1, source_target_pairs={{0,8},{2,10},{4,12},{6,14},{8,0},{10,2},{12,4},{14,6},{1,9},{3,11}... | collective-permute-start | bytes 884744 | tf_op jit(solution)/shard_map/ppermute | solution.py:925
  86.6 18.9 %collective-permute-start.18 = (bf16[2,144,1152]{2,1,0:T(8,128)(2,1)S(1)}, bf16[2,144,1152]{2,1,0:T(8,128)(2,1)S(1)}, u32[]{:S(2)}, u32[]{:S(2)}) collective-permute-start(bf16[2,144,1152]{2,1,0:T(8,128)(2,1)S(1)} %collective-permute-done.12.rest_5_), channel_id=1, source_target_pairs={{0,16},{16,0},{1,17},{17,1},{2,18},{18,2},{3,19},{19,3},{4,20},{20... | collective-permute-start | bytes 1990664 | tf_op jit(solution)/shard_map/ppermute | solution.py:925
  88.1 17.4 %collective-permute-start.22 = (bf16[2,144,1152]{2,1,0:T(8,128)(2,1)S(1)}, bf16[2,144,1152]{2,1,0:T(8,128)(2,1)S(1)}, u32[]{:S(2)}, u32[]{:S(2)}) collective-permute-start(bf16[2,144,1152]{2,1,0:T(8,128)(2,1)S(1)} %maximum_select_fusion.1.rest_0_.rest_3_), channel_id=1, source_target_pairs={{0,2},{2,0},{4,6},{6,4},{8,10},{10,8},{12,14},{14,12},{1,3},{3,1},... | collective-permute-start | bytes 1990664 | tf_op jit(solution)/shard_map/ppermute | solution.py:925
  89.7 15.8 %collective-permute-start.23 = (bf16[2,144,1152]{2,1,0:T(8,128)(2,1)S(1)}, bf16[2,144,1152]{2,1,0:T(8,128)(2,1)S(1)}, u32[]{:S(2)}, u32[]{:S(2)}) collective-permute-start(bf16[2,144,1152]{2,1,0:T(8,128)(2,1)S(1)} %copy-done.19), channel_id=1, source_target_pairs={{0,1},{1,0},{2,3},{3,2},{4,5},{5,4},{6,7},{7,6},{8,9},{9,8},{10,11... | collective-permute-start | bytes 1990664 | tf_op jit(solution)/shard_map/ppermute | solution.py:925
  89.7 15.7 %collective-permute-start.24 = (bf16[2,8,16,1152]{3,2,1,0:T(8,128)(2,1)S(1)}, bf16[2,8,16,1152]{3,2,1,0:T(8,128)(2,1)S(1)}, u32[]{:S(2)}, u32[]{:S(2)}) collective-permute-start(bf16[2,8,16,1152]{3,2,1,0:T(8,128)(2,1)S(1)} %get-tuple-element.287), channel_id=1, source_target_pairs={{0,4},{2,6},{4,0},{6,2},{8,12},{10,14},{12,8},{14,10},{1,5},{3,7},... | collective-permute-start | bytes 1769480 | tf_op jit(solution)/shard_map/ppermute | solution.py:925
  109.6 42.7 %collective-permute-start.30 = (bf16[2,144,1152]{2,1,0:T(8,128)(2,1)S(1)}, bf16[2,144,1152]{2,1,0:T(8,128)(2,1)}, u32[]{:S(2)}, u32[]{:S(2)}) collective-permute-start(bf16[2,144,1152]{2,1,0:T(8,128)(2,1)S(1)} %broadcast_select_fusion.rest_4_.rest_7_), channel_id=1, source_target_pairs={{0,2},{2,0},{4,6},{6,4},{8,10},{10,8},{12,14},{14,12},{1,3},{3,1},... | collective-permute-start | bytes 1990664 | tf_op jit(solution)/shard_map/ppermute | solution.py:925
  110.6 41.7 %collective-permute-start.29 = (bf16[2,144,1152]{2,1,0:T(8,128)(2,1)S(1)}, bf16[2,144,1152]{2,1,0:T(8,128)(2,1)}, u32[]{:S(2)}, u32[]{:S(2)}) collective-permute-start(bf16[2,144,1152]{2,1,0:T(8,128)(2,1)S(1)} %broadcast_select_fusion.rest_4_.rest_7_), channel_id=1, source_target_pairs={{0,16},{16,0},{1,17},{17,1},{2,18},{18,2},{3,19},{19,3},{4,20},{20... | collective-permute-start | bytes 1990664 | tf_op jit(solution)/shard_map/ppermute | solution.py:925
  111.5 33.2 %collective-permute-start.31 = (bf16[2,4,16,1152]{3,2,1,0:T(8,128)(2,1)S(1)}, bf16[2,4,16,1152]{3,2,1,0:T(8,128)(2,1)S(1)}, u32[]{:S(2)}, u32[]{:S(2)}) collective-permute-start(bf16[2,4,16,1152]{3,2,1,0:T(8,128)(2,1)S(1)} %slice.139), channel_id=1, source_target_pairs={{0,8},{2,10},{4,12},{6,14},{8,0},{10,2},{12,4},{14,6},{1,9},{3,11}... | collective-permute-start | bytes 884744 | tf_op jit(solution)/shard_map/ppermute | solution.py:925
  112.8 39.5 %collective-permute-start.32 = (bf16[2,8,16,1152]{3,2,1,0:T(8,128)(2,1)S(1)}, bf16[2,8,16,1152]{3,2,1,0:T(8,128)(2,1)S(1)}, u32[]{:S(2)}, u32[]{:S(2)}) collective-permute-start(bf16[2,8,16,1152]{3,2,1,0:T(8,128)(2,1)S(1)} %get-tuple-element.343), channel_id=1, source_target_pairs={{0,12},{2,14},{4,8},{6,10},{8,4},{10,6},{12,0},{14,2},{1,13},{3,15... | collective-permute-start | bytes 1769480 | tf_op jit(solution)/shard_map/ppermute | solution.py:925
  114.3 38.1 %collective-permute-start.28 = (bf16[2,144,1152]{2,1,0:T(8,128)(2,1)S(1)}, bf16[2,144,1152]{2,1,0:T(8,128)(2,1)}, u32[]{:S(2)}, u32[]{:S(2)}) collective-permute-start(bf16[2,144,1152]{2,1,0:T(8,128)(2,1)S(1)} %collective-permute-done.22.rest_1_.rest_4_), channel_id=1, source_target_pairs={{0,16},{16,0},{1,17},{17,1},{2,18},{18,2},{3,19},{19,3},{4,20},{20... | collective-permute-start | bytes 1990664 | tf_op jit(solution)/shard_map/ppermute | solution.py:925
  152.3 4.4 collective-permute-start.34
  152.4 4.3 collective-permute-start.33
  152.9 3.8 collective-permute-start.35
  156.8 35.8 %collective-permute-start.36 = (bf16[4,4,16,1152]{3,2,1,0:T(8,128)(2,1)}, bf16[4,4,16,1152]{3,2,1,0:T(8,128)(2,1)}, u32[]{:S(2)}, u32[]{:S(2)}) collective-permute-start(bf16[4,4,16,1152]{3,2,1,0:T(8,128)(2,1)} %get-tuple-element.357), channel_id=1, source_target_pairs={{0,2},{2,0},{4,6},{6,4},{8,10},{10,8},{12,14},{14,12},{1,3},{3,1},... | collective-permute-start | bytes 1769480 | tf_op jit(solution)/shard_map/ppermute | solution.py:925
  157.5 35.1 %collective-permute-start.37 = (bf16[4,4,16,1152]{3,2,1,0:T(8,128)(2,1)}, bf16[4,4,16,1152]{3,2,1,0:T(8,128)(2,1)}, u32[]{:S(2)}, u32[]{:S(2)}) collective-permute-start(bf16[4,4,16,1152]{3,2,1,0:T(8,128)(2,1)} %get-tuple-element.358), channel_id=1, source_target_pairs={{0,16},{16,0},{1,17},{17,1},{2,18},{18,2},{3,19},{19,3},{4,20},{20... | collective-permute-start | bytes 1769480 | tf_op jit(solution)/shard_map/ppermute | solution.py:925
  159.0 33.7 %collective-permute-start.38 = (bf16[4,4,16,1152]{3,2,1,0:T(8,128)(2,1)}, bf16[4,4,16,1152]{3,2,1,0:T(8,128)(2,1)}, u32[]{:S(2)}, u32[]{:S(2)}) collective-permute-start(bf16[4,4,16,1152]{3,2,1,0:T(8,128)(2,1)} %get-tuple-element.359), channel_id=1, source_target_pairs={{0,18},{2,16},{4,22},{6,20},{8,26},{10,24},{12,30},{14,28},{16,2},... | collective-permute-start | bytes 1769480 | tf_op jit(solution)/shard_map/ppermute | solution.py:999
  160.3 37.8 %collective-permute-start.40 = (bf16[2,8,16,1152]{3,2,1,0:T(8,128)(2,1)}, bf16[2,8,16,1152]{3,2,1,0:T(8,128)(2,1)}, u32[]{:S(2)}, u32[]{:S(2)}) collective-permute-start(bf16[2,8,16,1152]{3,2,1,0:T(8,128)(2,1)} %get-tuple-element.364), channel_id=1, source_target_pairs={{0,2},{2,0},{4,6},{6,4},{8,10},{10,8},{12,14},{14,12},{1,3},{3,1},... | collective-permute-start | bytes 1769480 | tf_op jit(solution)/shard_map/ppermute | solution.py:925
  161.0 39.1 %collective-permute-start.39 = (bf16[2,144,1152]{2,1,0:T(8,128)(2,1)}, bf16[2,144,1152]{2,1,0:T(8,128)(2,1)}, u32[]{:S(2)}, u32[]{:S(2)}) collective-permute-start(bf16[2,144,1152]{2,1,0:T(8,128)(2,1)} %collective-permute-done.30.rest_5_.rest_8_), channel_id=1, source_target_pairs={{0,16},{16,0},{1,17},{17,1},{2,18},{18,2},{3,19},{19,3},{4,20},{20... | collective-permute-start | bytes 1990664 | tf_op jit(solution)/shard_map/ppermute | solution.py:925
  204.1 65.2 %collective-permute-start.47 = (bf16[4,4,16,1152]{3,2,1,0:T(8,128)(2,1)S(1)}, bf16[4,4,16,1152]{3,2,1,0:T(8,128)(2,1)S(1)}, u32[]{:S(2)}, u32[]{:S(2)}) collective-permute-start(bf16[4,4,16,1152]{3,2,1,0:T(8,128)(2,1)S(1)} %pad_maximum_fusion.5), channel_id=1, source_target_pairs={{0,8},{2,10},{4,12},{6,14},{8,0},{10,2},{12,4},{14,6},{1,9},{3,11}... | collective-permute-start | bytes 1769480 | tf_op jit(solution)/shard_map/ppermute | solution.py:925
  204.2 14.6 %collective-permute-start.42 = (bf16[2,8,16,1152]{3,2,1,0:T(8,128)(2,1)S(1)}, bf16[2,8,16,1152]{3,2,1,0:T(8,128)(2,1)S(1)}, u32[]{:S(2)}, u32[]{:S(2)}) collective-permute-start(bf16[2,8,16,1152]{3,2,1,0:T(8,128)(2,1)S(1)} %copy-done.52), channel_id=1, source_target_pairs={{0,2},{2,0},{4,6},{6,4},{8,10},{10,8},{12,14},{14,12},{1,3},{3,1},... | collective-permute-start | bytes 1769480 | tf_op jit(solution)/shard_map/ppermute | solution.py:925
  205.6 13.2 %collective-permute-start.41 = (bf16[2,144,1152]{2,1,0:T(8,128)(2,1)}, bf16[2,144,1152]{2,1,0:T(8,128)(2,1)S(1)}, u32[]{:S(2)}, u32[]{:S(2)}) collective-permute-start(bf16[2,144,1152]{2,1,0:T(8,128)(2,1)} %collective-permute-done.39.rest_7_.rest_10_), channel_id=1, source_target_pairs={{0,1},{1,0},{2,3},{3,2},{4,5},{5,4},{6,7},{7,6},{8,9},{9,8},{10,11... | collective-permute-start | bytes 1990664 | tf_op jit(solution)/shard_map/ppermute | solution.py:925
  205.8 63.8 %collective-permute-start.48 = (bf16[4,4,16,1152]{3,2,1,0:T(8,128)(2,1)S(1)}, bf16[4,4,16,1152]{3,2,1,0:T(8,128)(2,1)S(1)}, u32[]{:S(2)}, u32[]{:S(2)}) collective-permute-start(bf16[4,4,16,1152]{3,2,1,0:T(8,128)(2,1)S(1)} %pad_maximum_fusion.6), channel_id=1, source_target_pairs={{0,12},{2,14},{4,8},{6,10},{8,4},{10,6},{12,0},{14,2},{1,13},{3,15... | collective-permute-start | bytes 1769480 | tf_op jit(solution)/shard_map/ppermute | solution.py:925
  218.9 23.5 %collective-permute-start.43 = (bf16[4,4,16,1152]{3,2,1,0:T(8,128)(2,1)S(1)}, bf16[4,4,16,1152]{3,2,1,0:T(8,128)(2,1)S(1)}, u32[]{:S(2)}, u32[]{:S(2)}) collective-permute-start(bf16[4,4,16,1152]{3,2,1,0:T(8,128)(2,1)S(1)} %copy-done.60), channel_id=1, source_target_pairs={{0,2},{2,0},{4,6},{6,4},{8,10},{10,8},{12,14},{14,12},{1,3},{3,1},... | collective-permute-start | bytes 1769480 | tf_op jit(solution)/shard_map/ppermute | solution.py:925
  220.3 22.1 %collective-permute-start.44 = (bf16[4,4,16,1152]{3,2,1,0:T(8,128)(2,1)S(1)}, bf16[4,4,16,1152]{3,2,1,0:T(8,128)(2,1)S(1)}, u32[]{:S(2)}, u32[]{:S(2)}) collective-permute-start(bf16[4,4,16,1152]{3,2,1,0:T(8,128)(2,1)S(1)} %copy-done.59), channel_id=1, source_target_pairs={{0,16},{16,0},{1,17},{17,1},{2,18},{18,2},{3,19},{19,3},{4,20},{20... | collective-permute-start | bytes 1769480 | tf_op jit(solution)/shard_map/ppermute | solution.py:925
  221.5 24.9 %collective-permute-start.45 = (bf16[4,4,16,1152]{3,2,1,0:T(8,128)(2,1)S(1)}, bf16[4,4,16,1152]{3,2,1,0:T(8,128)(2,1)S(1)}, u32[]{:S(2)}, u32[]{:S(2)}) collective-permute-start(bf16[4,4,16,1152]{3,2,1,0:T(8,128)(2,1)S(1)} %copy-done.58), channel_id=1, source_target_pairs={{0,18},{2,16},{4,22},{6,20},{8,26},{10,24},{12,30},{14,28},{16,2},... | collective-permute-start | bytes 1769480 | tf_op jit(solution)/shard_map/ppermute | solution.py:999
  246.7 63.0 %collective-permute-start.52 = (bf16[4,4,16,1152]{3,2,1,0:T(8,128)(2,1)S(1)}, bf16[4,4,16,1152]{3,2,1,0:T(8,128)(2,1)S(1)}, u32[]{:S(2)}, u32[]{:S(2)}) collective-permute-start(bf16[4,4,16,1152]{3,2,1,0:T(8,128)(2,1)S(1)} %pad_maximum_fusion.10), channel_id=1, source_target_pairs={{0,12},{2,14},{4,8},{6,10},{8,4},{10,6},{12,0},{14,2},{1,13},{3,15... | collective-permute-start | bytes 1769480 | tf_op jit(solution)/shard_map/ppermute | solution.py:925
  247.3 26.0 %collective-permute-start.46 = (bf16[4,4,16,1152]{3,2,1,0:T(8,128)(2,1)S(1)}, bf16[4,4,16,1152]{3,2,1,0:T(8,128)(2,1)S(1)}, u32[]{:S(2)}, u32[]{:S(2)}) collective-permute-start(bf16[4,4,16,1152]{3,2,1,0:T(8,128)(2,1)S(1)} %pad_maximum_fusion.4), channel_id=1, source_target_pairs={{0,4},{2,6},{4,0},{6,2},{8,12},{10,14},{12,8},{14,10},{1,5},{3,7},... | collective-permute-start | bytes 1769480 | tf_op jit(solution)/shard_map/ppermute | solution.py:925
  273.3 36.4 %collective-permute-start.50 = (bf16[4,4,16,1152]{3,2,1,0:T(8,128)(2,1)S(1)}, bf16[4,4,16,1152]{3,2,1,0:T(8,128)(2,1)S(1)}, u32[]{:S(2)}, u32[]{:S(2)}) collective-permute-start(bf16[4,4,16,1152]{3,2,1,0:T(8,128)(2,1)S(1)} %pad_maximum_fusion.8), channel_id=1, source_target_pairs={{0,4},{2,6},{4,0},{6,2},{8,12},{10,14},{12,8},{14,10},{1,5},{3,7},... | collective-permute-start | bytes 1769480 | tf_op jit(solution)/shard_map/ppermute | solution.py:925
  274.8 34.8 %collective-permute-start.51 = (bf16[4,4,16,1152]{3,2,1,0:T(8,128)(2,1)S(1)}, bf16[4,4,16,1152]{3,2,1,0:T(8,128)(2,1)S(1)}, u32[]{:S(2)}, u32[]{:S(2)}) collective-permute-start(bf16[4,4,16,1152]{3,2,1,0:T(8,128)(2,1)S(1)} %pad_maximum_fusion.9), channel_id=1, source_target_pairs={{0,8},{2,10},{4,12},{6,14},{8,0},{10,2},{12,4},{14,6},{1,9},{3,11}... | collective-permute-start | bytes 1769480 | tf_op jit(solution)/shard_map/ppermute | solution.py:925
  275.4 34.3 %collective-permute-start.49 = (bf16[4,128,1152]{2,1,0:T(8,128)(2,1)S(1)}, bf16[4,128,1152]{2,1,0:T(8,128)(2,1)S(1)}, u32[]{:S(2)}, u32[]{:S(2)}) collective-permute-start(bf16[4,128,1152]{2,1,0:T(8,128)(2,1)S(1)} %get-tuple-element.402), channel_id=1, source_target_pairs={{0,2},{2,0},{4,6},{6,4},{8,10},{10,8},{12,14},{14,12},{1,3},{3,1},... | collective-permute-start | bytes 3538952 | tf_op jit(solution)/shard_map/ppermute | solution.py:925
  310.5 47.7 %collective-permute-start.53 = (bf16[2,128,1152]{2,1,0:T(8,128)(2,1)S(1)}, bf16[2,128,1152]{2,1,0:T(8,128)(2,1)S(1)}, u32[]{:S(2)}, u32[]{:S(2)}) collective-permute-start(bf16[2,128,1152]{2,1,0:T(8,128)(2,1)S(1)} %pad_maximum_fusion.12), channel_id=1, source_target_pairs={{0,4},{2,6},{4,0},{6,2},{8,12},{10,14},{12,8},{14,10},{1,5},{3,7},... | collective-permute-start | bytes 1769480 | tf_op jit(solution)/shard_map/ppermute | solution.py:925
  312.2 46.0 %collective-permute-start.54 = (bf16[2,128,1152]{2,1,0:T(8,128)(2,1)S(1)}, bf16[2,128,1152]{2,1,0:T(8,128)(2,1)S(1)}, u32[]{:S(2)}, u32[]{:S(2)}) collective-permute-start(bf16[2,128,1152]{2,1,0:T(8,128)(2,1)S(1)} %pad_maximum_fusion.13), channel_id=1, source_target_pairs={{0,8},{2,10},{4,12},{6,14},{8,0},{10,2},{12,4},{14,6},{1,9},{3,11}... | collective-permute-start | bytes 1769480 | tf_op jit(solution)/shard_map/ppermute | solution.py:925
  313.5 50.4 %collective-permute-start.55 = (bf16[2,128,1152]{2,1,0:T(8,128)(2,1)S(1)}, bf16[2,128,1152]{2,1,0:T(8,128)(2,1)S(1)}, u32[]{:S(2)}, u32[]{:S(2)}) collective-permute-start(bf16[2,128,1152]{2,1,0:T(8,128)(2,1)S(1)} %pad_maximum_fusion.14), channel_id=1, source_target_pairs={{0,12},{2,14},{4,8},{6,10},{8,4},{10,6},{12,0},{14,2},{1,13},{3,15... | collective-permute-start | bytes 1769480 | tf_op jit(solution)/shard_map/ppermute | solution.py:925
  363.9 6.5 %collective-permute-start.56 = (bf16[64,1152]{1,0:T(8,128)(2,1)S(1)}, bf16[64,1152]{1,0:T(8,128)(2,1)S(1)}, u32[]{:S(2)}, u32[]{:S(2)}) collective-permute-start(bf16[64,1152]{1,0:T(8,128)(2,1)S(1)} %get-tuple-element.439), channel_id=1, source_target_pairs={{0,2},{2,0},{4,6},{6,4},{8,10},{10,8},{12,14},{14,12},{1,3},{3,1},... | collective-permute-start | bytes 442376 | tf_op jit(solution)/shard_map/ppermute | solution.py:925
  364.6 7.3 %collective-permute-start.57 = (bf16[64,1152]{1,0:T(8,128)(2,1)S(1)}, bf16[64,1152]{1,0:T(8,128)(2,1)S(1)}, u32[]{:S(2)}, u32[]{:S(2)}) collective-permute-start(bf16[64,1152]{1,0:T(8,128)(2,1)S(1)} %get-tuple-element.440), channel_id=1, source_target_pairs={{0,4},{2,6},{4,0},{6,2},{8,12},{10,14},{12,8},{14,10},{1,5},{3,7},... | collective-permute-start | bytes 442376 | tf_op jit(solution)/shard_map/ppermute | solution.py:925
  364.6 48.0 %collective-permute-start.58 = (bf16[64,1152]{1,0:T(8,128)(2,1)S(1)}, bf16[64,1152]{1,0:T(8,128)(2,1)S(1)}, u32[]{:S(2)}, u32[]{:S(2)}) collective-permute-start(bf16[64,1152]{1,0:T(8,128)(2,1)S(1)} %get-tuple-element.441), channel_id=1, source_target_pairs={{0,6},{2,4},{4,2},{6,0},{8,14},{10,12},{12,10},{14,8},{1,7},{3,5},... | collective-permute-start | bytes 442376 | tf_op jit(solution)/shard_map/ppermute | solution.py:925
  367.4 45.2 %collective-permute-start.59 = (bf16[64,1152]{1,0:T(8,128)(2,1)S(1)}, bf16[64,1152]{1,0:T(8,128)(2,1)S(1)}, u32[]{:S(2)}, u32[]{:S(2)}) collective-permute-start(bf16[64,1152]{1,0:T(8,128)(2,1)S(1)} %get-tuple-element.442), channel_id=1, source_target_pairs={{0,8},{2,10},{4,12},{6,14},{8,0},{10,2},{12,4},{14,6},{1,9},{3,11}... | collective-permute-start | bytes 442376 | tf_op jit(solution)/shard_map/ppermute | solution.py:925
  368.3 44.3 %collective-permute-start.60 = (bf16[64,1152]{1,0:T(8,128)(2,1)S(1)}, bf16[64,1152]{1,0:T(8,128)(2,1)S(1)}, u32[]{:S(2)}, u32[]{:S(2)}) collective-permute-start(bf16[64,1152]{1,0:T(8,128)(2,1)S(1)} %get-tuple-element.443), channel_id=1, source_target_pairs={{0,10},{2,8},{4,14},{6,12},{8,2},{10,0},{12,6},{14,4},{1,11},{3,9}... | collective-permute-start | bytes 442376 | tf_op jit(solution)/shard_map/ppermute | solution.py:925
  370.4 42.2 %collective-permute-start.61 = (bf16[64,1152]{1,0:T(8,128)(2,1)S(1)}, bf16[64,1152]{1,0:T(8,128)(2,1)S(1)}, u32[]{:S(2)}, u32[]{:S(2)}) collective-permute-start(bf16[64,1152]{1,0:T(8,128)(2,1)S(1)} %get-tuple-element.444), channel_id=1, source_target_pairs={{0,12},{2,14},{4,8},{6,10},{8,4},{10,6},{12,0},{14,2},{1,13},{3,15... | collective-permute-start | bytes 442376 | tf_op jit(solution)/shard_map/ppermute | solution.py:925
  371.9 40.7 %collective-permute-start.62 = (bf16[64,1152]{1,0:T(8,128)(2,1)S(1)}, bf16[64,1152]{1,0:T(8,128)(2,1)S(1)}, u32[]{:S(2)}, u32[]{:S(2)}) collective-permute-start(bf16[64,1152]{1,0:T(8,128)(2,1)S(1)} %get-tuple-element.445), channel_id=1, source_target_pairs={{0,14},{2,12},{4,10},{6,8},{8,6},{10,4},{12,2},{14,0},{1,15},{3,13... | collective-permute-start | bytes 442376 | tf_op jit(solution)/shard_map/ppermute | solution.py:925
  412.6 7.6 %collective-permute-start.63 = (bf16[64,1152]{1,0:T(8,128)(2,1)S(1)}, bf16[64,1152]{1,0:T(8,128)(2,1)S(1)}, u32[]{:S(2)}, u32[]{:S(2)}) collective-permute-start(bf16[64,1152]{1,0:T(8,128)(2,1)S(1)} %get-tuple-element.455), channel_id=1, source_target_pairs={{0,2},{2,0},{4,6},{6,4},{8,10},{10,8},{12,14},{14,12},{1,3},{3,1},... | collective-permute-start | bytes 442376 | tf_op jit(solution)/shard_map/ppermute | solution.py:925
  413.4 7.8 %collective-permute-start.64 = (bf16[64,1152]{1,0:T(8,128)(2,1)S(1)}, bf16[64,1152]{1,0:T(8,128)(2,1)S(1)}, u32[]{:S(2)}, u32[]{:S(2)}) collective-permute-start(bf16[64,1152]{1,0:T(8,128)(2,1)S(1)} %get-tuple-element.456), channel_id=1, source_target_pairs={{0,4},{2,6},{4,0},{6,2},{8,12},{10,14},{12,8},{14,10},{1,5},{3,7},... | collective-permute-start | bytes 442376 | tf_op jit(solution)/shard_map/ppermute | solution.py:925
  416.4 11.7 %collective-permute-start.65 = (bf16[64,1152]{1,0:T(8,128)(2,1)S(1)}, bf16[64,1152]{1,0:T(8,128)(2,1)S(1)}, u32[]{:S(2)}, u32[]{:S(2)}) collective-permute-start(bf16[64,1152]{1,0:T(8,128)(2,1)S(1)} %get-tuple-element.457), channel_id=1, source_target_pairs={{0,6},{2,4},{4,2},{6,0},{8,14},{10,12},{12,10},{14,8},{1,7},{3,5},... | collective-permute-start | bytes 442376 | tf_op jit(solution)/shard_map/ppermute | solution.py:925
  416.6 13.5 %collective-permute-start.66 = (bf16[64,1152]{1,0:T(8,128)(2,1)S(1)}, bf16[64,1152]{1,0:T(8,128)(2,1)S(1)}, u32[]{:S(2)}, u32[]{:S(2)}) collective-permute-start(bf16[64,1152]{1,0:T(8,128)(2,1)S(1)} %get-tuple-element.458), channel_id=1, source_target_pairs={{0,8},{2,10},{4,12},{6,14},{8,0},{10,2},{12,4},{14,6},{1,9},{3,11}... | collective-permute-start | bytes 442376 | tf_op jit(solution)/shard_map/ppermute | solution.py:925
  418.5 16.2 %collective-permute-start.67 = (bf16[64,1152]{1,0:T(8,128)(2,1)S(1)}, bf16[64,1152]{1,0:T(8,128)(2,1)S(1)}, u32[]{:S(2)}, u32[]{:S(2)}) collective-permute-start(bf16[64,1152]{1,0:T(8,128)(2,1)S(1)} %get-tuple-element.459), channel_id=1, source_target_pairs={{0,10},{2,8},{4,14},{6,12},{8,2},{10,0},{12,6},{14,4},{1,11},{3,9}... | collective-permute-start | bytes 442376 | tf_op jit(solution)/shard_map/ppermute | solution.py:925
  420.2 18.5 %collective-permute-start.68 = (bf16[64,1152]{1,0:T(8,128)(2,1)S(1)}, bf16[64,1152]{1,0:T(8,128)(2,1)S(1)}, u32[]{:S(2)}, u32[]{:S(2)}) collective-permute-start(bf16[64,1152]{1,0:T(8,128)(2,1)S(1)} %get-tuple-element.460), channel_id=1, source_target_pairs={{0,12},{2,14},{4,8},{6,10},{8,4},{10,6},{12,0},{14,2},{1,13},{3,15... | collective-permute-start | bytes 442376 | tf_op jit(solution)/shard_map/ppermute | solution.py:925
  421.1 19.3 %collective-permute-start.69 = (bf16[64,1152]{1,0:T(8,128)(2,1)S(1)}, bf16[64,1152]{1,0:T(8,128)(2,1)S(1)}, u32[]{:S(2)}, u32[]{:S(2)}) collective-permute-start(bf16[64,1152]{1,0:T(8,128)(2,1)S(1)} %get-tuple-element.461), channel_id=1, source_target_pairs={{0,14},{2,12},{4,10},{6,8},{8,6},{10,4},{12,2},{14,0},{1,15},{3,13... | collective-permute-start | bytes 442376 | tf_op jit(solution)/shard_map/ppermute | solution.py:925
  (72 other events, 2444.9 us)
